TPU v7x, 32 devices: a whole 2x2x4 slice. The times are simulated.
32 devices in a mesh: ctx: 8 (over y, x, core), row: 4 (over z).
Axes of the slice: x: 2, y: 2, z: 4, core: 2. Of those that a mesh axis runs over, the one named last changes fastest.
Arguments:
- latent_cache: bfloat16 [32768, 576], P(('ctx', 'row')), may hold values from -8 to 8
- index_keys: bfloat16 [32768, 128], P('ctx'), may hold values from -6 to 6
- query_latent: bfloat16 [128, 128, 576], P(('row', 'ctx')), may hold values from -100 to 99
- index_query: bfloat16 [128, 64, 128], P(('row', 'ctx')), may hold values from -0.5 to 0.5
- index_gates: bfloat16 [128, 64], P(('row', 'ctx')), may hold values from -0.75 to 0.75
- selected: int32 [128, 2048], P(('row', 'ctx')), may hold values from 0 to 32767, as said below
Outputs:
- attended: bfloat16 [128, 128, 512], P(('row', 'ctx'))
- index_scores: float32 [128, 32768], P('row', 'ctx')
Inputs may be any that keep to these rules, and one draw needn't show every extreme that they name: `selected`: each row names 2048 different tokens. Among the tokens of one index of ctx (s * 4096 <= t < (s + 1) * 4096) a row names at most 256, and exactly 256 in one such range; a row names at most one token in each aligned run of 16 tokens.
All inputs are finite; a program needn't handle non-finite values.
Results may differ from a plain program's by a relative error of at most 0.0045.
Values may be sent and summed in bfloat16 or wider, within the bound.
No kernel may reach another device: no remote copies, remote signals or barrier semaphores. Data moves between devices by JAX's collectives and lax.ppermute only.
A program may use at most 256 MiB of HBM per device.

v0:
```python
import jax
import jax.numpy as jnp
from jax import lax
from jax.sharding import PartitionSpec as P

LATENT = 512
SCORE_DIM = 192
SEL_MOST = 256
TOK_DEV = 4096


def index_block(iquery, gates, index_keys):
    count = iquery.shape[0]
    groups = count // 8
    heads = iquery.shape[1]
    query_blocks = iquery.reshape(groups, 8 * heads, iquery.shape[2])
    gate_blocks = gates.astype(jnp.float32).reshape(groups, 8, heads)

    def one_block(pair):
        block, gate = pair
        logits = jnp.einsum("qd,td->qt", block, index_keys, preferred_element_type=jnp.float32)
        logits = logits.reshape(8, heads, logits.shape[1])
        return jnp.sum(gate[:, :, None] * jnp.maximum(logits, 0.0), axis=1)

    result = lax.map(one_block, (query_blocks, gate_blocks))
    return result.reshape(count, result.shape[2])


def slot_table(place, value, slots):

    def one_row(pair):
        where_to, what = pair
        hit = where_to[:, None] == jnp.arange(slots, dtype=jnp.int32)[None, :]
        return jnp.max(jnp.where(hit, what[:, None], -1), axis=0)

    return lax.map(one_row, (place, value))


def pick_rows(source, table, spacing):
    blocks = source.reshape(source.shape[0] // spacing, spacing, source.shape[1])
    offset = table % spacing
    onehot = (
        (offset[:, :, None] == jnp.arange(spacing, dtype=jnp.int32)[None, None, :])
        & (table >= 0)[:, :, None]
    ).astype(jnp.bfloat16)
    rows_out = jnp.einsum("gsj,sjd->gsd", onehot, blocks, preferred_element_type=jnp.float32)
    return rows_out.astype(jnp.bfloat16)


def weigh(queries, keys, valid):
    scores = jnp.einsum(
        "ghd,gsd->ghs", queries, keys, preferred_element_type=jnp.float32
    ) * SCORE_DIM ** (-0.5)
    return jnp.where(valid[:, None, :], scores, -1e30)


def combine(masked, peak, keys, valid):
    weights = jnp.where(valid[:, None, :], jnp.exp(masked - peak[:, :, None]), 0.0).astype(
        jnp.bfloat16
    )
    totals = jnp.sum(weights.astype(jnp.float32), axis=2)
    sums = jnp.einsum(
        "ghs,gsd->ghd", weights, keys[:, :, :LATENT], preferred_element_type=jnp.float32
    )
    return (sums, totals)


def body(latent_cache, index_keys, query_latent, index_query, index_gates, selected):
    spacing = TOK_DEV // SEL_MOST
    slab = lax.all_gather(latent_cache, "row", axis=0, tiled=True)
    queries, iquery, gates = (
        lax.all_gather(query_latent, "ctx", axis=0, tiled=True),
        lax.all_gather(index_query, "ctx", axis=0, tiled=True),
        lax.all_gather(index_gates, "ctx", axis=0, tiled=True),
    )
    picks = lax.all_gather(selected, "ctx", axis=0, tiled=True)
    index_scores = index_block(iquery, gates, index_keys)
    local = picks - lax.axis_index("ctx") * TOK_DEV
    mine = (local >= 0) & (local < TOK_DEV)
    place = jnp.where(mine, local // spacing, SEL_MOST)
    table = slot_table(place, local, SEL_MOST)
    valid = table >= 0
    keys = pick_rows(slab, table, spacing)
    masked = weigh(queries, keys, valid)
    peak = lax.pmax(jnp.max(masked, axis=2), "ctx")
    sums, totals = combine(masked, peak, keys, valid)
    summed, total = (
        lax.psum_scatter(sums, "ctx", scatter_dimension=0, tiled=True),
        lax.psum_scatter(totals, "ctx", scatter_dimension=0, tiled=True),
    )
    attended = (summed / total[:, :, None]).astype(jnp.bfloat16)
    return (attended, index_scores)


def solution(mesh):
    return jax.shard_map(
        body,
        mesh=mesh,
        in_specs=(
            P(("ctx", "row"), None),
            P("ctx", None),
            P(("row", "ctx"), None, None),
            P(("row", "ctx"), None, None),
            P(("row", "ctx"), None),
            P(("row", "ctx"), None),
        ),
        out_specs=(P(("row", "ctx"), None, None), P("row", "ctx")),
        check_vma=False,
    )
```

profile of v0, /device:TPU:0, one launch (start us, length us, event | category | flops | bytes accessed | tf_op | source)
XLA Modules:
  0.0 270.8 jit_solution(16321856759675454812)
XLA Ops:
  8.7 11.0 %all-gather = s32[8,4,2048]{2,1,0:T(4,128)S(1)} all-gather(s32[1,4,2048]{2,1,0:T(4,128)} %bitcast.72), channel_id=1, replica_groups=mesh['ctx'=8,'row'=4] {'ctx'}, dimensions={0}, use_global_device_ids=true | all-gather | bytes 294912 | tf_op jit(solution)/shard_map/all_gather | solution.py:76
  20.0 41.7 %while.22 = (s32[]{:T(128)}, s32[32,256]{1,0:T(8,128)S(1)}, s32[32,2048]{1,0:T(8,128)S(1)}, s32[32,2048]{1,0:T(8,128)S(1)}) while((s32[]{:T(128)}, s32[32,256]{1,0:T(8,128)S(1)}, s32[32,2048]{1,0:T(8,128)S(1)}, s32[32,2048]{1,0:T(8,128)S(1)}) %tuple.46), condition=%wide.region_2.3_spmd.clone, body=%wide.region_0.2_spmd.sunk.clone | while | flops 1572610 | bytes 52285 | solution.py:36
  20.0 1.2 select_reduce_fusion.3
  21.3 1.2 select_reduce_fusion.3
  22.6 1.2 select_reduce_fusion.3
  23.9 1.2 select_reduce_fusion.3
  25.2 1.2 select_reduce_fusion.3
  26.5 1.2 select_reduce_fusion.3
  27.8 1.2 select_reduce_fusion.3
  29.2 1.2 select_reduce_fusion.3
  30.5 1.2 select_reduce_fusion.3
  31.8 1.2 select_reduce_fusion.3
  33.1 1.2 select_reduce_fusion.3
  34.4 1.2 select_reduce_fusion.3
  35.7 1.2 select_reduce_fusion.3
  37.0 1.2 select_reduce_fusion.3
  38.3 1.2 select_reduce_fusion.3
  39.6 1.2 select_reduce_fusion.3
  40.9 1.2 select_reduce_fusion.3
  42.2 1.2 select_reduce_fusion.3
  43.5 1.2 select_reduce_fusion.3
  44.8 1.2 select_reduce_fusion.3
  46.1 1.2 select_reduce_fusion.3
  47.4 1.2 select_reduce_fusion.3
  48.7 1.2 select_reduce_fusion.3
  50.0 1.2 select_reduce_fusion.3
  51.3 1.2 select_reduce_fusion.3
  52.6 1.2 select_reduce_fusion.3
  53.9 1.2 select_reduce_fusion.3
  61.9 39.8 %all-gather.5.cloned.1.call-done = bf16[4096,576]{0,1:T(8,128)(2,1)} async-done(((bf16[1024,576]{0,1:T(8,128)(2,1)}), bf16[4096,576]{0,1:T(8,128)(2,1)}) %all-gather.5.cloned.1.call-update) | async-done | bytes 4718608 | tf_op jit(solution)/shard_map/all_gather | solution.py:70
  101.7 7.6 %copy.22 = bf16[4096,576]{1,0:T(8,128)(2,1)} copy(bf16[4096,576]{0,1:T(8,128)(2,1)} %all-gather.5.cloned.1.call-done) | data formatting | bytes 9437184 | tf_op jit(solution)/shard_map/all_gather | solution.py:70
  109.3 7.5 %convert_bitcast_fusion = bf16[32,256,576]{2,0,1:T(8,128)(2,1)} fusion(bf16[256,16,576]{2,1,0:T(8,128)(2,1)} %bitcast.64, s32[32,256]{0,1:T(8,128)S(1)} %copy.20, pred[32,256]{0,1:T(8,128)(4,1)S(1)} %copy.21), kind=kOutput, calls=%fused_computation.11 | convolution fusion | flops 155975680 | bytes 14196736 | tf_op jit(solution)/shard_map/gsj,sjd->gsd/dot_general | solution.py:46
  116.8 8.6 %slice.4 = bf16[32,256,512]{2,0,1:T(8,128)(2,1)} slice(bf16[32,256,576]{2,0,1:T(8,128)(2,1)} %convert_bitcast_fusion), slice={[0:32], [0:256], [0:512]} | slice | bytes 16777216 | tf_op jit(solution)/shard_map/slice | solution.py:63
  125.4 15.5 %all-gather.7.cloned.1.call-done = bf16[32,128,576]{1,2,0:T(8,128)(2,1)} async-done(((bf16[4,128,576]{1,2,0:T(8,128)(2,1)}), bf16[32,128,576]{1,2,0:T(8,128)(2,1)}) %all-gather.7.cloned.1.call-update) | async-done | bytes 4718608 | tf_op jit(solution)/shard_map/all_gather | solution.py:72
  141.0 11.7 %bitcast_reduce_fusion = (f32[32,128]{1,0:T(8,128)S(1)}, f32[32,256,128]{2,1,0:T(8,128)}) fusion(pred[32,256]{1,0:T(8,128)(4,1)S(1)} %broadcast_compare_fusion, bf16[32,128,576]{1,2,0:T(8,128)(2,1)} %all-gather.7.cloned.1.call-done, bf16[32,256,576]{2,0,1:T(8,128)(2,1)} %convert_bitcast_fusion), kind=kOutput, calls=%fused_computation.15 | convolution fusion | flops 1211101184 | bytes 18374656 | tf_op jit(solution)/shard_map/ghd,gsd->ghs/dot_general | solution.py:51
  152.7 23.5 %pmax.7 = f32[32,128]{1,0:T(8,128)S(1)} all-reduce(f32[32,128]{1,0:T(8,128)S(1)} %get-tuple-element.73), channel_id=1, replica_groups=mesh['ctx'=8,'row'=4] {'ctx'}, use_global_device_ids=true, to_apply=%region_4.5 | all-reduce | flops 4096 | bytes 32768 | tf_op jit(solution)/shard_map/pmax | solution.py:85
  176.1 14.2 %fusion.3 = f32[32,128,512]{2,1,0:T(8,128)} fusion(bf16[32,256,512]{2,0,1:T(8,128)(2,1)} %slice.4, f32[32,256,128]{2,1,0:T(8,128)} %get-tuple-element.74, f32[32,128]{1,0:T(8,128)S(1)} %pmax.7, pred[32,256]{1,0:T(8,128)(4,1)S(1)} %broadcast_compare_fusion), kind=kOutput, calls=%fused_computation.12 | convolution fusion | flops 1078984704 | bytes 20996096 | tf_op jit(solution)/shard_map/ghs,gsd->ghd/dot_general | solution.py:62
  192.2 8.9 %all-gather.1 = bf16[8,4,64]{2,1,0:T(4,128)(2,1)S(1)} all-gather(bf16[1,4,64]{2,1,0:T(4,128)(2,1)S(1)} %bitcast.74), channel_id=1, replica_groups=mesh['ctx'=8,'row'=4] {'ctx'}, dimensions={0}, use_global_device_ids=true | all-gather | bytes 4608 | tf_op jit(solution)/shard_map/all_gather | solution.py:74
  201.1 9.1 %all_gather.19 = bf16[32,64,128]{2,1,0:T(8,128)(2,1)S(1)} all-gather(bf16[4,64,128]{2,1,0:T(8,128)(2,1)S(1)} %copy-done), channel_id=1, replica_groups=mesh['ctx'=8,'row'=4] {'ctx'}, dimensions={0}, use_global_device_ids=true | all-gather | bytes 589824 | tf_op jit(solution)/shard_map/all_gather | solution.py:73
  210.2 8.0 %while.23 = (s32[]{:T(128)}, f32[4,8,4096]{2,1,0:T(8,128)}, f32[4,8,64]{2,1,0:T(8,128)S(1)}, bf16[4,512,128]{2,1,0:T(8,128)(2,1)S(1)}, bf16[4096,128]{1,0:T(8,128)(2,1)S(1)}) while((s32[]{:T(128)}, f32[4,8,4096]{2,1,0:T(8,128)}, f32[4,8,64]{2,1,0:T(8,128)S(1)}, bf16[4,512,128]{2,1,0:T(8,128)(2,1)S(1)}, ...), condition=%wide.region_10.11_spmd.clone, body=%wide.region_8.10_spmd.sunk.clone | while | flops 543129600 | bytes 1841733 | solution.py:25
  210.2 1.3 multiply_reduce_fusion.3
  212.2 1.3 multiply_reduce_fusion.3
  214.2 1.3 multiply_reduce_fusion.3
  216.2 1.3 multiply_reduce_fusion.3
  218.2 6.1 %convert_reduce_fusion = f32[32,128]{1,0:T(8,128)S(1)} fusion(f32[32,128]{1,0:T(8,128)S(1)} %pmax.7, f32[32,256,128]{2,1,0:T(8,128)} %get-tuple-element.74, pred[32,256]{1,0:T(8,128)(4,1)S(1)} %broadcast_compare_fusion), kind=kLoop, calls=%fused_computation.19 | loop fusion | flops 7335936 | bytes 4235264 | tf_op jit(solution)/shard_map/reduce_sum | solution.py:61
  224.3 24.0 %all-reduce = f32[32,128]{1,0:T(8,128)S(1)} all-reduce(f32[32,128]{1,0:T(8,128)S(1)} %convert_reduce_fusion), channel_id=3, replica_groups=mesh['ctx'=8,'row'=4] {'ctx'}, use_global_device_ids=true, to_apply=%region_7.8.clone | all-reduce | flops 4096 | bytes 32768
  248.3 13.8 %reduce-scatter.2.cloned.1.call-done = f32[4,128,512]{2,1,0:T(8,128)} async-done(((f32[32,128,512]{2,1,0:T(8,128)}), f32[4,128,512]{2,1,0:T(8,128)}) %reduce-scatter.2.cloned.1.call-update) | async-done | bytes 1048592 | tf_op jit(solution)/shard_map/reduce_scatter | solution.py:88
  262.1 2.2 divide_convert_fusion
  (107 shorter events, 14.1 us)
Async XLA Ops:
  7.2 94.5 %all-gather.5.cloned.1.call-start = ((), (), s32[]{:S(2)}) async-start(), calls=%async_computation.1 | async-start | bytes 5898240 | tf_op jit(solution)/shard_map/all_gather | solution.py:70
  7.9 133.1 %all-gather.7.cloned.1.call-start = ((), (), s32[]{:S(2)}) async-start(), calls=%async_computation.2 | async-start | bytes 5308416 | tf_op jit(solution)/shard_map/all_gather | solution.py:72
  8.6 253.5 %reduce-scatter.2.cloned.1.call-start = ((), (), s32[]{:S(2)}) async-start(), calls=%async_computation.3 | async-start | bytes 9437184 | tf_op jit(solution)/shard_map/reduce_scatter | solution.py:88
  190.3 0.7 copy-start.3
  190.3 1.9 copy-start.1
  190.3 10.8 %copy-start = (bf16[4,64,128]{2,1,0:T(8,128)(2,1)S(1)}, bf16[4,64,128]{2,1,0:T(8,128)(2,1)}, u32[]{:S(2)}) copy-start(bf16[4,64,128]{2,1,0:T(8,128)(2,1)} %param.13) | copy-start | bytes 196612
  190.3 19.8 %copy-start.2 = (bf16[4096,128]{1,0:T(8,128)(2,1)S(1)}, bf16[4096,128]{1,0:T(8,128)(2,1)}, u32[]{:S(2)}) copy-start(bf16[4096,128]{1,0:T(8,128)(2,1)} %param.11) | copy-start | bytes 3145732
Sparse Core Ops, SparseCore 0:
  9.6 92.0 all-gather.4
  103.6 37.3 all-gather.6
  190.5 71.5 reduce-scatter.1
where the time goes:
time: 271 us
  blocking collectives  76.4 us (28%)
  waiting for transfers between devices  70.4 us (26%)
  other arithmetic  47.2 us (17%)
  matrix products  38.5 us (14%)
  local copies, waits for them, and re-layouts  22.5 us (8%)
  between operations  14.5 us (5%)
    all_gather x1, waiting for transfers between devices, body(): slab = lax.all_gather(latent_cache, 'row', axis=0, tiled=True)  39.8 us
    reduce_max x32, other arithmetic, one_row(): return jnp.max(jnp.where(hit, what[:, None], -1), axis=0)  38.7 us
    unnamed x1, blocking collectives  24 us
    pmax x1, blocking collectives, body(): peak = lax.pmax(jnp.max(masked, axis=2), 'ctx')  23.5 us
    all_gather x1, waiting for transfers between devices, body(): lax.all_gather(query_latent, 'ctx', axis=0, tiled=True)  15.5 us
    dot_general x1, matrix products, combine(): jnp.einsum('ghs,gsd->ghd', weights, keys[:, :, :LATENT], preferred_elemen...  14.2 us
    reduce_scatter x1, waiting for transfers between devices, body(): lax.psum_scatter(sums, 'ctx', scatter_dimension=0, tiled=True)  13.8 us
    dot_general x1, matrix products, weigh(): jnp.einsum('ghd,gsd->ghs', queries, keys, preferred_element_type=jnp.floa...  11.7 us
  transfers between devices with their start and end apart: 3, of which 3 were waited for; matrix products, arithmetic and copies ran while one was open for 29% of the time, Pallas kernels for 0%

commit v1 on v0

v1 whole, which is shorter than its diff:
```python
import functools

import jax
import jax.numpy as jnp
from jax import lax
from jax.experimental import pallas as pl
from jax.experimental.pallas import tpu as pltpu
from jax.sharding import PartitionSpec as P

LATENT = 512
SCORE_DIM = 192
SEL_MOST = 256
TOK_DEV = 4096
RUN = TOK_DEV // SEL_MOST
LANES = 128
AUX = 16
SCALE = SCORE_DIM ** (-0.5) * 1.4426950408889634
VMEM = pltpu.VMEM


def whole_vmem(count):
    return [pl.BlockSpec(memory_space=VMEM)] * count


def params():
    return pltpu.CompilerParams(vmem_limit_bytes=56 * 1024 * 1024)


def table_kernel(query_ref, selected_ref, out_ref):
    rows, width, _ = query_ref.shape
    his = out_ref.shape[1] - width
    picks = selected_ref.shape[1]
    hi_at = lax.broadcasted_iota(jnp.int32, (his, picks), 0)
    lo_at = lax.broadcasted_iota(jnp.int32, (LANES, picks), 0)
    out_ref[:, :width, :] = query_ref[...]
    for row in range(rows):
        token = selected_ref[row : row + 1, :]
        offset = (token % RUN + 1).astype(jnp.float32)
        run = token // RUN
        high = (hi_at == run // LANES).astype(jnp.float32).astype(jnp.bfloat16)
        low = jnp.where(lo_at == run % LANES, offset, 0.0).astype(jnp.bfloat16)
        table = lax.dot_general(
            high, low, (((1,), (1,)), ((), ())), preferred_element_type=jnp.float32
        )
        out_ref[row, width:, :] = table.astype(jnp.bfloat16)


def with_table(query, selected, his):
    rows, width, heads = query.shape
    return pl.pallas_call(
        table_kernel,
        out_shape=jax.ShapeDtypeStruct((rows, width + his, heads), jnp.bfloat16),
        in_specs=whole_vmem(2),
        out_specs=pl.BlockSpec(memory_space=VMEM),
        compiler_params=params(),
        name="table",
    )(query, selected)


def three(value):
    first = value.astype(jnp.bfloat16).astype(jnp.float32)
    rest = value - first
    second = rest.astype(jnp.bfloat16).astype(jnp.float32)
    return [first, second, rest - second]


def aux_tile(total, peak):
    pad = jnp.zeros((AUX - 6, LANES), jnp.float32)
    return jnp.concatenate(three(total) + three(peak) + [pad], axis=0).astype(jnp.bfloat16)


def attend_kernel(blocks, shards, per, width, masked, where_ref, *refs):
    packs, slabs = refs[:blocks], refs[blocks : blocks + shards]
    outs = refs[blocks + shards : 2 * blocks + shards]
    keys = refs[2 * blocks + shards]
    rows = blocks * per
    tokens = slabs[0].shape[1]
    runs = tokens // RUN
    span = RUN * RUN
    his = packs[0].shape[1] - width
    hi_at = lax.broadcasted_iota(jnp.int32, (his, LANES), 0)
    lane_at = lax.broadcasted_iota(jnp.int32, (RUN, span), 1).astype(jnp.float32)
    tables = [
        packs[row // per][row % per, width:, :].astype(jnp.float32) for row in range(rows)
    ]
    valid = []
    for shard in range(shards):
        own = [
            jnp.sum(jnp.where(hi_at == where_ref[2 * shard], table, 0.0), axis=0, keepdims=True)
            for table in tables
        ]
        line = jnp.concatenate(own, axis=0)
        line = jnp.where(where_ref[2 * shard + 1] == 1, pltpu.roll(line, runs, 1), line)
        column = jnp.transpose(line)[:runs, :]
        base = (lax.broadcasted_iota(jnp.int32, column.shape, 0) % RUN * RUN).astype(jnp.float32)
        target = jnp.where(column > 0.0, base + column - 1.0, -1.0)
        valid.append(column)
        for at in range(runs // RUN):
            hits = [
                (lane_at == target[at * RUN : (at + 1) * RUN, row : row + 1])
                .astype(jnp.float32)
                .astype(jnp.bfloat16)
                for row in range(rows)
            ]
            picked = lax.dot_general(
                jnp.concatenate(hits, axis=0),
                slabs[shard][:, at * span : (at + 1) * span],
                (((1,), (1,)), ((), ())),
                preferred_element_type=jnp.float32,
            ).astype(jnp.bfloat16)
            start = shard * runs + at * RUN
            keys[:, start : start + RUN, :] = picked.reshape(rows, RUN, width)
    for row in range(rows):
        block, at = row // per, row % per
        mine = keys[row]
        scores = jnp.dot(mine, packs[block][at, :width, :], preferred_element_type=jnp.float32)
        if masked:
            known = jnp.concatenate([v[:, row : row + 1] for v in valid], axis=0) > 0.0
            known = jnp.broadcast_to(known, scores.shape)
            scores = jnp.where(known, scores, -1e30)
        top = jnp.max(scores, axis=0, keepdims=True)
        weights = jnp.exp2((scores - top) * SCALE)
        if masked:
            weights = jnp.where(known, weights, 0.0)
        weights = weights.astype(jnp.bfloat16)
        total = jnp.sum(weights.astype(jnp.float32), axis=0, keepdims=True)
        sums = lax.dot_general(
            weights, mine[:, :LATENT], (((0,), (0,)), ((), ())), preferred_element_type=jnp.float32
        )
        heads = sums.shape[0]
        outs[block][at * heads : (at + 1) * heads, :] = sums.astype(jnp.bfloat16)
        outs[block][per * heads :, at * LANES : (at + 1) * LANES] = aux_tile(total, top * SCALE)


def attend(packs, slabs, where, width, masked):
    blocks, shards = len(packs), len(slabs)
    per, _, heads = packs[0].shape
    slots = shards * (slabs[0].shape[1] // RUN)
    rows = blocks * per
    out = jax.ShapeDtypeStruct((per * heads + AUX, LATENT), jnp.bfloat16)
    return pl.pallas_call(
        functools.partial(attend_kernel, blocks, shards, per, width, masked),
        out_shape=[out] * blocks,
        in_specs=[pl.BlockSpec(memory_space=pltpu.SMEM)] + whole_vmem(blocks + shards),
        out_specs=whole_vmem(blocks),
        scratch_shapes=[pltpu.VMEM((rows, slots, width), jnp.bfloat16)],
        compiler_params=params(),
        cost_estimate=pl.CostEstimate(
            flops=2 * rows * slots * (heads * (width + LATENT) + RUN * RUN * width),
            bytes_accessed=rows * heads * (width + LATENT) * 2 + shards * slabs[0].size * 2,
            transcendentals=rows * slots * heads,
        ),
        name="attend",
    )(where, *packs, *slabs)


def combine_kernel(per, heads, last, *refs):
    parts, out = refs[:-1], refs[-1]
    for at in range(per):
        lanes = pl.ds(at * LANES, LANES)
        totals, peaks = [], []
        for part in parts:
            aux = part[per * heads :, lanes].astype(jnp.float32)
            totals.append(aux[0:1] + aux[1:2] + aux[2:3])
            peaks.append(aux[3:4] + aux[4:5] + aux[5:6])
        peak = functools.reduce(jnp.maximum, peaks)
        shares = [jnp.exp2(p - peak) for p in peaks]
        total = functools.reduce(jnp.add, [s * t for s, t in zip(shares, totals)])
        if last:
            shares = [s / total for s in shares]
        pad = -len(shares) % 8
        columns = jnp.transpose(
            jnp.concatenate(shares + [jnp.zeros((pad, LANES), jnp.float32)] * (pad > 0), axis=0)
        )
        mixed = None
        for i, part in enumerate(parts):
            term = part[at * heads : (at + 1) * heads, :].astype(jnp.float32) * columns[:, i : i + 1]
            mixed = term if mixed is None else mixed + term
        if last:
            out[at] = mixed.astype(jnp.bfloat16)
        else:
            out[at * heads : (at + 1) * heads, :] = mixed.astype(jnp.bfloat16)
            out[per * heads :, lanes] = aux_tile(total, peak)


def combine(parts, per, last):
    heads = (parts[0].shape[0] - AUX) // per
    shape = (per, heads, LATENT) if last else parts[0].shape
    return pl.pallas_call(
        functools.partial(combine_kernel, per, heads, last),
        out_shape=jax.ShapeDtypeStruct(shape, jnp.bfloat16),
        in_specs=whole_vmem(len(parts)),
        out_specs=pl.BlockSpec(memory_space=VMEM),
        compiler_params=params(),
        name="combine",
    )(*parts)


def index_block(iquery, gates, index_keys):
    count, heads, size = iquery.shape
    groups = count // 8
    query_blocks = iquery.reshape(groups, 8 * heads, size)
    gate_blocks = gates.astype(jnp.float32).reshape(groups, 8, heads)

    def one_block(pair):
        block, gate = pair
        logits = jnp.einsum("qd,td->qt", block, index_keys, preferred_element_type=jnp.float32)
        logits = logits.reshape(8, heads, logits.shape[1])
        return jnp.sum(gate[:, :, None] * jnp.maximum(logits, 0.0), axis=1)

    result = lax.map(one_block, (query_blocks, gate_blocks))
    return result.reshape(count, result.shape[2])


def solution(mesh):
    columns, planes = mesh.shape["ctx"], mesh.shape["row"]
    chips = columns // 2
    token_masks = [1] if planes > 1 else []
    row_masks = list(range(2, planes, 2))

    def swap(array, axis, mask):
        size = mesh.shape[axis]
        return lax.ppermute(array, axis, [(i, i ^ mask) for i in range(size)])

    def body(latent_cache, index_keys, query_latent, index_query, index_gates, selected):
        here, plane = lax.axis_index("ctx"), lax.axis_index("row")
        per, _, width = query_latent.shape
        tokens = latent_cache.shape[0]
        all_runs = tokens * columns * planes // RUN
        his = all_runs // LANES
        masked = all_runs != selected.shape[1]
        slab = jnp.swapaxes(latent_cache, 0, 1)
        query = jnp.swapaxes(query_latent, 1, 2)

        packed = with_table(query, selected, his)
        slabs, where = [], []
        for mask in [0] + token_masks:
            one = swap(slab, "row", mask) if mask else slab
            slabs += [one, swap(one, "ctx", 1)]
            for column in (here, here ^ 1):
                start = (column * planes + (plane ^ mask)) * (tokens // RUN)
                where += [start // LANES, start % LANES // (tokens // RUN)]
        where = jnp.stack(where).astype(jnp.int32)

        groups = {}
        for mask in row_masks + [0]:
            first = swap(packed, "row", mask) if mask else packed
            groups[mask] = [first] + [swap(first, "ctx", 2 * p) for p in range(1, chips)]

        iquery = lax.all_gather(index_query, "ctx", axis=0, tiled=True)
        gates = lax.all_gather(index_gates, "ctx", axis=0, tiled=True)
        index_scores = index_block(iquery, gates, index_keys)

        parts = []
        for mask in row_masks + [0]:
            packs, done = groups[mask], []
            step = min(4, chips)
            for at in range(0, chips, step):
                done += attend(packs[at : at + step], slabs, where, width, masked)
            mine = [done[0]] + [swap(done[p], "ctx", 2 * p) for p in range(1, chips)]
            if mask:
                parts.append(swap(combine(mine, per, False), "row", mask))
            else:
                parts += mine
        attended = combine(parts, per, True)
        return attended, index_scores

    return jax.shard_map(
        body,
        mesh=mesh,
        in_specs=(
            P(("ctx", "row"), None),
            P("ctx", None),
            P(("row", "ctx"), None, None),
            P(("row", "ctx"), None, None),
            P(("row", "ctx"), None),
            P(("row", "ctx"), None),
        ),
        out_specs=(P(("row", "ctx"), None, None), P("row", "ctx")),
        check_vma=False,
    )
```

time: 271 us -> 198 us (0.73)
  other arithmetic: 47.2 us -> 0.01 us
  Pallas kernels: 0 us -> 33 us
  matrix products: 38.5 us -> 10 us
  starting transfers between devices: 0.11 us -> 23.1 us
  blocking collectives: 76.4 us -> 56.1 us
  local copies, waits for them, and re-layouts: 22.5 us -> 5.19 us
  between operations: 14.5 us -> 0.72 us
    ppermute x0 -> x17, waiting for transfers between devices: none -> 69.6 us  [swap(): return lax.ppermute(array, axis, [(i, i ^ mask) for i in range(size)])]
    all_gather x2 -> x0, waiting for transfers between devices: 55.3 us -> none  [the longest x1 39.8 us: body(): slab = lax.all_gather(latent_cache, 'row', axis=0, tiled=True)]
    reduce_max x32 -> x0, other arithmetic: 38.7 us -> none  [one_row(): return jnp.max(jnp.where(hit, what[:, None], -1), axis=0)]
    dot_general x3 -> x0, matrix products: 33.4 us -> none  [the longest x1 14.2 us: combine(): jnp.einsum('ghs,gsd->ghd', weights, keys[:, :, :LATENT], preferred_elemen...]
    pallas_call x0 -> x5, Pallas kernels: none -> 33 us  [the longest x2 24.1 us: attend(): pl.pallas_call(functools.partial(attend_kernel, blocks, shards, per, widt...]
    all_gather x3 -> x2, blocking collectives: 28.9 us -> 56.1 us  [the longest x1 29.9 us: body(): iquery = lax.all_gather(index_query, 'ctx', axis=0, tiled=True)]
    unnamed x1 -> x0, blocking collectives: 24 us -> none
    pmax x1 -> x0, blocking collectives: 23.5 us -> none  [body(): peak = lax.pmax(jnp.max(masked, axis=2), 'ctx')]
  transfers between devices with their start and end apart: 3 -> 17, of which waited for: 3 -> 5; matrix products, arithmetic and copies ran while one was open for 29% -> 7% of each run, Pallas kernels for 0% -> 15%
where the time goes in v1:
time: 198 us
  waiting for transfers between devices  69.6 us (35%)
  blocking collectives  56.1 us (28%)
  Pallas kernels  33 us (17%)
  starting transfers between devices  23.1 us (12%)
  matrix products  10 us (5%)
  local copies, waits for them, and re-layouts  5.19 us (3%)
    ppermute x17, waiting for transfers between devices, swap(): return lax.ppermute(array, axis, [(i, i ^ mask) for i in range(size)])  69.6 us
    all_gather x1, blocking collectives, body(): iquery = lax.all_gather(index_query, 'ctx', axis=0, tiled=True)  29.9 us
    all_gather x1, blocking collectives, body(): gates = lax.all_gather(index_gates, 'ctx', axis=0, tiled=True)  26.2 us
    pallas_call x2, Pallas kernels, attend(): pl.pallas_call(functools.partial(attend_kernel, blocks, shards, per, widt...  24.1 us
    ppermute x17, starting transfers between devices, swap(): return lax.ppermute(array, axis, [(i, i ^ mask) for i in range(size)])  23.1 us
    dot_general x4, matrix products, one_block(): jnp.einsum('qd,td->qt', block, index_keys, preferred_element_type=jnp.flo...  10 us
    pallas_call x2, Pallas kernels, combine(): pl.pallas_call(functools.partial(combine_kernel, per, heads, last), out_s...  6.36 us
  transfers between devices with their start and end apart: 17, of which 5 were waited for; matrix products, arithmetic and copies ran while one was open for 7% of the time, Pallas kernels for 15%

profile of v1, /device:TPU:0, one launch (start us, length us, event | category | flops | bytes accessed | tf_op | source)
XLA Modules:
  0.0 197.8 jit_solution(11015289435231941861)
XLA Ops:
  0.6 3.1 %collective-permute-start.5 = (bf16[576,1024]{1,0:T(8,128)(2,1)}, bf16[576,1024]{1,0:T(8,128)(2,1)S(1)}, u32[]{:S(2)}, u32[]{:S(2)}) collective-permute-start(bf16[576,1024]{1,0:T(8,128)(2,1)} %bitcast.41), channel_id=1, source_target_pairs={{0,1},{1,0},{2,3},{3,2},{4,5},{5,4},{6,7},{7,6},{8,9},{9,8},{10,11... | collective-permute-start | bytes 3538952 | tf_op jit(solution)/shard_map/ppermute | solution.py:223
  3.7 0.0 collective-permute-start.4
  3.7 2.5 %table.1.refs_0_ = bf16[4,592,128]{2,1,0:T(8,128)(2,1)} custom-call(bf16[4,576,128]{2,1,0:T(8,128)(2,1)} %bitcast.38, s32[4,2048]{1,0:T(4,128)} %selected_ref.1), custom_call_target="tpu_custom_call" | custom-call | tf_op jit(solution)/shard_map/table/pallas_call | solution.py:50
  6.3 2.6 %collective-permute-start = (bf16[4,592,128]{2,1,0:T(8,128)(2,1)}, bf16[4,592,128]{2,1,0:T(8,128)(2,1)}, u32[]{:S(2)}, u32[]{:S(2)}) collective-permute-start(bf16[4,592,128]{2,1,0:T(8,128)(2,1)} %table.1.refs_0_), channel_id=1, source_target_pairs={{0,2},{1,3},{2,0},{3,1},{4,6},{5,7},{6,4},{7,5},{8,10},{9,11},{10,... | collective-permute-start | bytes 1818632 | tf_op jit(solution)/shard_map/ppermute | solution.py:223
  8.9 34.0 %collective-permute-done.5.refs_6_ = bf16[576,1024]{1,0:T(8,128)(2,1)S(1)} collective-permute-done((bf16[576,1024]{1,0:T(8,128)(2,1)}, bf16[576,1024]{1,0:T(8,128)(2,1)S(1)}, u32[]{:S(2)}, u32[]{:S(2)}) %collective-permute-start.5) | collective-permute-done | bytes 1179680 | tf_op jit(solution)/shard_map/ppermute | solution.py:223
  42.9 0.0 collective-permute-start.6
  42.9 0.0 collective-permute-done.refs_0_
  42.9 1.7 collective-permute-start.1
  44.6 1.5 collective-permute-start.2
  46.2 0.3 collective-permute-start.3
  46.5 0.0 collective-permute-done.4.refs_5_
  46.5 1.7 collective-permute-start.11
  48.1 11.7 %collective-permute-done.1.refs_1_ = bf16[4,592,128]{2,1,0:T(8,128)(2,1)} collective-permute-done((bf16[4,592,128]{2,1,0:T(8,128)(2,1)}, bf16[4,592,128]{2,1,0:T(8,128)(2,1)}, u32[]{:S(2)}, u32[]{:S(2)}) %collective-permute-start.1) | collective-permute-done | bytes 606240 | tf_op jit(solution)/shard_map/ppermute | solution.py:223
  59.8 1.7 collective-permute-start.12
  61.5 12.1 %collective-permute-done.2.refs_2_ = bf16[4,592,128]{2,1,0:T(8,128)(2,1)} collective-permute-done((bf16[4,592,128]{2,1,0:T(8,128)(2,1)}, bf16[4,592,128]{2,1,0:T(8,128)(2,1)}, u32[]{:S(2)}, u32[]{:S(2)}) %collective-permute-start.2) | collective-permute-done | bytes 606240 | tf_op jit(solution)/shard_map/ppermute | solution.py:223
  73.6 1.7 collective-permute-start.13
  75.3 0.6 stack.35.where_ref
  75.9 26.2 %all-gather = bf16[8,4,64]{2,1,0:T(4,128)(2,1)S(1)} all-gather(bf16[1,4,64]{2,1,0:T(4,128)(2,1)S(1)} %bitcast.40), channel_id=1, replica_groups=mesh['ctx'=8,'row'=4] {'ctx'}, dimensions={0}, use_global_device_ids=true | all-gather | bytes 4608 | tf_op jit(solution)/shard_map/all_gather | solution.py:251
  102.1 0.0 collective-permute-done.3.refs_3_
  102.1 0.0 collective-permute-done.6.refs_7_
  102.1 12.1 %attend.2 = (bf16[528,512]{1,0:T(8,128)(2,1)}, bf16[528,512]{1,0:T(8,128)(2,1)}, bf16[528,512]{1,0:T(8,128)(2,1)}, bf16[528,512]{1,0:T(8,128)(2,1)}) custom-call(s32[8]{0:T(128)} %stack.35.where_ref, bf16[4,592,128]{2,1,0:T(8,128)(2,1)} %collective-permute-done.refs_0_, bf16[4,592,128]{2,1,0:T(8,128)(2,1)} %collective-permute-done.1.refs_1_, ...), custom_call_target="tpu_custom_call" | custom-call | flops 2348810240 | bytes 9175040 | tf_op jit(solution)/shard_map/attend/pallas_call | solution.py:141
  114.2 2.0 %collective-permute-start.7 = (bf16[528,512]{1,0:T(8,128)(2,1)}, bf16[528,512]{1,0:T(8,128)(2,1)S(1)}, u32[]{:S(2)}, u32[]{:S(2)}) collective-permute-start(bf16[528,512]{1,0:T(8,128)(2,1)} %get-tuple-element.38), channel_id=1, source_target_pairs={{0,8},{4,12},{8,0},{12,4},{16,24},{20,28},{24,16},{28,20},{1,9},{5... | collective-permute-start | bytes 1622024 | tf_op jit(solution)/shard_map/ppermute | solution.py:223
  116.2 1.5 collective-permute-start.8
  117.7 0.0 collective-permute-done.11.refs_1_
  117.7 0.0 collective-permute-start.9
  117.8 29.9 %all_gather.7 = bf16[32,64,128]{2,1,0:T(8,128)(2,1)S(1)} all-gather(bf16[4,64,128]{2,1,0:T(8,128)(2,1)S(1)} %copy-done.7), channel_id=1, replica_groups=mesh['ctx'=8,'row'=4] {'ctx'}, dimensions={0}, use_global_device_ids=true | all-gather | bytes 589824 | tf_op jit(solution)/shard_map/all_gather | solution.py:250
  147.7 12.0 %attend.3 = (bf16[528,512]{1,0:T(8,128)(2,1)}, bf16[528,512]{1,0:T(8,128)(2,1)}, bf16[528,512]{1,0:T(8,128)(2,1)}, bf16[528,512]{1,0:T(8,128)(2,1)}) custom-call(s32[8]{0:T(128)} %stack.35.where_ref, bf16[4,592,128]{2,1,0:T(8,128)(2,1)} %table.1.refs_0_, bf16[4,592,128]{2,1,0:T(8,128)(2,1)} %copy-done.11, ...), custom_call_target="tpu_custom_call" | custom-call | flops 2348810240 | bytes 9175040 | tf_op jit(solution)/shard_map/attend/pallas_call | solution.py:141
  159.7 0.4 collective-permute-start.14
  160.2 1.6 collective-permute-start.15
  161.8 0.0 collective-permute-done.7.refs_1_
  161.8 1.5 collective-permute-start.16
  163.3 0.8 copy-done.5
  164.1 0.2 copy-done.6
  164.2 3.1 %combine.2 = bf16[528,512]{1,0:T(8,128)(2,1)} custom-call(bf16[528,512]{1,0:T(8,128)(2,1)} %get-tuple-element.37.refs_0_, bf16[528,512]{1,0:T(8,128)(2,1)} %copy-done.4, bf16[528,512]{1,0:T(8,128)(2,1)} %copy-done.5, bf16[528,512]{1,0:T(8,128)(2,1)} %copy-done.6), custom_call_target="tpu_custom_call" | custom-call | tf_op jit(solution)/shard_map/combine/pallas_call | solution.py:189
  167.3 1.8 collective-permute-start.10
  169.1 12.9 %while.10 = (s32[]{:T(128)}, f32[4,8,4096]{2,1,0:T(8,128)}, f32[4,8,64]{2,1,0:T(8,128)S(1)}, bf16[4,512,128]{2,1,0:T(8,128)(2,1)S(1)}, bf16[4096,128]{1,0:T(8,128)(2,1)}, /*index=5*/s32[]{:T(128)}) while((s32[]{:T(128)}, f32[4,8,4096]{2,1,0:T(8,128)}, f32[4,8,64]{2,1,0:T(8,128)S(1)}, bf16[4,512,128]{2,1,0:T(8,128)(2,1)S(1)}, ...), condition=%wide.region_2.3_spmd, body=%wide.region_0.2_spmd.sunk | while | flops 543129600 | bytes 1841241 | solution.py:211
  169.1 2.5 %multiply_reduce_fusion.2 = f32[8,4096]{1,0:T(8,128)S(1)} fusion(bf16[8,64,128]{2,1,0:T(8,128)(2,1)S(1)} %bitcast.36, f32[8,64]{1,0:T(8,128)S(1)} %dynamic-slice_bitcast_fusion.2, bf16[4096,128]{1,0:T(8,128)(2,1)} %get-tuple-element.103), kind=kOutput, calls=%fused_computation.clone.1 | convolution fusion | flops 543129600 | bytes 1312768 | tf_op jit(solution)/shard_map/while/body/eval_jaxpr/qd,td->qt/dot_general | solution.py:207
  171.7 0.7 bitcast_dynamic-update-slice_fusion.2
  172.4 2.5 %multiply_reduce_fusion.2 = f32[8,4096]{1,0:T(8,128)S(1)} fusion(bf16[8,64,128]{2,1,0:T(8,128)(2,1)S(1)} %bitcast.36, f32[8,64]{1,0:T(8,128)S(1)} %dynamic-slice_bitcast_fusion.2, bf16[4096,128]{1,0:T(8,128)(2,1)} %get-tuple-element.103), kind=kOutput, calls=%fused_computation.clone.1 | convolution fusion | flops 543129600 | bytes 1312768 | tf_op jit(solution)/shard_map/while/body/eval_jaxpr/qd,td->qt/dot_general | solution.py:207
  174.9 0.7 bitcast_dynamic-update-slice_fusion.2
  175.6 2.5 %multiply_reduce_fusion.2 = f32[8,4096]{1,0:T(8,128)S(1)} fusion(bf16[8,64,128]{2,1,0:T(8,128)(2,1)S(1)} %bitcast.36, f32[8,64]{1,0:T(8,128)S(1)} %dynamic-slice_bitcast_fusion.2, bf16[4096,128]{1,0:T(8,128)(2,1)} %get-tuple-element.103), kind=kOutput, calls=%fused_computation.clone.1 | convolution fusion | flops 543129600 | bytes 1312768 | tf_op jit(solution)/shard_map/while/body/eval_jaxpr/qd,td->qt/dot_general | solution.py:207
  178.1 0.7 bitcast_dynamic-update-slice_fusion.2
  178.8 2.5 %multiply_reduce_fusion.2 = f32[8,4096]{1,0:T(8,128)S(1)} fusion(bf16[8,64,128]{2,1,0:T(8,128)(2,1)S(1)} %bitcast.36, f32[8,64]{1,0:T(8,128)S(1)} %dynamic-slice_bitcast_fusion.2, bf16[4096,128]{1,0:T(8,128)(2,1)} %get-tuple-element.103), kind=kOutput, calls=%fused_computation.clone.1 | convolution fusion | flops 543129600 | bytes 1312768 | tf_op jit(solution)/shard_map/while/body/eval_jaxpr/qd,td->qt/dot_general | solution.py:207
  181.3 0.7 bitcast_dynamic-update-slice_fusion.2
  182.0 4.2 %collective-permute-done.15.refs_3_ = bf16[528,512]{1,0:T(8,128)(2,1)S(1)} collective-permute-done((bf16[528,512]{1,0:T(8,128)(2,1)}, bf16[528,512]{1,0:T(8,128)(2,1)S(1)}, u32[]{:S(2)}, u32[]{:S(2)}) %collective-permute-start.15) | collective-permute-done | bytes 540704 | tf_op jit(solution)/shard_map/ppermute | solution.py:223
  186.2 7.5 %collective-permute-done.10.refs_0_ = bf16[528,512]{1,0:T(8,128)(2,1)S(1)} collective-permute-done((bf16[528,512]{1,0:T(8,128)(2,1)}, bf16[528,512]{1,0:T(8,128)(2,1)S(1)}, u32[]{:S(2)}, u32[]{:S(2)}) %collective-permute-start.10) | collective-permute-done | bytes 540704 | tf_op jit(solution)/shard_map/ppermute | solution.py:223
  193.7 0.8 copy-done.3
  194.5 3.3 %combine.3 = bf16[4,128,512]{2,1,0:T(8,128)(2,1)} custom-call(bf16[528,512]{1,0:T(8,128)(2,1)} %copy-done.3, bf16[528,512]{1,0:T(8,128)(2,1)} %get-tuple-element.41.refs_1_, bf16[528,512]{1,0:T(8,128)(2,1)} %copy-done, bf16[528,512]{1,0:T(8,128)(2,1)} %copy-done.1, bf16[528,512]{1,0:T(8,128)(2,1)} %copy-done.2), custom_call_target="tpu_custom_call" | custom-call | tf_op jit(solution)/shard_map/combine/pallas_call | solution.py:189
  (37 shorter events, 0.1 us)
Async XLA Ops:
  0.6 75.3 %copy-start.8 = (bf16[4,64]{1,0:T(4,128)(2,1)S(1)}, bf16[4,64]{1,0:T(4,128)(2,1)}, u32[]{:S(2)}) copy-start(bf16[4,64]{1,0:T(4,128)(2,1)} %param.12) | copy-start | bytes 1540
  0.6 42.3 %collective-permute-start.5 = (bf16[576,1024]{1,0:T(8,128)(2,1)}, bf16[576,1024]{1,0:T(8,128)(2,1)S(1)}, u32[]{:S(2)}, u32[]{:S(2)}) collective-permute-start(bf16[576,1024]{1,0:T(8,128)(2,1)} %bitcast.41), channel_id=1, source_target_pairs={{0,1},{1,0},{2,3},{3,2},{4,5},{5,4},{6,7},{7,6},{8,9},{9,8},{10,11... | collective-permute-start | bytes 3538952 | tf_op jit(solution)/shard_map/ppermute | solution.py:223
  3.7 42.7 %collective-permute-start.4 = (bf16[576,1024]{1,0:T(8,128)(2,1)}, bf16[576,1024]{1,0:T(8,128)(2,1)S(1)}, u32[]{:S(2)}, u32[]{:S(2)}) collective-permute-start(bf16[576,1024]{1,0:T(8,128)(2,1)} %bitcast.42), channel_id=1, source_target_pairs={{0,4},{4,0},{8,12},{12,8},{16,20},{20,16},{24,28},{28,24},{1,5},{5... | collective-permute-start | bytes 3538952 | tf_op jit(solution)/shard_map/ppermute | solution.py:223
  6.3 36.6 %collective-permute-start = (bf16[4,592,128]{2,1,0:T(8,128)(2,1)}, bf16[4,592,128]{2,1,0:T(8,128)(2,1)}, u32[]{:S(2)}, u32[]{:S(2)}) collective-permute-start(bf16[4,592,128]{2,1,0:T(8,128)(2,1)} %table.1.refs_0_), channel_id=1, source_target_pairs={{0,2},{1,3},{2,0},{3,1},{4,6},{5,7},{6,4},{7,5},{8,10},{9,11},{10,... | collective-permute-start | bytes 1818632 | tf_op jit(solution)/shard_map/ppermute | solution.py:223
  42.9 59.2 %copy-start.9 = (bf16[576,1024]{1,0:T(8,128)(2,1)}, bf16[576,1024]{1,0:T(8,128)(2,1)S(1)}, u32[]{:S(2)}) copy-start(bf16[576,1024]{1,0:T(8,128)(2,1)S(1)} %collective-permute-done.5.refs_6_) | copy-start | bytes 3538948
  42.9 59.2 %collective-permute-start.6 = (bf16[576,1024]{1,0:T(8,128)(2,1)S(1)}, bf16[576,1024]{1,0:T(8,128)(2,1)}, u32[]{:S(2)}, u32[]{:S(2)}) collective-permute-start(bf16[576,1024]{1,0:T(8,128)(2,1)S(1)} %collective-permute-done.5.refs_6_), channel_id=1, source_target_pairs={{0,4},{4,0},{8,12},{12,8},{16,20},{20,16},{24,28},{28,24},{1,5},{5... | collective-permute-start | bytes 3538952 | tf_op jit(solution)/shard_map/ppermute | solution.py:223
  42.9 16.9 %collective-permute-start.1 = (bf16[4,592,128]{2,1,0:T(8,128)(2,1)}, bf16[4,592,128]{2,1,0:T(8,128)(2,1)}, u32[]{:S(2)}, u32[]{:S(2)}) collective-permute-start(bf16[4,592,128]{2,1,0:T(8,128)(2,1)} %collective-permute-done.refs_0_), channel_id=1, source_target_pairs={{0,8},{4,12},{8,0},{12,4},{16,24},{20,28},{24,16},{28,20},{1,9},{5... | collective-permute-start | bytes 1818632 | tf_op jit(solution)/shard_map/ppermute | solution.py:223
  44.6 29.0 %collective-permute-start.2 = (bf16[4,592,128]{2,1,0:T(8,128)(2,1)}, bf16[4,592,128]{2,1,0:T(8,128)(2,1)}, u32[]{:S(2)}, u32[]{:S(2)}) collective-permute-start(bf16[4,592,128]{2,1,0:T(8,128)(2,1)} %collective-permute-done.refs_0_), channel_id=1, source_target_pairs={{0,16},{4,20},{8,24},{12,28},{16,0},{20,4},{24,8},{28,12},{1,17},{... | collective-permute-start | bytes 1818632 | tf_op jit(solution)/shard_map/ppermute | solution.py:223
  46.2 55.9 %collective-permute-start.3 = (bf16[4,592,128]{2,1,0:T(8,128)(2,1)}, bf16[4,592,128]{2,1,0:T(8,128)(2,1)}, u32[]{:S(2)}, u32[]{:S(2)}) collective-permute-start(bf16[4,592,128]{2,1,0:T(8,128)(2,1)} %collective-permute-done.refs_0_), channel_id=1, source_target_pairs={{0,24},{4,28},{8,16},{12,20},{16,8},{20,12},{24,0},{28,4},{1,25},{... | collective-permute-start | bytes 1818632 | tf_op jit(solution)/shard_map/ppermute | solution.py:223
  46.5 55.6 %copy-start.10 = (bf16[576,1024]{1,0:T(8,128)(2,1)}, bf16[576,1024]{1,0:T(8,128)(2,1)S(1)}, u32[]{:S(2)}) copy-start(bf16[576,1024]{1,0:T(8,128)(2,1)S(1)} %collective-permute-done.4.refs_5_) | copy-start | bytes 3538948
  46.5 71.3 %collective-permute-start.11 = (bf16[4,592,128]{2,1,0:T(8,128)(2,1)}, bf16[4,592,128]{2,1,0:T(8,128)(2,1)S(1)}, u32[]{:S(2)}, u32[]{:S(2)}) collective-permute-start(bf16[4,592,128]{2,1,0:T(8,128)(2,1)} %table.1.refs_0_), channel_id=1, source_target_pairs={{0,8},{4,12},{8,0},{12,4},{16,24},{20,28},{24,16},{28,20},{1,9},{5... | collective-permute-start | bytes 1818632 | tf_op jit(solution)/shard_map/ppermute | solution.py:223
  59.8 87.9 %collective-permute-start.12 = (bf16[4,592,128]{2,1,0:T(8,128)(2,1)}, bf16[4,592,128]{2,1,0:T(8,128)(2,1)}, u32[]{:S(2)}, u32[]{:S(2)}) collective-permute-start(bf16[4,592,128]{2,1,0:T(8,128)(2,1)} %table.1.refs_0_), channel_id=1, source_target_pairs={{0,16},{4,20},{8,24},{12,28},{16,0},{20,4},{24,8},{28,12},{1,17},{... | collective-permute-start | bytes 1818632 | tf_op jit(solution)/shard_map/ppermute | solution.py:223
  73.6 74.1 %collective-permute-start.13 = (bf16[4,592,128]{2,1,0:T(8,128)(2,1)}, bf16[4,592,128]{2,1,0:T(8,128)(2,1)}, u32[]{:S(2)}, u32[]{:S(2)}) collective-permute-start(bf16[4,592,128]{2,1,0:T(8,128)(2,1)} %table.1.refs_0_), channel_id=1, source_target_pairs={{0,24},{4,28},{8,16},{12,20},{16,8},{20,12},{24,0},{28,4},{1,25},{... | collective-permute-start | bytes 1818632 | tf_op jit(solution)/shard_map/ppermute | solution.py:223
  102.1 15.7 %copy-start.7 = (bf16[4,64,128]{2,1,0:T(8,128)(2,1)S(1)}, bf16[4,64,128]{2,1,0:T(8,128)(2,1)}, u32[]{:S(2)}) copy-start(bf16[4,64,128]{2,1,0:T(8,128)(2,1)} %param.11) | copy-start | bytes 196612
  114.2 47.6 %collective-permute-start.7 = (bf16[528,512]{1,0:T(8,128)(2,1)}, bf16[528,512]{1,0:T(8,128)(2,1)S(1)}, u32[]{:S(2)}, u32[]{:S(2)}) collective-permute-start(bf16[528,512]{1,0:T(8,128)(2,1)} %get-tuple-element.38), channel_id=1, source_target_pairs={{0,8},{4,12},{8,0},{12,4},{16,24},{20,28},{24,16},{28,20},{1,9},{5... | collective-permute-start | bytes 1622024 | tf_op jit(solution)/shard_map/ppermute | solution.py:223
  116.2 47.1 %collective-permute-start.8 = (bf16[528,512]{1,0:T(8,128)(2,1)}, bf16[528,512]{1,0:T(8,128)(2,1)S(1)}, u32[]{:S(2)}, u32[]{:S(2)}) collective-permute-start(bf16[528,512]{1,0:T(8,128)(2,1)} %get-tuple-element.39), channel_id=1, source_target_pairs={{0,16},{4,20},{8,24},{12,28},{16,0},{20,4},{24,8},{28,12},{1,17},{... | collective-permute-start | bytes 1622024 | tf_op jit(solution)/shard_map/ppermute | solution.py:223
  117.7 30.0 %copy-start.11 = (bf16[4,592,128]{2,1,0:T(8,128)(2,1)}, bf16[4,592,128]{2,1,0:T(8,128)(2,1)S(1)}, u32[]{:S(2)}) copy-start(bf16[4,592,128]{2,1,0:T(8,128)(2,1)S(1)} %collective-permute-done.11.refs_1_) | copy-start | bytes 1818628
  117.7 45.5 %collective-permute-start.9 = (bf16[528,512]{1,0:T(8,128)(2,1)}, bf16[528,512]{1,0:T(8,128)(2,1)S(1)}, u32[]{:S(2)}, u32[]{:S(2)}) collective-permute-start(bf16[528,512]{1,0:T(8,128)(2,1)} %get-tuple-element.40), channel_id=1, source_target_pairs={{0,24},{4,28},{8,16},{12,20},{16,8},{20,12},{24,0},{28,4},{1,25},{... | collective-permute-start | bytes 1622024 | tf_op jit(solution)/shard_map/ppermute | solution.py:223
  159.7 22.2 %collective-permute-start.14 = (bf16[528,512]{1,0:T(8,128)(2,1)}, bf16[528,512]{1,0:T(8,128)(2,1)S(1)}, u32[]{:S(2)}, u32[]{:S(2)}) collective-permute-start(bf16[528,512]{1,0:T(8,128)(2,1)} %get-tuple-element.42), channel_id=1, source_target_pairs={{0,8},{4,12},{8,0},{12,4},{16,24},{20,28},{24,16},{28,20},{1,9},{5... | collective-permute-start | bytes 1622024 | tf_op jit(solution)/shard_map/ppermute | solution.py:223
  160.2 26.0 %collective-permute-start.15 = (bf16[528,512]{1,0:T(8,128)(2,1)}, bf16[528,512]{1,0:T(8,128)(2,1)S(1)}, u32[]{:S(2)}, u32[]{:S(2)}) collective-permute-start(bf16[528,512]{1,0:T(8,128)(2,1)} %get-tuple-element.43), channel_id=1, source_target_pairs={{0,16},{4,20},{8,24},{12,28},{16,0},{20,4},{24,8},{28,12},{1,17},{... | collective-permute-start | bytes 1622024 | tf_op jit(solution)/shard_map/ppermute | solution.py:223
  161.8 1.5 copy-start.4
  161.8 24.4 %collective-permute-start.16 = (bf16[528,512]{1,0:T(8,128)(2,1)}, bf16[528,512]{1,0:T(8,128)(2,1)S(1)}, u32[]{:S(2)}, u32[]{:S(2)}) collective-permute-start(bf16[528,512]{1,0:T(8,128)(2,1)} %get-tuple-element.44), channel_id=1, source_target_pairs={{0,24},{4,28},{8,16},{12,20},{16,8},{20,12},{24,0},{28,4},{1,25},{... | collective-permute-start | bytes 1622024 | tf_op jit(solution)/shard_map/ppermute | solution.py:223
  163.3 0.8 copy-start.5
  163.3 1.0 copy-start.6
  167.3 26.4 %collective-permute-start.10 = (bf16[528,512]{1,0:T(8,128)(2,1)}, bf16[528,512]{1,0:T(8,128)(2,1)S(1)}, u32[]{:S(2)}, u32[]{:S(2)}) collective-permute-start(bf16[528,512]{1,0:T(8,128)(2,1)} %combine.2), channel_id=1, source_target_pairs={{0,2},{1,3},{2,0},{3,1},{4,6},{5,7},{6,4},{7,5},{8,10},{9,11},{10,... | collective-permute-start | bytes 1622024 | tf_op jit(solution)/shard_map/ppermute | solution.py:223
  182.0 11.7 %copy-start = (bf16[528,512]{1,0:T(8,128)(2,1)}, bf16[528,512]{1,0:T(8,128)(2,1)S(1)}, u32[]{:S(2)}) copy-start(bf16[528,512]{1,0:T(8,128)(2,1)S(1)} %collective-permute-done.14.refs_2_) | copy-start | bytes 1622020
  186.2 7.5 %copy-start.1 = (bf16[528,512]{1,0:T(8,128)(2,1)}, bf16[528,512]{1,0:T(8,128)(2,1)S(1)}, u32[]{:S(2)}) copy-start(bf16[528,512]{1,0:T(8,128)(2,1)S(1)} %collective-permute-done.15.refs_3_) | copy-start | bytes 1622020
  186.2 7.5 %copy-start.2 = (bf16[528,512]{1,0:T(8,128)(2,1)}, bf16[528,512]{1,0:T(8,128)(2,1)S(1)}, u32[]{:S(2)}) copy-start(bf16[528,512]{1,0:T(8,128)(2,1)S(1)} %collective-permute-done.16.refs_4_) | copy-start | bytes 1622020
  193.7 0.8 copy-start.3

commit v2 on v1

v2 whole, which is shorter than its diff:
```python
import functools

import jax
import jax.numpy as jnp
from jax import lax
from jax.experimental import pallas as pl
from jax.experimental.pallas import tpu as pltpu
from jax.sharding import PartitionSpec as P

LATENT = 512
SCORE_DIM = 192
SEL_MOST = 256
TOK_DEV = 4096
RUN = TOK_DEV // SEL_MOST
LANES = 128
AUX = 16
BATCH = 4
SCALE = SCORE_DIM ** (-0.5) * 1.4426950408889634
VMEM = pltpu.VMEM
TINY = pl.CostEstimate(flops=1000, bytes_accessed=1000, transcendentals=0)


def whole_vmem(count):
    return [pl.BlockSpec(memory_space=VMEM)] * count


def params(mib):
    return pltpu.CompilerParams(vmem_limit_bytes=mib * 1024 * 1024)


def near(arrays):
    return [pltpu.with_memory_space_constraint(a, VMEM) for a in arrays]


def table_kernel(query_ref, selected_ref, out_ref):
    rows, width, _ = query_ref.shape
    his = out_ref.shape[1] - width
    picks = selected_ref.shape[1]
    hi_at = lax.broadcasted_iota(jnp.int32, (his, picks), 0)
    lo_at = lax.broadcasted_iota(jnp.int32, (LANES, picks), 0)
    out_ref[:, :width, :] = query_ref[...]
    for row in range(rows):
        token = selected_ref[row : row + 1, :]
        offset = (token % RUN + 1).astype(jnp.float32)
        run = token // RUN
        high = (hi_at == run // LANES).astype(jnp.float32).astype(jnp.bfloat16)
        low = jnp.where(lo_at == run % LANES, offset, 0.0).astype(jnp.bfloat16)
        table = lax.dot_general(
            high, low, (((1,), (1,)), ((), ())), preferred_element_type=jnp.float32
        )
        out_ref[row, width:, :] = table.astype(jnp.bfloat16)


def with_table(query, selected, his):
    rows, width, heads = query.shape
    return pl.pallas_call(
        table_kernel,
        out_shape=jax.ShapeDtypeStruct((rows, width + his, heads), jnp.bfloat16),
        in_specs=whole_vmem(2),
        out_specs=pl.BlockSpec(memory_space=VMEM),
        compiler_params=params(8),
        cost_estimate=TINY,
        name="table",
    )(query, selected)


def three(value):
    first = value.astype(jnp.bfloat16).astype(jnp.float32)
    rest = value - first
    second = rest.astype(jnp.bfloat16).astype(jnp.float32)
    return [first, second, rest - second]


def aux_tile(total, peak):
    pad = jnp.zeros((AUX - 6, LANES), jnp.float32)
    return jnp.concatenate(three(total) + three(peak) + [pad], axis=0).astype(jnp.bfloat16)


def attend_kernel(blocks, shards, per, width, masked, where_ref, *refs):
    packs, slabs = refs[:blocks], refs[blocks : blocks + shards]
    outs = refs[blocks + shards : 2 * blocks + shards]
    keys = refs[2 * blocks + shards]
    rows = blocks * per
    span = RUN * RUN
    his = packs[0].shape[1] - width
    hi_at = lax.broadcasted_iota(jnp.int32, (his, LANES), 0)
    lane_at = lax.broadcasted_iota(jnp.int32, (RUN, span), 1).astype(jnp.float32)
    tables = [
        packs[row // per][row % per, width:, :].astype(jnp.float32) for row in range(rows)
    ]
    valid, begin = [], 0
    for shard in range(shards):
        runs = slabs[shard].shape[1] // RUN
        own = [
            jnp.sum(jnp.where(hi_at == where_ref[2 * shard], table, 0.0), axis=0, keepdims=True)
            for table in tables
        ]
        line = jnp.concatenate(own, axis=0)
        line = pltpu.roll(line, where_ref[2 * shard + 1], 1)
        column = jnp.transpose(line)[:runs, :]
        base = (lax.broadcasted_iota(jnp.int32, column.shape, 0) % RUN * RUN).astype(jnp.float32)
        target = jnp.where(column > 0.0, base + column - 1.0, -1.0)
        valid.append(column)
        for at in range(runs // RUN):
            hits = [
                (lane_at == target[at * RUN : (at + 1) * RUN, row : row + 1])
                .astype(jnp.float32)
                .astype(jnp.bfloat16)
                for row in range(rows)
            ]
            picked = lax.dot_general(
                jnp.concatenate(hits, axis=0),
                slabs[shard][:, at * span : (at + 1) * span],
                (((1,), (1,)), ((), ())),
                preferred_element_type=jnp.float32,
            ).astype(jnp.bfloat16)
            start = begin + at * RUN
            keys[:, start : start + RUN, :] = picked.reshape(rows, RUN, width)
        begin += runs
    for first in range(0, rows, BATCH):
        group = range(first, min(first + BATCH, rows))
        logits = [
            jnp.dot(
                keys[row],
                packs[row // per][row % per, :width, :],
                preferred_element_type=jnp.float32,
            )
            for row in group
        ]
        done = []
        for row, scores in zip(group, logits):
            if masked:
                known = jnp.concatenate([v[:, row : row + 1] for v in valid], axis=0) > 0.0
                known = jnp.broadcast_to(known, scores.shape)
                scores = jnp.where(known, scores, -1e30)
            top = jnp.max(scores, axis=0, keepdims=True)
            weights = jnp.exp2((scores - top) * SCALE)
            if masked:
                weights = jnp.where(known, weights, 0.0)
            weights = weights.astype(jnp.bfloat16)
            total = jnp.sum(weights.astype(jnp.float32), axis=0, keepdims=True)
            done.append((weights, total, top * SCALE))
        for row, (weights, total, peak) in zip(group, done):
            block, at = row // per, row % per
            sums = lax.dot_general(
                weights,
                keys[row, :, :LATENT],
                (((0,), (0,)), ((), ())),
                preferred_element_type=jnp.float32,
            )
            heads = sums.shape[0]
            outs[block][at * heads : (at + 1) * heads, :] = sums.astype(jnp.bfloat16)
            outs[block][per * heads :, at * LANES : (at + 1) * LANES] = aux_tile(total, peak)


def attend(packs, slabs, where, width, masked):
    blocks, shards = len(packs), len(slabs)
    per, _, heads = packs[0].shape
    slots = sum(slab.shape[1] for slab in slabs) // RUN
    rows = blocks * per
    out = VMEM((per * heads + AUX, LATENT), jnp.bfloat16)
    return pl.pallas_call(
        functools.partial(attend_kernel, blocks, shards, per, width, masked),
        out_shape=[out] * blocks,
        in_specs=[pl.BlockSpec(memory_space=pltpu.SMEM)] + whole_vmem(blocks + shards),
        out_specs=whole_vmem(blocks),
        scratch_shapes=[pltpu.VMEM((rows, slots, width), jnp.bfloat16)],
        compiler_params=params(14),
        cost_estimate=TINY,
        name="attend",
    )(where, *near(packs), *near(slabs))


def combine_kernel(per, heads, last, *refs):
    parts, out = refs[:-1], refs[-1]
    for at in range(per):
        lanes = pl.ds(at * LANES, LANES)
        totals, peaks = [], []
        for part in parts:
            aux = part[per * heads :, lanes].astype(jnp.float32)
            totals.append(aux[0:1] + aux[1:2] + aux[2:3])
            peaks.append(aux[3:4] + aux[4:5] + aux[5:6])
        peak = functools.reduce(jnp.maximum, peaks)
        shares = [jnp.exp2(p - peak) for p in peaks]
        total = functools.reduce(jnp.add, [s * t for s, t in zip(shares, totals)])
        if last:
            shares = [s / total for s in shares]
        pad = -len(shares) % 8
        columns = jnp.transpose(
            jnp.concatenate(shares + [jnp.zeros((pad, LANES), jnp.float32)] * (pad > 0), axis=0)
        )
        mixed = None
        for i, part in enumerate(parts):
            term = part[at * heads : (at + 1) * heads, :].astype(jnp.float32) * columns[:, i : i + 1]
            mixed = term if mixed is None else mixed + term
        if last:
            out[at] = mixed.astype(jnp.bfloat16)
        else:
            out[at * heads : (at + 1) * heads, :] = mixed.astype(jnp.bfloat16)
            out[per * heads :, lanes] = aux_tile(total, peak)


def combine(parts, per, last):
    heads = (parts[0].shape[0] - AUX) // per
    if last:
        out = jax.ShapeDtypeStruct((per, heads, LATENT), jnp.bfloat16)
    else:
        out = VMEM(parts[0].shape, jnp.bfloat16)
    return pl.pallas_call(
        functools.partial(combine_kernel, per, heads, last),
        out_shape=out,
        in_specs=whole_vmem(len(parts)),
        out_specs=pl.BlockSpec(memory_space=VMEM),
        compiler_params=params(8),
        cost_estimate=TINY,
        name="combine",
    )(*near(parts))


def index_kernel(heads, meta_ref, keys_ref, out_ref, gate_scr):
    rows = meta_ref.shape[0]
    tokens = keys_ref.shape[0]

    @pl.when(pl.program_id(0) == 0)
    def _():
        for first in range(0, rows, 8):
            lines = jnp.concatenate(
                [meta_ref[first + i, heads : heads + 8, :].astype(jnp.float32)[:1] for i in range(8)],
                axis=0,
            )
            turned = jnp.transpose(lines)
            for i in range(8):
                gate_scr[first + i] = jnp.broadcast_to(turned[:heads, i : i + 1], (heads, LANES))

    for first in range(0, rows, 8):
        queries = jnp.concatenate([meta_ref[first + i, :heads, :] for i in range(8)], axis=0)
        logits = lax.dot_general(
            queries, keys_ref[...], (((1,), (1,)), ((), ())), preferred_element_type=jnp.float32
        )
        lines = []
        for i in range(8):
            gate = jnp.concatenate([gate_scr[first + i]] * (tokens // LANES), axis=1)
            terms = jnp.maximum(logits[i * heads : (i + 1) * heads, :], 0.0) * gate
            lines.append(jnp.sum(terms, axis=0, keepdims=True))
        out_ref[first : first + 8, :] = jnp.concatenate(lines, axis=0)


def index_block(meta, index_keys, heads):
    rows, tall, size = meta.shape
    tokens = index_keys.shape[0]
    block = 512
    return pl.pallas_call(
        functools.partial(index_kernel, heads),
        grid=(tokens // block,),
        out_shape=jax.ShapeDtypeStruct((rows, tokens), jnp.float32),
        in_specs=[
            pl.BlockSpec((rows, tall, size), lambda i: (0, 0, 0)),
            pl.BlockSpec((block, size), lambda i: (i, 0)),
        ],
        out_specs=pl.BlockSpec((rows, block), lambda i: (0, i)),
        scratch_shapes=[VMEM((rows, heads, LANES), jnp.float32)],
        compiler_params=params(14),
        cost_estimate=TINY,
        name="index",
    )(meta, index_keys)


def solution(mesh):
    columns, planes = mesh.shape["ctx"], mesh.shape["row"]
    token_columns = [0, 2] if columns > 2 else [0]
    token_planes = [0, 1] if planes > 1 else [0]
    row_columns = list(range(0, columns, 4))
    row_planes = list(range(0, planes, 2))

    def swap(array, axis, mask):
        size = mesh.shape[axis]
        return lax.ppermute(array, axis, [(i, i ^ mask) for i in range(size)])

    def body(latent_cache, index_keys, query_latent, index_query, index_gates, selected):
        here, plane = lax.axis_index("ctx"), lax.axis_index("row")
        per, _, width = query_latent.shape
        heads = index_query.shape[1]
        tokens = latent_cache.shape[0]
        runs = tokens // RUN
        all_runs = runs * columns * planes
        masked = all_runs != selected.shape[1]
        slab = jnp.swapaxes(latent_cache, 0, 1)
        query = jnp.swapaxes(query_latent, 1, 2)

        def after(array, *others):
            return lax.optimization_barrier((array, *others))[0]

        gate_rows = jnp.pad(
            index_gates[:, None, :], ((0, 0), (0, AUX - 1), (0, LANES - index_gates.shape[1]))
        )
        meta = jnp.concatenate([index_query, gate_rows], axis=1)
        bit = 1
        while bit < columns:
            other = swap(meta, "ctx", bit)
            low, high = jnp.concatenate([meta, other]), jnp.concatenate([other, meta])
            meta = jnp.where(here & bit == 0, low, high)
            bit *= 2

        packed = with_table(query, selected, all_runs // LANES)
        starts = {across: swap(packed, "row", across) if across else packed for across in row_planes}
        groups = {
            across: {mask: swap(start, "ctx", mask) if mask else start for mask in row_columns}
            for across, start in starts.items()
        }
        near_queries = list(groups[0].values()) + list(starts.values())
        far_queries = [pack for group in groups.values() for pack in group.values()]
        index_scores = index_block(after(meta, *near_queries), index_keys, heads)

        half = tokens // 2
        pieces, sent, shown = [(0, 0, slab)], [], []
        for across in token_planes[1:]:
            for offset in (0, half):
                piece = slab[:, offset : offset + half]
                sent.append(swap(after(piece, *sent[-1:]), "row", across))
                pieces.append((across, offset, sent[-1]))
        slabs, where = [], []
        for across, offset, piece in pieces:
            for mask in token_columns:
                one = piece
                if mask:
                    late = list(starts.values()) if offset else []
                    one = swap(after(piece, *late, *shown[-1:]), "ctx", mask)
                    shown.append(one)
                for core in (0, 1):
                    if core and mask and offset:
                        one = after(one, index_scores, *far_queries)
                    slabs.append(swap(one, "ctx", 1) if core else one)
                    start = (here ^ mask ^ core) * planes + (plane ^ across)
                    start = (start * tokens + offset) // RUN
                    where += [start // LANES, (-start) % LANES]
        where = jnp.stack(where).astype(jnp.int32)

        parts, last = [], after(where, index_scores)
        for across in row_planes[1:] + row_planes[:1]:
            mine = []
            for mask in reversed(row_columns):
                (done,) = attend([groups[across][mask]], slabs, last, width, masked)
                last = after(where, done)
                mine.append(swap(done, "ctx", mask) if mask else done)
            if across:
                parts.append(swap(combine(mine, per, False), "row", across))
            else:
                parts += mine
        attended = combine(parts, per, True)
        return attended, index_scores

    return jax.shard_map(
        body,
        mesh=mesh,
        in_specs=(
            P(("ctx", "row"), None),
            P("ctx", None),
            P(("row", "ctx"), None, None),
            P(("row", "ctx"), None, None),
            P(("row", "ctx"), None),
            P(("row", "ctx"), None),
        ),
        out_specs=(P(("row", "ctx"), None, None), P("row", "ctx")),
        check_vma=False,
    )
```

time: 198 us -> 116 us (0.59)
  blocking collectives: 56.1 us -> 0 us
  waiting for transfers between devices: 69.6 us -> 50.7 us
  matrix products: 10 us -> 0 us
  Pallas kernels: 33 us -> 38.1 us
  local copies, waits for them, and re-layouts: 5.19 us -> 2.89 us
    all_gather x2 -> x0, blocking collectives: 56.1 us -> none  [the longest x1 29.9 us: body(): iquery = lax.all_gather(index_query, 'ctx', axis=0, tiled=True)]
    ppermute x17 -> x20, waiting for transfers between devices: 69.6 us -> 50.7 us  [swap(): return lax.ppermute(array, axis, [(i, i ^ mask) for i in range(size)])]
    dot_general x4 -> x0, matrix products: 10 us -> none  [one_block(): jnp.einsum('qd,td->qt', block, index_keys, preferred_element_type=jnp.flo...]
    pallas_call x0 -> x1, Pallas kernels: none -> 6.82 us  [index_block(): pl.pallas_call(functools.partial(index_kernel, heads), grid=(tokens // bl...]
    pallas_call x2, Pallas kernels: 6.36 us -> 1.82 us  [combine(): pl.pallas_call(functools.partial(combine_kernel, per, heads, last), out_s...]
    pallas_call x2 -> x4, Pallas kernels: 24.1 us -> 27.9 us  [attend(): pl.pallas_call(functools.partial(attend_kernel, blocks, shards, per, widt...]
    dynamic_update_slice x4 -> x0, local copies, waits for them, and re-layouts: 2.68 us -> none  [index_block(): result = lax.map(one_block, (query_blocks, gate_blocks))]
    slice x0 -> x1, local copies, waits for them, and re-layouts: none -> 2.37 us  [body(): piece = slab[:, offset:offset + half]]
  transfers between devices with their start and end apart: 17 -> 20, of which waited for: 5 -> 9; matrix products, arithmetic and copies ran while one was open for 7% -> 3% of each run, Pallas kernels for 15% -> 26%
where the time goes in v2:
time: 116 us
  waiting for transfers between devices  50.7 us (44%)
  Pallas kernels  38.1 us (33%)
  starting transfers between devices  21.5 us (19%)
  local copies, waits for them, and re-layouts  2.89 us (2%)
  other arithmetic  1.54 us (1%)
  between operations  1.17 us (1%)
    ppermute x20, waiting for transfers between devices, swap(): return lax.ppermute(array, axis, [(i, i ^ mask) for i in range(size)])  50.7 us
    pallas_call x4, Pallas kernels, attend(): pl.pallas_call(functools.partial(attend_kernel, blocks, shards, per, widt...  27.9 us
    ppermute x20, starting transfers between devices, swap(): return lax.ppermute(array, axis, [(i, i ^ mask) for i in range(size)])  21.5 us
    pallas_call x1, Pallas kernels, index_block(): pl.pallas_call(functools.partial(index_kernel, heads), grid=(tokens // bl...  6.82 us
    slice x1, local copies, waits for them, and re-layouts, body(): piece = slab[:, offset:offset + half]  2.37 us
  transfers between devices with their start and end apart: 20, of which 9 were waited for; matrix products, arithmetic and copies ran while one was open for 3% of the time, Pallas kernels for 26%

profile of v2, /device:TPU:0, one launch (start us, length us, event | category | flops | bytes accessed | tf_op | source)
XLA Modules:
  0.0 115.9 jit_solution(18347499868410482766)
XLA Ops:
  0.7 3.0 %collective-permute-start.7 = (bf16[576,1024]{1,0:T(8,128)(2,1)}, bf16[576,1024]{1,0:T(8,128)(2,1)S(1)}, u32[]{:S(2)}, u32[]{:S(2)}) collective-permute-start(bf16[576,1024]{1,0:T(8,128)(2,1)} %bitcast.27), channel_id=1, source_target_pairs={{0,8},{4,12},{8,0},{12,4},{16,24},{20,28},{24,16},{28,20},{1,9},{5... | collective-permute-start | bytes 3538952 | tf_op jit(solution)/shard_map/ppermute | solution.py:277
  3.7 2.4 %fusion = (bf16[576,512]{1,0:T(8,128)(2,1)}, bf16[576,512]{1,0:T(8,128)(2,1)}) fusion(bf16[576,1024]{1,0:T(8,128)(2,1)} %bitcast.28), kind=kLoop, calls=%fused_computation.4 | loop fusion | bytes 2359296 | tf_op jit(solution)/shard_map/slice | solution.py:318
  6.0 1.6 %collective-permute-start.9 = (bf16[576,512]{1,0:T(8,128)(2,1)}, bf16[576,512]{1,0:T(8,128)(2,1)}, u32[]{:S(2)}, u32[]{:S(2)}) collective-permute-start(bf16[576,512]{1,0:T(8,128)(2,1)} %get-tuple-element.21), channel_id=1, source_target_pairs={{0,1},{1,0},{2,3},{3,2},{4,5},{5,4},{6,7},{7,6},{8,9},{9,8},{10,11... | collective-permute-start | bytes 1769480 | tf_op jit(solution)/shard_map/ppermute | solution.py:277
  7.6 0.0 copy-start
  7.7 0.1 collective-permute-start
  7.8 1.5 %table.1.refs_0_ = bf16[4,592,128]{2,1,0:T(8,128)(2,1)} custom-call(bf16[4,576,128]{2,1,0:T(8,128)(2,1)S(1)} %bitcast.34, s32[4,2048]{1,0:T(4,128)S(1)} %copy-done.3), custom_call_target="tpu_custom_call" | custom-call | flops 1000 | bytes 1000 | tf_op jit(solution)/shard_map/table/pallas_call | solution.py:56
  9.3 2.6 %collective-permute-start.4 = (bf16[4,592,128]{2,1,0:T(8,128)(2,1)}, bf16[4,592,128]{2,1,0:T(8,128)(2,1)}, u32[]{:S(2)}, u32[]{:S(2)}) collective-permute-start(bf16[4,592,128]{2,1,0:T(8,128)(2,1)} %table.1.refs_0_), channel_id=1, source_target_pairs={{0,2},{1,3},{2,0},{3,1},{4,6},{5,7},{6,4},{7,5},{8,10},{9,11},{10,... | collective-permute-start | bytes 1818632 | tf_op jit(solution)/shard_map/ppermute | solution.py:277
  11.9 0.6 collective-permute-start.1
  12.5 1.5 %collective-permute-start.3 = (bf16[4,592,128]{2,1,0:T(8,128)(2,1)}, bf16[4,592,128]{2,1,0:T(8,128)(2,1)}, u32[]{:S(2)}, u32[]{:S(2)}) collective-permute-start(bf16[4,592,128]{2,1,0:T(8,128)(2,1)} %table.1.refs_0_), channel_id=1, source_target_pairs={{0,16},{4,20},{8,24},{12,28},{16,0},{20,4},{24,8},{28,12},{1,17},{... | collective-permute-start | bytes 1818632 | tf_op jit(solution)/shard_map/ppermute | solution.py:277
  14.0 16.8 %collective-permute-done.9.refs_5_ = bf16[576,512]{1,0:T(8,128)(2,1)} collective-permute-done((bf16[576,512]{1,0:T(8,128)(2,1)}, bf16[576,512]{1,0:T(8,128)(2,1)}, u32[]{:S(2)}, u32[]{:S(2)}) %collective-permute-start.9) | collective-permute-done | bytes 589856 | tf_op jit(solution)/shard_map/ppermute | solution.py:277
  30.8 0.0 collective-permute-start.13
  30.8 0.0 collective-permute-done.7.refs_3_
  30.8 1.9 %collective-permute-start.11 = (bf16[576,512]{1,0:T(8,128)(2,1)}, bf16[576,512]{1,0:T(8,128)(2,1)}, u32[]{:S(2)}, u32[]{:S(2)}) collective-permute-start(bf16[576,512]{1,0:T(8,128)(2,1)} %collective-permute-done.9.refs_5_), channel_id=1, source_target_pairs={{0,8},{4,12},{8,0},{12,4},{16,24},{20,28},{24,16},{28,20},{1,9},{5... | collective-permute-start | bytes 1769480 | tf_op jit(solution)/shard_map/ppermute | solution.py:277
  32.7 1.5 %collective-permute-done.1 = bf16[8,80,128]{2,1,0:T(8,128)(2,1)S(1)} collective-permute-done((bf16[8,80,128]{2,1,0:T(8,128)(2,1)S(1)}, bf16[8,80,128]{2,1,0:T(8,128)(2,1)S(1)}, u32[]{:S(2)}, u32[]{:S(2)}) %collective-permute-start.1) | collective-permute-done | bytes 163872 | tf_op jit(solution)/shard_map/ppermute | solution.py:277
  34.2 0.0 copy-start.4
  34.2 2.1 %collective-permute-start.2 = (bf16[16,80,128]{2,1,0:T(8,128)(2,1)S(1)}, bf16[16,80,128]{2,1,0:T(8,128)(2,1)S(1)}, u32[]{:S(2)}, u32[]{:S(2)}) collective-permute-start(bf16[16,80,128]{2,1,0:T(8,128)(2,1)S(1)} %maximum_select_fusion.1), channel_id=1, source_target_pairs={{0,16},{4,20},{8,24},{12,28},{16,0},{20,4},{24,8},{28,12},{1,17},{... | collective-permute-start | bytes 983048 | tf_op jit(solution)/shard_map/ppermute | solution.py:277
  36.4 3.3 %collective-permute-done.4.refs_0_ = bf16[4,592,128]{2,1,0:T(8,128)(2,1)} collective-permute-done((bf16[4,592,128]{2,1,0:T(8,128)(2,1)}, bf16[4,592,128]{2,1,0:T(8,128)(2,1)}, u32[]{:S(2)}, u32[]{:S(2)}) %collective-permute-start.4) | collective-permute-done | bytes 606240 | tf_op jit(solution)/shard_map/ppermute | solution.py:277
  39.7 1.5 %collective-permute-start.5 = (bf16[4,592,128]{2,1,0:T(8,128)(2,1)}, bf16[4,592,128]{2,1,0:T(8,128)(2,1)}, u32[]{:S(2)}, u32[]{:S(2)}) collective-permute-start(bf16[4,592,128]{2,1,0:T(8,128)(2,1)} %collective-permute-done.4.refs_0_), channel_id=1, source_target_pairs={{0,16},{4,20},{8,24},{12,28},{16,0},{20,4},{24,8},{28,12},{1,17},{... | collective-permute-start | bytes 1818632 | tf_op jit(solution)/shard_map/ppermute | solution.py:277
  41.2 7.1 %collective-permute-done.13.refs_9_ = bf16[576,512]{1,0:T(8,128)(2,1)} collective-permute-done((bf16[576,512]{1,0:T(8,128)(2,1)}, bf16[576,512]{1,0:T(8,128)(2,1)}, u32[]{:S(2)}, u32[]{:S(2)}) %collective-permute-start.13) | collective-permute-done | bytes 589856 | tf_op jit(solution)/shard_map/ppermute | solution.py:277
  48.3 0.0 collective-permute-done.11.refs_7_
  48.3 0.7 collective-permute-start.15
  49.0 0.0 copy-start.5
  49.0 0.5 collective-permute-start.10
  49.5 0.2 copy-done.5
  49.8 0.5 collective-permute-start.8
  50.3 1.5 %maximum_select_fusion.meta_ref = bf16[32,80,128]{2,1,0:T(8,128)(2,1)S(1)} fusion(bf16[16,80,128]{2,1,0:T(8,128)(2,1)} %copy-done.5, bf16[16,80,128]{2,1,0:T(8,128)(2,1)} %copy-done.4, pred[]{:T(512)S(6)} %eq.22), kind=kLoop, calls=%fused_computation | loop fusion | flops 983040 | bytes 1310721 | tf_op jit(solution)/shard_map/jit(_where)/select_n | solution.py:301
  51.7 0.2 copy-done.1
  51.9 6.8 %index.1 = f32[32,4096]{1,0:T(8,128)} custom-call(bf16[32,80,128]{2,1,0:T(8,128)(2,1)S(1)} %maximum_select_fusion.meta_ref, bf16[4096,128]{1,0:T(8,128)(2,1)S(1)} %copy-done.1), custom_call_target="tpu_custom_call" | custom-call | flops 1000 | bytes 1000 | tf_op jit(solution)/shard_map/index/pallas_call | solution.py:252
  58.7 0.0 collective-permute-done.5.refs_0_
  58.7 0.0 collective-permute-start.14
  58.7 2.9 %collective-permute-done.15.refs_11_ = bf16[576,512]{1,0:T(8,128)(2,1)} collective-permute-done((bf16[576,512]{1,0:T(8,128)(2,1)}, bf16[576,512]{1,0:T(8,128)(2,1)}, u32[]{:S(2)}, u32[]{:S(2)}) %collective-permute-start.15) | collective-permute-done | bytes 589856 | tf_op jit(solution)/shard_map/ppermute | solution.py:277
  61.6 0.5 collective-permute-start.16
  62.5 0.1 stack.99.where_ref
  62.6 0.0 collective-permute-done.6.refs_2_
  62.6 1.3 %collective-permute-done.12.refs_8_ = bf16[576,512]{1,0:T(8,128)(2,1)} collective-permute-done((bf16[576,512]{1,0:T(8,128)(2,1)}, bf16[576,512]{1,0:T(8,128)(2,1)}, u32[]{:S(2)}, u32[]{:S(2)}) %collective-permute-start.12) | collective-permute-done | bytes 589856 | tf_op jit(solution)/shard_map/ppermute | solution.py:277
  64.0 0.8 collective-permute-done.16.refs_12_
  64.8 6.9 %attend.4 = bf16[528,512]{1,0:T(8,128)(2,1)S(1)} custom-call(s32[24]{0:T(128)S(1)} %stack.99.where_ref, bf16[4,592,128]{2,1,0:T(8,128)(2,1)} %collective-permute-done.5.refs_0_, bf16[576,1024]{1,0:T(8,128)(2,1)S(1)} %bitcast.30, bf16[576,1024]{1,0:T(8,128)(2,1)S(1)} %collective-permute-done.6.refs_2_, bf16[576,1024]{1,0:T(8,128)(2,1)S(1)} %collective-permute-done.7.refs_3_, ...), custom_call_target="tpu_custom_call" | custom-call | flops 1000 | bytes 1000 | tf_op jit(solution)/shard_map/attend/pallas_call | solution.py:162
  71.7 1.6 %collective-permute-start.17 = (bf16[528,512]{1,0:T(8,128)(2,1)S(1)}, bf16[528,512]{1,0:T(8,128)(2,1)S(1)}, u32[]{:S(2)}, u32[]{:S(2)}) collective-permute-start(bf16[528,512]{1,0:T(8,128)(2,1)S(1)} %attend.4), channel_id=1, source_target_pairs={{0,16},{4,20},{8,24},{12,28},{16,0},{20,4},{24,8},{28,12},{1,17},{... | collective-permute-start | bytes 1622024 | tf_op jit(solution)/shard_map/ppermute | solution.py:277
  73.3 6.9 %attend.5.refs_1_ = bf16[528,512]{1,0:T(8,128)(2,1)S(1)} custom-call(s32[24]{0:T(128)S(1)} %stack.99.where_ref, bf16[4,592,128]{2,1,0:T(8,128)(2,1)} %collective-permute-done.4.refs_0_, bf16[576,1024]{1,0:T(8,128)(2,1)S(1)} %bitcast.31, bf16[576,1024]{1,0:T(8,128)(2,1)S(1)} %collective-permute-done.6.refs_2_, ...), custom_call_target="tpu_custom_call" | custom-call | flops 1000 | bytes 1000 | tf_op jit(solution)/shard_map/attend/pallas_call | solution.py:162
  80.3 6.9 %attend.6 = bf16[528,512]{1,0:T(8,128)(2,1)S(1)} custom-call(s32[24]{0:T(128)S(1)} %stack.99.where_ref, bf16[4,592,128]{2,1,0:T(8,128)(2,1)} %collective-permute-done.3.refs_0_, bf16[576,1024]{1,0:T(8,128)(2,1)S(1)} %bitcast.32, bf16[576,1024]{1,0:T(8,128)(2,1)S(1)} %collective-permute-done.6.refs_2_, bf16[576,1024]{1,0:T(8,128)(2,1)S(1)} %collective-permute-done.7.refs_3_, ...), custom_call_target="tpu_custom_call" | custom-call | flops 1000 | bytes 1000 | tf_op jit(solution)/shard_map/attend/pallas_call | solution.py:162
  87.2 0.6 collective-permute-start.19
  87.8 0.0 collective-permute-done.17.refs_0_
  87.8 0.5 combine.2
  88.2 2.2 %collective-permute-start.18 = (bf16[528,512]{1,0:T(8,128)(2,1)S(1)}, bf16[528,512]{1,0:T(8,128)(2,1)S(1)}, u32[]{:S(2)}, u32[]{:S(2)}) collective-permute-start(bf16[528,512]{1,0:T(8,128)(2,1)S(1)} %combine.2), channel_id=1, source_target_pairs={{0,2},{1,3},{2,0},{3,1},{4,6},{5,7},{6,4},{7,5},{8,10},{9,11},{10,... | collective-permute-start | bytes 1622024 | tf_op jit(solution)/shard_map/ppermute | solution.py:277
  90.5 7.1 %attend.7.refs_2_ = bf16[528,512]{1,0:T(8,128)(2,1)S(1)} custom-call(s32[24]{0:T(128)S(1)} %stack.99.where_ref, bf16[4,592,128]{2,1,0:T(8,128)(2,1)} %table.1.refs_0_, bf16[576,1024]{1,0:T(8,128)(2,1)S(1)} %bitcast.33, bf16[576,1024]{1,0:T(8,128)(2,1)S(1)} %collective-permute-done.6.refs_2_, bf16[576,1024]{1,0:T(8,128)(2,1)S(1)} %collective-permute-done.7.refs_3_, ...), custom_call_target="tpu_custom_call" | custom-call | flops 1000 | bytes 1000 | tf_op jit(solution)/shard_map/attend/pallas_call | solution.py:162
  97.6 3.7 %collective-permute-done.19.refs_1_ = bf16[528,512]{1,0:T(8,128)(2,1)S(1)} collective-permute-done((bf16[528,512]{1,0:T(8,128)(2,1)S(1)}, bf16[528,512]{1,0:T(8,128)(2,1)S(1)}, u32[]{:S(2)}, u32[]{:S(2)}) %collective-permute-start.19) | collective-permute-done | bytes 540704 | tf_op jit(solution)/shard_map/ppermute | solution.py:277
  101.3 13.3 %collective-permute-done.18.refs_0_ = bf16[528,512]{1,0:T(8,128)(2,1)S(1)} collective-permute-done((bf16[528,512]{1,0:T(8,128)(2,1)S(1)}, bf16[528,512]{1,0:T(8,128)(2,1)S(1)}, u32[]{:S(2)}, u32[]{:S(2)}) %collective-permute-start.18) | collective-permute-done | bytes 540704 | tf_op jit(solution)/shard_map/ppermute | solution.py:277
  114.5 1.4 %combine.3 = bf16[4,128,512]{2,1,0:T(8,128)(2,1)} custom-call(bf16[528,512]{1,0:T(8,128)(2,1)S(1)} %collective-permute-done.18.refs_0_, bf16[528,512]{1,0:T(8,128)(2,1)S(1)} %collective-permute-done.19.refs_1_, bf16[528,512]{1,0:T(8,128)(2,1)S(1)} %attend.7.refs_2_), custom_call_target="tpu_custom_call" | custom-call | flops 1000 | bytes 1000 | tf_op jit(solution)/shard_map/combine/pallas_call | solution.py:209
  (24 shorter events, 0.1 us)
Async XLA Ops:
  0.6 7.0 %copy-start.7 = (bf16[4,64]{1,0:T(4,128)(2,1)S(1)}, bf16[4,64]{1,0:T(4,128)(2,1)}, u32[]{:S(2)}) copy-start(bf16[4,64]{1,0:T(4,128)(2,1)} %param.10) | copy-start | bytes 1540
  0.6 7.0 %copy-start.6 = (bf16[4,64,128]{2,1,0:T(8,128)(2,1)S(1)}, bf16[4,64,128]{2,1,0:T(8,128)(2,1)}, u32[]{:S(2)}) copy-start(bf16[4,64,128]{2,1,0:T(8,128)(2,1)} %param.9) | copy-start | bytes 196612
  0.7 7.1 %copy-start.2 = (bf16[4,128,576]{1,2,0:T(8,128)(2,1)S(1)}, bf16[4,128,576]{1,2,0:T(8,128)(2,1)}, u32[]{:S(2)}) copy-start(bf16[4,128,576]{1,2,0:T(8,128)(2,1)} %param.8) | copy-start | bytes 1769476
  0.7 7.1 %copy-start.3 = (s32[4,2048]{1,0:T(4,128)S(1)}, s32[4,2048]{1,0:T(4,128)}, u32[]{:S(2)}) copy-start(s32[4,2048]{1,0:T(4,128)} %selected_ref.1) | copy-start | bytes 98308
  0.7 30.2 %collective-permute-start.7 = (bf16[576,1024]{1,0:T(8,128)(2,1)}, bf16[576,1024]{1,0:T(8,128)(2,1)S(1)}, u32[]{:S(2)}, u32[]{:S(2)}) collective-permute-start(bf16[576,1024]{1,0:T(8,128)(2,1)} %bitcast.27), channel_id=1, source_target_pairs={{0,8},{4,12},{8,0},{12,4},{16,24},{20,28},{24,16},{28,20},{1,9},{5... | collective-permute-start | bytes 3538952 | tf_op jit(solution)/shard_map/ppermute | solution.py:277
  6.0 24.8 %collective-permute-start.9 = (bf16[576,512]{1,0:T(8,128)(2,1)}, bf16[576,512]{1,0:T(8,128)(2,1)}, u32[]{:S(2)}, u32[]{:S(2)}) collective-permute-start(bf16[576,512]{1,0:T(8,128)(2,1)} %get-tuple-element.21), channel_id=1, source_target_pairs={{0,1},{1,0},{2,3},{3,2},{4,5},{5,4},{6,7},{7,6},{8,9},{9,8},{10,11... | collective-permute-start | bytes 1769480 | tf_op jit(solution)/shard_map/ppermute | solution.py:277
  7.6 41.4 %copy-start = (bf16[1024,576]{0,1:T(8,128)(2,1)S(1)}, bf16[1024,576]{0,1:T(8,128)(2,1)}, u32[]{:S(2)}) copy-start(bf16[1024,576]{0,1:T(8,128)(2,1)} %param.6) | copy-start | bytes 3538948
  7.7 4.2 %collective-permute-start = (bf16[4,80,128]{2,1,0:T(8,128)(2,1)S(1)}, bf16[4,80,128]{2,1,0:T(8,128)(2,1)S(1)}, u32[]{:S(2)}, u32[]{:S(2)}) collective-permute-start(bf16[4,80,128]{2,1,0:T(8,128)(2,1)S(1)} %pad_maximum_fusion), channel_id=1, source_target_pairs={{0,4},{4,0},{8,12},{12,8},{16,20},{20,16},{24,28},{28,24},{1,5},{5... | collective-permute-start | bytes 245768 | tf_op jit(solution)/shard_map/ppermute | solution.py:277
  9.3 30.4 %collective-permute-start.4 = (bf16[4,592,128]{2,1,0:T(8,128)(2,1)}, bf16[4,592,128]{2,1,0:T(8,128)(2,1)}, u32[]{:S(2)}, u32[]{:S(2)}) collective-permute-start(bf16[4,592,128]{2,1,0:T(8,128)(2,1)} %table.1.refs_0_), channel_id=1, source_target_pairs={{0,2},{1,3},{2,0},{3,1},{4,6},{5,7},{6,4},{7,5},{8,10},{9,11},{10,... | collective-permute-start | bytes 1818632 | tf_op jit(solution)/shard_map/ppermute | solution.py:277
  11.9 22.3 %collective-permute-start.1 = (bf16[8,80,128]{2,1,0:T(8,128)(2,1)S(1)}, bf16[8,80,128]{2,1,0:T(8,128)(2,1)S(1)}, u32[]{:S(2)}, u32[]{:S(2)}) collective-permute-start(bf16[8,80,128]{2,1,0:T(8,128)(2,1)S(1)} %maximum_select_fusion.2), channel_id=1, source_target_pairs={{0,8},{4,12},{8,0},{12,4},{16,24},{20,28},{24,16},{28,20},{1,9},{5... | collective-permute-start | bytes 491528 | tf_op jit(solution)/shard_map/ppermute | solution.py:277
  12.5 37.0 %collective-permute-start.3 = (bf16[4,592,128]{2,1,0:T(8,128)(2,1)}, bf16[4,592,128]{2,1,0:T(8,128)(2,1)}, u32[]{:S(2)}, u32[]{:S(2)}) collective-permute-start(bf16[4,592,128]{2,1,0:T(8,128)(2,1)} %table.1.refs_0_), channel_id=1, source_target_pairs={{0,16},{4,20},{8,24},{12,28},{16,0},{20,4},{24,8},{28,12},{1,17},{... | collective-permute-start | bytes 1818632 | tf_op jit(solution)/shard_map/ppermute | solution.py:277
  30.8 17.5 %collective-permute-start.13 = (bf16[576,512]{1,0:T(8,128)(2,1)}, bf16[576,512]{1,0:T(8,128)(2,1)}, u32[]{:S(2)}, u32[]{:S(2)}) collective-permute-start(bf16[576,512]{1,0:T(8,128)(2,1)} %get-tuple-element.14), channel_id=1, source_target_pairs={{0,1},{1,0},{2,3},{3,2},{4,5},{5,4},{6,7},{7,6},{8,9},{9,8},{10,11... | collective-permute-start | bytes 1769480 | tf_op jit(solution)/shard_map/ppermute | solution.py:277
  30.8 17.5 %collective-permute-start.11 = (bf16[576,512]{1,0:T(8,128)(2,1)}, bf16[576,512]{1,0:T(8,128)(2,1)}, u32[]{:S(2)}, u32[]{:S(2)}) collective-permute-start(bf16[576,512]{1,0:T(8,128)(2,1)} %collective-permute-done.9.refs_5_), channel_id=1, source_target_pairs={{0,8},{4,12},{8,0},{12,4},{16,24},{20,28},{24,16},{28,20},{1,9},{5... | collective-permute-start | bytes 1769480 | tf_op jit(solution)/shard_map/ppermute | solution.py:277
  34.2 15.3 %copy-start.4 = (bf16[16,80,128]{2,1,0:T(8,128)(2,1)}, bf16[16,80,128]{2,1,0:T(8,128)(2,1)S(1)}, u32[]{:S(2)}) copy-start(bf16[16,80,128]{2,1,0:T(8,128)(2,1)S(1)} %maximum_select_fusion.1) | copy-start | bytes 983044
  34.2 14.8 %collective-permute-start.2 = (bf16[16,80,128]{2,1,0:T(8,128)(2,1)S(1)}, bf16[16,80,128]{2,1,0:T(8,128)(2,1)S(1)}, u32[]{:S(2)}, u32[]{:S(2)}) collective-permute-start(bf16[16,80,128]{2,1,0:T(8,128)(2,1)S(1)} %maximum_select_fusion.1), channel_id=1, source_target_pairs={{0,16},{4,20},{8,24},{12,28},{16,0},{20,4},{24,8},{28,12},{1,17},{... | collective-permute-start | bytes 983048 | tf_op jit(solution)/shard_map/ppermute | solution.py:277
  39.7 19.0 %collective-permute-start.5 = (bf16[4,592,128]{2,1,0:T(8,128)(2,1)}, bf16[4,592,128]{2,1,0:T(8,128)(2,1)}, u32[]{:S(2)}, u32[]{:S(2)}) collective-permute-start(bf16[4,592,128]{2,1,0:T(8,128)(2,1)} %collective-permute-done.4.refs_0_), channel_id=1, source_target_pairs={{0,16},{4,20},{8,24},{12,28},{16,0},{20,4},{24,8},{28,12},{1,17},{... | collective-permute-start | bytes 1818632 | tf_op jit(solution)/shard_map/ppermute | solution.py:277
  48.3 13.3 %collective-permute-start.15 = (bf16[576,512]{1,0:T(8,128)(2,1)}, bf16[576,512]{1,0:T(8,128)(2,1)}, u32[]{:S(2)}, u32[]{:S(2)}) collective-permute-start(bf16[576,512]{1,0:T(8,128)(2,1)} %collective-permute-done.13.refs_9_), channel_id=1, source_target_pairs={{0,8},{4,12},{8,0},{12,4},{16,24},{20,28},{24,16},{28,20},{1,9},{5... | collective-permute-start | bytes 1769480 | tf_op jit(solution)/shard_map/ppermute | solution.py:277
  49.0 13.6 %collective-permute-start.6 = (bf16[576,1024]{1,0:T(8,128)(2,1)S(1)}, bf16[576,1024]{1,0:T(8,128)(2,1)S(1)}, u32[]{:S(2)}, u32[]{:S(2)}) collective-permute-start(bf16[576,1024]{1,0:T(8,128)(2,1)S(1)} %bitcast.29), channel_id=1, source_target_pairs={{0,4},{4,0},{8,12},{12,8},{16,20},{20,16},{24,28},{28,24},{1,5},{5... | collective-permute-start | bytes 3538952 | tf_op jit(solution)/shard_map/ppermute | solution.py:277
  49.0 0.7 copy-start.5
  49.0 12.6 %collective-permute-start.10 = (bf16[576,512]{1,0:T(8,128)(2,1)}, bf16[576,512]{1,0:T(8,128)(2,1)}, u32[]{:S(2)}, u32[]{:S(2)}) collective-permute-start(bf16[576,512]{1,0:T(8,128)(2,1)} %collective-permute-done.9.refs_5_), channel_id=1, source_target_pairs={{0,4},{4,0},{8,12},{12,8},{16,20},{20,16},{24,28},{28,24},{1,5},{5... | collective-permute-start | bytes 1769480 | tf_op jit(solution)/shard_map/ppermute | solution.py:277
  49.8 14.2 %collective-permute-start.8 = (bf16[576,1024]{1,0:T(8,128)(2,1)S(1)}, bf16[576,1024]{1,0:T(8,128)(2,1)}, u32[]{:S(2)}, u32[]{:S(2)}) collective-permute-start(bf16[576,1024]{1,0:T(8,128)(2,1)S(1)} %collective-permute-done.7.refs_3_), channel_id=1, source_target_pairs={{0,4},{4,0},{8,12},{12,8},{16,20},{20,16},{24,28},{28,24},{1,5},{5... | collective-permute-start | bytes 3538952 | tf_op jit(solution)/shard_map/ppermute | solution.py:277
  50.3 1.6 %copy-start.1 = (bf16[4096,128]{1,0:T(8,128)(2,1)S(1)}, bf16[4096,128]{1,0:T(8,128)(2,1)}, u32[]{:S(2)}) copy-start(bf16[4096,128]{1,0:T(8,128)(2,1)} %keys_ref.1) | copy-start | bytes 3145732
  58.7 3.9 %collective-permute-start.14 = (bf16[576,512]{1,0:T(8,128)(2,1)}, bf16[576,512]{1,0:T(8,128)(2,1)}, u32[]{:S(2)}, u32[]{:S(2)}) collective-permute-start(bf16[576,512]{1,0:T(8,128)(2,1)} %collective-permute-done.13.refs_9_), channel_id=1, source_target_pairs={{0,4},{4,0},{8,12},{12,8},{16,20},{20,16},{24,28},{28,24},{1,5},{5... | collective-permute-start | bytes 1769480 | tf_op jit(solution)/shard_map/ppermute | solution.py:277
  61.6 2.3 %collective-permute-start.12 = (bf16[576,512]{1,0:T(8,128)(2,1)}, bf16[576,512]{1,0:T(8,128)(2,1)}, u32[]{:S(2)}, u32[]{:S(2)}) collective-permute-start(bf16[576,512]{1,0:T(8,128)(2,1)} %collective-permute-done.11.refs_7_), channel_id=1, source_target_pairs={{0,4},{4,0},{8,12},{12,8},{16,20},{20,16},{24,28},{28,24},{1,5},{5... | collective-permute-start | bytes 1769480 | tf_op jit(solution)/shard_map/ppermute | solution.py:277
  61.6 3.2 %collective-permute-start.16 = (bf16[576,512]{1,0:T(8,128)(2,1)}, bf16[576,512]{1,0:T(8,128)(2,1)}, u32[]{:S(2)}, u32[]{:S(2)}) collective-permute-start(bf16[576,512]{1,0:T(8,128)(2,1)} %collective-permute-done.15.refs_11_), channel_id=1, source_target_pairs={{0,4},{4,0},{8,12},{12,8},{16,20},{20,16},{24,28},{28,24},{1,5},{5... | collective-permute-start | bytes 1769480 | tf_op jit(solution)/shard_map/ppermute | solution.py:277
  71.7 16.0 %collective-permute-start.17 = (bf16[528,512]{1,0:T(8,128)(2,1)S(1)}, bf16[528,512]{1,0:T(8,128)(2,1)S(1)}, u32[]{:S(2)}, u32[]{:S(2)}) collective-permute-start(bf16[528,512]{1,0:T(8,128)(2,1)S(1)} %attend.4), channel_id=1, source_target_pairs={{0,16},{4,20},{8,24},{12,28},{16,0},{20,4},{24,8},{28,12},{1,17},{... | collective-permute-start | bytes 1622024 | tf_op jit(solution)/shard_map/ppermute | solution.py:277
  87.2 14.1 %collective-permute-start.19 = (bf16[528,512]{1,0:T(8,128)(2,1)S(1)}, bf16[528,512]{1,0:T(8,128)(2,1)S(1)}, u32[]{:S(2)}, u32[]{:S(2)}) collective-permute-start(bf16[528,512]{1,0:T(8,128)(2,1)S(1)} %attend.6), channel_id=1, source_target_pairs={{0,16},{4,20},{8,24},{12,28},{16,0},{20,4},{24,8},{28,12},{1,17},{... | collective-permute-start | bytes 1622024 | tf_op jit(solution)/shard_map/ppermute | solution.py:277
  88.2 26.3 %collective-permute-start.18 = (bf16[528,512]{1,0:T(8,128)(2,1)S(1)}, bf16[528,512]{1,0:T(8,128)(2,1)S(1)}, u32[]{:S(2)}, u32[]{:S(2)}) collective-permute-start(bf16[528,512]{1,0:T(8,128)(2,1)S(1)} %combine.2), channel_id=1, source_target_pairs={{0,2},{1,3},{2,0},{3,1},{4,6},{5,7},{6,4},{7,5},{8,10},{9,11},{10,... | collective-permute-start | bytes 1622024 | tf_op jit(solution)/shard_map/ppermute | solution.py:277

commit v3 on v2

--- a/solution.py
+++ b/solution.py
@@ -17,6 +17,7 @@
 BATCH = 4
 SCALE = SCORE_DIM ** (-0.5) * 1.4426950408889634
 VMEM = pltpu.VMEM
+LONG = pl.CostEstimate(flops=1000, bytes_accessed=60000000, transcendentals=0)
 TINY = pl.CostEstimate(flops=1000, bytes_accessed=1000, transcendentals=0)
 
 
@@ -76,10 +77,10 @@
     return jnp.concatenate(three(total) + three(peak) + [pad], axis=0).astype(jnp.bfloat16)
 
 
-def attend_kernel(blocks, shards, per, width, masked, where_ref, *refs):
+def attend_kernel(blocks, shards, per, width, masked, parts, where_ref, *refs):
     packs, slabs = refs[:blocks], refs[blocks : blocks + shards]
-    outs = refs[blocks + shards : 2 * blocks + shards]
-    keys = refs[2 * blocks + shards]
+    outs, keys = refs[blocks + shards : -1], refs[-1]
+    some = per // parts
     rows = blocks * per
     span = RUN * RUN
     his = packs[0].shape[1] - width
@@ -149,21 +150,22 @@
                 preferred_element_type=jnp.float32,
             )
             heads = sums.shape[0]
-            outs[block][at * heads : (at + 1) * heads, :] = sums.astype(jnp.bfloat16)
-            outs[block][per * heads :, at * LANES : (at + 1) * LANES] = aux_tile(total, peak)
-
-
-def attend(packs, slabs, where, width, masked):
+            out, at = outs[block * parts + at // some], at % some
+            out[at * heads : (at + 1) * heads, :] = sums.astype(jnp.bfloat16)
+            out[some * heads :, at * LANES : (at + 1) * LANES] = aux_tile(total, peak)
+
+
+def attend(packs, slabs, where, width, masked, parts):
     blocks, shards = len(packs), len(slabs)
     per, _, heads = packs[0].shape
     slots = sum(slab.shape[1] for slab in slabs) // RUN
     rows = blocks * per
-    out = VMEM((per * heads + AUX, LATENT), jnp.bfloat16)
-    return pl.pallas_call(
-        functools.partial(attend_kernel, blocks, shards, per, width, masked),
-        out_shape=[out] * blocks,
+    out = VMEM((per // parts * heads + AUX, LATENT), jnp.bfloat16)
+    return pl.pallas_call(
+        functools.partial(attend_kernel, blocks, shards, per, width, masked, parts),
+        out_shape=[out] * (blocks * parts),
         in_specs=[pl.BlockSpec(memory_space=pltpu.SMEM)] + whole_vmem(blocks + shards),
-        out_specs=whole_vmem(blocks),
+        out_specs=whole_vmem(blocks * parts),
         scratch_shapes=[pltpu.VMEM((rows, slots, width), jnp.bfloat16)],
         compiler_params=params(14),
         cost_estimate=TINY,
@@ -171,15 +173,16 @@
     )(where, *near(packs), *near(slabs))
 
 
-def combine_kernel(per, heads, last, *refs):
-    parts, out = refs[:-1], refs[-1]
-    for at in range(per):
-        lanes = pl.ds(at * LANES, LANES)
-        totals, peaks = [], []
-        for part in parts:
-            aux = part[per * heads :, lanes].astype(jnp.float32)
+def combine_kernel(begins, rows, heads, last, *refs):
+    parts, out = refs[: len(begins)], refs[-1]
+    for row in rows:
+        blocks, totals, peaks = [], [], []
+        for ref, begin in zip(parts, begins):
+            some, at = (ref.shape[0] - AUX) // heads, row - begin
+            aux = ref[some * heads :, at * LANES : (at + 1) * LANES].astype(jnp.float32)
             totals.append(aux[0:1] + aux[1:2] + aux[2:3])
             peaks.append(aux[3:4] + aux[4:5] + aux[5:6])
+            blocks.append(ref[at * heads : (at + 1) * heads, :].astype(jnp.float32))
         peak = functools.reduce(jnp.maximum, peaks)
         shares = [jnp.exp2(p - peak) for p in peaks]
         total = functools.reduce(jnp.add, [s * t for s, t in zip(shares, totals)])
@@ -189,32 +192,42 @@
         columns = jnp.transpose(
             jnp.concatenate(shares + [jnp.zeros((pad, LANES), jnp.float32)] * (pad > 0), axis=0)
         )
-        mixed = None
-        for i, part in enumerate(parts):
-            term = part[at * heads : (at + 1) * heads, :].astype(jnp.float32) * columns[:, i : i + 1]
-            mixed = term if mixed is None else mixed + term
+        terms = [block * columns[:, i : i + 1] for i, block in enumerate(blocks)]
+        mixed = functools.reduce(jnp.add, terms).astype(jnp.bfloat16)
+        at = row - rows[0]
         if last:
-            out[at] = mixed.astype(jnp.bfloat16)
+            out[at] = mixed
         else:
-            out[at * heads : (at + 1) * heads, :] = mixed.astype(jnp.bfloat16)
-            out[per * heads :, lanes] = aux_tile(total, peak)
-
-
-def combine(parts, per, last):
-    heads = (parts[0].shape[0] - AUX) // per
-    if last:
-        out = jax.ShapeDtypeStruct((per, heads, LATENT), jnp.bfloat16)
-    else:
-        out = VMEM(parts[0].shape, jnp.bfloat16)
-    return pl.pallas_call(
-        functools.partial(combine_kernel, per, heads, last),
-        out_shape=out,
+            out[at * heads : (at + 1) * heads, :] = mixed
+            out[len(rows) * heads :, at * LANES : (at + 1) * LANES] = aux_tile(total, peak)
+
+
+def combine(parts, begins, rows, heads):
+    return pl.pallas_call(
+        functools.partial(combine_kernel, begins, rows, heads, False),
+        out_shape=VMEM((len(rows) * heads + AUX, LATENT), jnp.bfloat16),
         in_specs=whole_vmem(len(parts)),
         out_specs=pl.BlockSpec(memory_space=VMEM),
         compiler_params=params(8),
         cost_estimate=TINY,
         name="combine",
     )(*near(parts))
+
+
+def finish(parts, begins, rows, per, heads, done, cost):
+    count, at = len(rows), rows[0] // len(rows)
+    more = [] if done is None else [done]
+    return pl.pallas_call(
+        functools.partial(combine_kernel, begins, rows, heads, True),
+        grid=(1,),
+        out_shape=jax.ShapeDtypeStruct((per, heads, LATENT), jnp.bfloat16),
+        in_specs=whole_vmem(len(parts)) + [pl.BlockSpec(memory_space=pl.ANY)] * len(more),
+        out_specs=pl.BlockSpec((count, heads, LATENT), lambda i: (at, 0, 0)),
+        input_output_aliases={len(parts): 0} if more else {},
+        compiler_params=params(8),
+        cost_estimate=cost,
+        name="finish",
+    )(*near(parts), *more)
 
 
 def index_kernel(heads, meta_ref, keys_ref, out_ref, gate_scr):
@@ -279,7 +292,7 @@
     def body(latent_cache, index_keys, query_latent, index_query, index_gates, selected):
         here, plane = lax.axis_index("ctx"), lax.axis_index("row")
         per, _, width = query_latent.shape
-        heads = index_query.shape[1]
+        heads = query_latent.shape[1]
         tokens = latent_cache.shape[0]
         runs = tokens // RUN
         all_runs = runs * columns * planes
@@ -309,7 +322,7 @@
         }
         near_queries = list(groups[0].values()) + list(starts.values())
         far_queries = [pack for group in groups.values() for pack in group.values()]
-        index_scores = index_block(after(meta, *near_queries), index_keys, heads)
+        index_scores = index_block(after(meta, *near_queries), index_keys, index_query.shape[1])
 
         half = tokens // 2
         pieces, sent, shown = [(0, 0, slab)], [], []
@@ -336,17 +349,34 @@
         where = jnp.stack(where).astype(jnp.int32)
 
         parts, last = [], after(where, index_scores)
+        split = 2
+        some = per // split
         for across in row_planes[1:] + row_planes[:1]:
             mine = []
             for mask in reversed(row_columns):
-                (done,) = attend([groups[across][mask]], slabs, last, width, masked)
-                last = after(where, done)
-                mine.append(swap(done, "ctx", mask) if mask else done)
+                done = attend(
+                    [groups[across][mask]], slabs, last, width, masked, split if across else 1
+                )
+                last = after(where, *done)
+                first = [] if across else [back[0] for back in parts]
+                mine.append([swap(after(a, *first), "ctx", mask) if mask else a for a in done])
             if across:
-                parts.append(swap(combine(mine, per, False), "row", across))
+                back = []
+                for i in range(split):
+                    rows = range(i * some, (i + 1) * some)
+                    mixed = combine([part[i] for part in mine], [rows[0]] * len(mine), rows, heads)
+                    back.append(swap(after(mixed, *back), "row", across))
+                    last = after(where, *done, mixed) if i == 0 else last
+                parts.append(back)
             else:
-                parts += mine
-        attended = combine(parts, per, True)
+                own = [part[0] for part in mine]
+        attended = None
+        for i in range(split):
+            rows = range(i * some, (i + 1) * some)
+            far = [back[i] for back in parts]
+            begins = [rows[0]] * len(far) + [0] * len(own)
+            cost = TINY if i == split - 1 else LONG
+            attended = finish(far + own, begins, rows, per, heads, attended, cost)
         return attended, index_scores
 
     return jax.shard_map(

time: 116 us -> 112 us (0.966)
  waiting for transfers between devices: 50.7 us -> 43.8 us
  starting transfers between devices: 21.5 us -> 23.8 us
    ppermute x20 -> x22, waiting for transfers between devices: 50.7 us -> 43.8 us  [swap(): return lax.ppermute(array, axis, [(i, i ^ mask) for i in range(size)])]
    ppermute x20 -> x22, starting transfers between devices: 21.5 us -> 23.8 us  [swap(): return lax.ppermute(array, axis, [(i, i ^ mask) for i in range(size)])]
    pallas_call x2 -> x4, Pallas kernels: 1.82 us -> 2.74 us  [the longest x2 2.23 us: finish(): pl.pallas_call(functools.partial(combine_kernel, begins, rows, heads, Tru...]
  transfers between devices with their start and end apart: 20 -> 22, of which waited for: 9 -> 11; matrix products, arithmetic and copies ran while one was open for 3% -> 4% of each run, Pallas kernels for 26% -> 27%
where the time goes in v3:
time: 112 us
  waiting for transfers between devices  43.8 us (39%)
  Pallas kernels  39 us (35%)
  starting transfers between devices  23.8 us (21%)
  local copies, waits for them, and re-layouts  2.85 us (3%)
  other arithmetic  1.54 us (1%)
  between operations  1.19 us (1%)
    ppermute x22, waiting for transfers between devices, swap(): return lax.ppermute(array, axis, [(i, i ^ mask) for i in range(size)])  43.8 us
    pallas_call x4, Pallas kernels, attend(): pl.pallas_call(functools.partial(attend_kernel, blocks, shards, per, widt...  27.9 us
    ppermute x22, starting transfers between devices, swap(): return lax.ppermute(array, axis, [(i, i ^ mask) for i in range(size)])  23.8 us
    pallas_call x1, Pallas kernels, index_block(): pl.pallas_call(functools.partial(index_kernel, heads), grid=(tokens // bl...  6.82 us
    slice x1, local copies, waits for them, and re-layouts, body(): piece = slab[:, offset:offset + half]  2.33 us
  transfers between devices with their start and end apart: 22, of which 11 were waited for; matrix products, arithmetic and copies ran while one was open for 4% of the time, Pallas kernels for 27%

profile of v3, /device:TPU:0, one launch (start us, length us, event | category | flops | bytes accessed | tf_op | source)
XLA Modules:
  0.0 112.2 jit_solution(10952872615395249801)
XLA Ops:
  0.7 3.0 %collective-permute-start.7 = (bf16[576,1024]{1,0:T(8,128)(2,1)}, bf16[576,1024]{1,0:T(8,128)(2,1)S(1)}, u32[]{:S(2)}, u32[]{:S(2)}) collective-permute-start(bf16[576,1024]{1,0:T(8,128)(2,1)} %bitcast.27), channel_id=1, source_target_pairs={{0,8},{4,12},{8,0},{12,4},{16,24},{20,28},{24,16},{28,20},{1,9},{5... | collective-permute-start | bytes 3538952 | tf_op jit(solution)/shard_map/ppermute | solution.py:290
  3.7 2.3 %fusion = (bf16[576,512]{1,0:T(8,128)(2,1)}, bf16[576,512]{1,0:T(8,128)(2,1)}) fusion(bf16[576,1024]{1,0:T(8,128)(2,1)} %bitcast.28), kind=kLoop, calls=%fused_computation.4 | loop fusion | bytes 2359296 | tf_op jit(solution)/shard_map/slice | solution.py:331
  6.0 1.6 %collective-permute-start.9 = (bf16[576,512]{1,0:T(8,128)(2,1)}, bf16[576,512]{1,0:T(8,128)(2,1)}, u32[]{:S(2)}, u32[]{:S(2)}) collective-permute-start(bf16[576,512]{1,0:T(8,128)(2,1)} %get-tuple-element.33), channel_id=1, source_target_pairs={{0,1},{1,0},{2,3},{3,2},{4,5},{5,4},{6,7},{7,6},{8,9},{9,8},{10,11... | collective-permute-start | bytes 1769480 | tf_op jit(solution)/shard_map/ppermute | solution.py:290
  7.6 0.0 copy-start
  7.6 0.1 collective-permute-start
  7.7 1.5 %table.1.refs_0_ = bf16[4,592,128]{2,1,0:T(8,128)(2,1)} custom-call(bf16[4,576,128]{2,1,0:T(8,128)(2,1)S(1)} %bitcast.34, s32[4,2048]{1,0:T(4,128)S(1)} %copy-done.3), custom_call_target="tpu_custom_call" | custom-call | flops 1000 | bytes 1000 | tf_op jit(solution)/shard_map/table/pallas_call | solution.py:57
  9.2 2.6 %collective-permute-start.4 = (bf16[4,592,128]{2,1,0:T(8,128)(2,1)}, bf16[4,592,128]{2,1,0:T(8,128)(2,1)}, u32[]{:S(2)}, u32[]{:S(2)}) collective-permute-start(bf16[4,592,128]{2,1,0:T(8,128)(2,1)} %table.1.refs_0_), channel_id=1, source_target_pairs={{0,2},{1,3},{2,0},{3,1},{4,6},{5,7},{6,4},{7,5},{8,10},{9,11},{10,... | collective-permute-start | bytes 1818632 | tf_op jit(solution)/shard_map/ppermute | solution.py:290
  11.9 0.6 collective-permute-start.1
  12.5 1.5 %collective-permute-start.3 = (bf16[4,592,128]{2,1,0:T(8,128)(2,1)}, bf16[4,592,128]{2,1,0:T(8,128)(2,1)}, u32[]{:S(2)}, u32[]{:S(2)}) collective-permute-start(bf16[4,592,128]{2,1,0:T(8,128)(2,1)} %table.1.refs_0_), channel_id=1, source_target_pairs={{0,16},{4,20},{8,24},{12,28},{16,0},{20,4},{24,8},{28,12},{1,17},{... | collective-permute-start | bytes 1818632 | tf_op jit(solution)/shard_map/ppermute | solution.py:290
  14.0 16.8 %collective-permute-done.9.refs_5_ = bf16[576,512]{1,0:T(8,128)(2,1)} collective-permute-done((bf16[576,512]{1,0:T(8,128)(2,1)}, bf16[576,512]{1,0:T(8,128)(2,1)}, u32[]{:S(2)}, u32[]{:S(2)}) %collective-permute-start.9) | collective-permute-done | bytes 589856 | tf_op jit(solution)/shard_map/ppermute | solution.py:290
  30.8 2.0 %collective-permute-start.11 = (bf16[576,512]{1,0:T(8,128)(2,1)}, bf16[576,512]{1,0:T(8,128)(2,1)}, u32[]{:S(2)}, u32[]{:S(2)}) collective-permute-start(bf16[576,512]{1,0:T(8,128)(2,1)} %collective-permute-done.9.refs_5_), channel_id=1, source_target_pairs={{0,8},{4,12},{8,0},{12,4},{16,24},{20,28},{24,16},{28,20},{1,9},{5... | collective-permute-start | bytes 1769480 | tf_op jit(solution)/shard_map/ppermute | solution.py:290
  32.7 1.5 %collective-permute-done.1 = bf16[8,80,128]{2,1,0:T(8,128)(2,1)S(1)} collective-permute-done((bf16[8,80,128]{2,1,0:T(8,128)(2,1)S(1)}, bf16[8,80,128]{2,1,0:T(8,128)(2,1)S(1)}, u32[]{:S(2)}, u32[]{:S(2)}) %collective-permute-start.1) | collective-permute-done | bytes 163872 | tf_op jit(solution)/shard_map/ppermute | solution.py:290
  34.2 0.0 copy-start.4
  34.2 2.1 %collective-permute-start.2 = (bf16[16,80,128]{2,1,0:T(8,128)(2,1)S(1)}, bf16[16,80,128]{2,1,0:T(8,128)(2,1)S(1)}, u32[]{:S(2)}, u32[]{:S(2)}) collective-permute-start(bf16[16,80,128]{2,1,0:T(8,128)(2,1)S(1)} %maximum_select_fusion.1), channel_id=1, source_target_pairs={{0,16},{4,20},{8,24},{12,28},{16,0},{20,4},{24,8},{28,12},{1,17},{... | collective-permute-start | bytes 983048 | tf_op jit(solution)/shard_map/ppermute | solution.py:290
  36.4 3.3 %collective-permute-done.4.refs_0_ = bf16[4,592,128]{2,1,0:T(8,128)(2,1)} collective-permute-done((bf16[4,592,128]{2,1,0:T(8,128)(2,1)}, bf16[4,592,128]{2,1,0:T(8,128)(2,1)}, u32[]{:S(2)}, u32[]{:S(2)}) %collective-permute-start.4) | collective-permute-done | bytes 606240 | tf_op jit(solution)/shard_map/ppermute | solution.py:290
  39.7 1.5 %collective-permute-start.5 = (bf16[4,592,128]{2,1,0:T(8,128)(2,1)}, bf16[4,592,128]{2,1,0:T(8,128)(2,1)}, u32[]{:S(2)}, u32[]{:S(2)}) collective-permute-start(bf16[4,592,128]{2,1,0:T(8,128)(2,1)} %collective-permute-done.4.refs_0_), channel_id=1, source_target_pairs={{0,16},{4,20},{8,24},{12,28},{16,0},{20,4},{24,8},{28,12},{1,17},{... | collective-permute-start | bytes 1818632 | tf_op jit(solution)/shard_map/ppermute | solution.py:290
  41.2 7.1 %collective-permute-done.13.refs_9_ = bf16[576,512]{1,0:T(8,128)(2,1)} collective-permute-done((bf16[576,512]{1,0:T(8,128)(2,1)}, bf16[576,512]{1,0:T(8,128)(2,1)}, u32[]{:S(2)}, u32[]{:S(2)}) %collective-permute-start.13) | collective-permute-done | bytes 589856 | tf_op jit(solution)/shard_map/ppermute | solution.py:290
  48.3 0.7 collective-permute-start.15
  49.0 0.0 copy-start.5
  49.0 0.5 collective-permute-start.10
  49.5 0.2 copy-done.5
  49.7 0.5 collective-permute-start.8
  50.2 1.5 %maximum_select_fusion.meta_ref = bf16[32,80,128]{2,1,0:T(8,128)(2,1)S(1)} fusion(bf16[16,80,128]{2,1,0:T(8,128)(2,1)} %copy-done.5, bf16[16,80,128]{2,1,0:T(8,128)(2,1)} %copy-done.4, pred[]{:T(512)S(6)} %eq.22), kind=kLoop, calls=%fused_computation | loop fusion | flops 983040 | bytes 1310721 | tf_op jit(solution)/shard_map/jit(_where)/select_n | solution.py:314
  51.7 0.2 copy-done.1
  51.9 6.8 %index.1 = f32[32,4096]{1,0:T(8,128)} custom-call(bf16[32,80,128]{2,1,0:T(8,128)(2,1)S(1)} %maximum_select_fusion.meta_ref, bf16[4096,128]{1,0:T(8,128)(2,1)S(1)} %copy-done.1), custom_call_target="tpu_custom_call" | custom-call | flops 1000 | bytes 1000 | tf_op jit(solution)/shard_map/index/pallas_call | solution.py:265
  58.7 0.0 collective-permute-start.14
  58.7 2.9 %collective-permute-done.15.refs_11_ = bf16[576,512]{1,0:T(8,128)(2,1)} collective-permute-done((bf16[576,512]{1,0:T(8,128)(2,1)}, bf16[576,512]{1,0:T(8,128)(2,1)}, u32[]{:S(2)}, u32[]{:S(2)}) %collective-permute-start.15) | collective-permute-done | bytes 589856 | tf_op jit(solution)/shard_map/ppermute | solution.py:290
  61.6 0.5 collective-permute-start.16
  62.4 0.1 stack.99.where_ref
  62.6 1.3 %collective-permute-done.12.refs_8_ = bf16[576,512]{1,0:T(8,128)(2,1)} collective-permute-done((bf16[576,512]{1,0:T(8,128)(2,1)}, bf16[576,512]{1,0:T(8,128)(2,1)}, u32[]{:S(2)}, u32[]{:S(2)}) %collective-permute-start.12) | collective-permute-done | bytes 589856 | tf_op jit(solution)/shard_map/ppermute | solution.py:290
  63.9 0.8 collective-permute-done.16.refs_12_
  64.8 6.9 %attend.4 = (bf16[272,512]{1,0:T(8,128)(2,1)S(1)}, bf16[272,512]{1,0:T(8,128)(2,1)S(1)}) custom-call(s32[24]{0:T(128)S(1)} %stack.99.where_ref, bf16[4,592,128]{2,1,0:T(8,128)(2,1)} %collective-permute-done.5.refs_0_, bf16[576,1024]{1,0:T(8,128)(2,1)S(1)} %bitcast.30, bf16[576,1024]{1,0:T(8,128)(2,1)S(1)} %collective-permute-done.6.refs_2_, ...), custom_call_target="tpu_custom_call" | custom-call | flops 1000 | bytes 1000 | tf_op jit(solution)/shard_map/attend/pallas_call | solution.py:164
  71.7 1.6 %collective-permute-start.18 = (bf16[272,512]{1,0:T(8,128)(2,1)S(1)}, bf16[272,512]{1,0:T(8,128)(2,1)S(1)}, u32[]{:S(2)}, u32[]{:S(2)}) collective-permute-start(bf16[272,512]{1,0:T(8,128)(2,1)S(1)} %get-tuple-element.24), channel_id=1, source_target_pairs={{0,16},{4,20},{8,24},{12,28},{16,0},{20,4},{24,8},{28,12},{1,17},{... | collective-permute-start | bytes 835592 | tf_op jit(solution)/shard_map/ppermute | solution.py:290
  73.3 6.9 %attend.5 = (bf16[272,512]{1,0:T(8,128)(2,1)S(1)}, bf16[272,512]{1,0:T(8,128)(2,1)S(1)}) custom-call(s32[24]{0:T(128)S(1)} %stack.99.where_ref, bf16[4,592,128]{2,1,0:T(8,128)(2,1)} %collective-permute-done.4.refs_0_, bf16[576,1024]{1,0:T(8,128)(2,1)S(1)} %bitcast.31, bf16[576,1024]{1,0:T(8,128)(2,1)S(1)} %collective-permute-done.6.refs_2_, ...), custom_call_target="tpu_custom_call" | custom-call | flops 1000 | bytes 1000 | tf_op jit(solution)/shard_map/attend/pallas_call | solution.py:164
  80.2 0.2 collective-permute-done.18.refs_0_
  80.5 0.3 combine.3
  80.7 2.2 %collective-permute-start.19 = (bf16[272,512]{1,0:T(8,128)(2,1)S(1)}, bf16[272,512]{1,0:T(8,128)(2,1)S(1)}, u32[]{:S(2)}, u32[]{:S(2)}) collective-permute-start(bf16[272,512]{1,0:T(8,128)(2,1)S(1)} %combine.3), channel_id=1, source_target_pairs={{0,2},{1,3},{2,0},{3,1},{4,6},{5,7},{6,4},{7,5},{8,10},{9,11},{10,... | collective-permute-start | bytes 835592 | tf_op jit(solution)/shard_map/ppermute | solution.py:290
  83.0 1.5 %collective-permute-start.17 = (bf16[272,512]{1,0:T(8,128)(2,1)S(1)}, bf16[272,512]{1,0:T(8,128)(2,1)S(1)}, u32[]{:S(2)}, u32[]{:S(2)}) collective-permute-start(bf16[272,512]{1,0:T(8,128)(2,1)S(1)} %get-tuple-element.23), channel_id=1, source_target_pairs={{0,16},{4,20},{8,24},{12,28},{16,0},{20,4},{24,8},{28,12},{1,17},{... | collective-permute-start | bytes 835592 | tf_op jit(solution)/shard_map/ppermute | solution.py:290
  84.5 6.9 %attend.6 = bf16[528,512]{1,0:T(8,128)(2,1)S(1)} custom-call(s32[24]{0:T(128)S(1)} %stack.99.where_ref, bf16[4,592,128]{2,1,0:T(8,128)(2,1)} %collective-permute-done.3.refs_0_, bf16[576,1024]{1,0:T(8,128)(2,1)S(1)} %bitcast.32, bf16[576,1024]{1,0:T(8,128)(2,1)S(1)} %collective-permute-done.6.refs_2_, bf16[576,1024]{1,0:T(8,128)(2,1)S(1)} %collective-permute-done.7.refs_3_, ...), custom_call_target="tpu_custom_call" | custom-call | flops 1000 | bytes 1000 | tf_op jit(solution)/shard_map/attend/pallas_call | solution.py:164
  91.4 4.4 %collective-permute-done.19.refs_0_ = bf16[272,512]{1,0:T(8,128)(2,1)S(1)} collective-permute-done((bf16[272,512]{1,0:T(8,128)(2,1)S(1)}, bf16[272,512]{1,0:T(8,128)(2,1)S(1)}, u32[]{:S(2)}, u32[]{:S(2)}) %collective-permute-start.19) | collective-permute-done | bytes 278560 | tf_op jit(solution)/shard_map/ppermute | solution.py:290
  95.8 1.2 %collective-permute-start.21 = (bf16[528,512]{1,0:T(8,128)(2,1)S(1)}, bf16[528,512]{1,0:T(8,128)(2,1)S(1)}, u32[]{:S(2)}, u32[]{:S(2)}) collective-permute-start(bf16[528,512]{1,0:T(8,128)(2,1)S(1)} %attend.6), channel_id=1, source_target_pairs={{0,16},{4,20},{8,24},{12,28},{16,0},{20,4},{24,8},{28,12},{1,17},{... | collective-permute-start | bytes 1622024 | tf_op jit(solution)/shard_map/ppermute | solution.py:290
  97.1 0.3 combine.2
  97.3 0.1 collective-permute-start.20
  97.4 7.1 %attend.7.refs_2_ = bf16[528,512]{1,0:T(8,128)(2,1)S(1)} custom-call(s32[24]{0:T(128)S(1)} %stack.99.where_ref, bf16[4,592,128]{2,1,0:T(8,128)(2,1)} %table.1.refs_0_, bf16[576,1024]{1,0:T(8,128)(2,1)S(1)} %bitcast.33, bf16[576,1024]{1,0:T(8,128)(2,1)S(1)} %collective-permute-done.6.refs_2_, bf16[576,1024]{1,0:T(8,128)(2,1)S(1)} %collective-permute-done.7.refs_3_, ...), custom_call_target="tpu_custom_call" | custom-call | flops 1000 | bytes 1000 | tf_op jit(solution)/shard_map/attend/pallas_call | solution.py:164
  104.6 4.2 %collective-permute-done.21.refs_1_ = bf16[528,512]{1,0:T(8,128)(2,1)S(1)} collective-permute-done((bf16[528,512]{1,0:T(8,128)(2,1)S(1)}, bf16[528,512]{1,0:T(8,128)(2,1)S(1)}, u32[]{:S(2)}, u32[]{:S(2)}) %collective-permute-start.21) | collective-permute-done | bytes 540704 | tf_op jit(solution)/shard_map/ppermute | solution.py:290
  108.8 1.1 finish.2.refs_3_
  109.9 1.2 %collective-permute-done.20.refs_0_ = bf16[272,512]{1,0:T(8,128)(2,1)S(1)} collective-permute-done((bf16[272,512]{1,0:T(8,128)(2,1)S(1)}, bf16[272,512]{1,0:T(8,128)(2,1)S(1)}, u32[]{:S(2)}, u32[]{:S(2)}) %collective-permute-start.20) | collective-permute-done | bytes 278560 | tf_op jit(solution)/shard_map/ppermute | solution.py:290
  111.0 1.1 finish.3
  (30 shorter events, 0.1 us)
Async XLA Ops:
  0.6 7.0 %copy-start.7 = (bf16[4,64]{1,0:T(4,128)(2,1)S(1)}, bf16[4,64]{1,0:T(4,128)(2,1)}, u32[]{:S(2)}) copy-start(bf16[4,64]{1,0:T(4,128)(2,1)} %param.10) | copy-start | bytes 1540
  0.6 7.0 %copy-start.6 = (bf16[4,64,128]{2,1,0:T(8,128)(2,1)S(1)}, bf16[4,64,128]{2,1,0:T(8,128)(2,1)}, u32[]{:S(2)}) copy-start(bf16[4,64,128]{2,1,0:T(8,128)(2,1)} %param.9) | copy-start | bytes 196612
  0.7 7.1 %copy-start.2 = (bf16[4,128,576]{1,2,0:T(8,128)(2,1)S(1)}, bf16[4,128,576]{1,2,0:T(8,128)(2,1)}, u32[]{:S(2)}) copy-start(bf16[4,128,576]{1,2,0:T(8,128)(2,1)} %param.8) | copy-start | bytes 1769476
  0.7 7.1 %copy-start.3 = (s32[4,2048]{1,0:T(4,128)S(1)}, s32[4,2048]{1,0:T(4,128)}, u32[]{:S(2)}) copy-start(s32[4,2048]{1,0:T(4,128)} %selected_ref.1) | copy-start | bytes 98308
  0.7 30.1 %collective-permute-start.7 = (bf16[576,1024]{1,0:T(8,128)(2,1)}, bf16[576,1024]{1,0:T(8,128)(2,1)S(1)}, u32[]{:S(2)}, u32[]{:S(2)}) collective-permute-start(bf16[576,1024]{1,0:T(8,128)(2,1)} %bitcast.27), channel_id=1, source_target_pairs={{0,8},{4,12},{8,0},{12,4},{16,24},{20,28},{24,16},{28,20},{1,9},{5... | collective-permute-start | bytes 3538952 | tf_op jit(solution)/shard_map/ppermute | solution.py:290
  6.0 24.8 %collective-permute-start.9 = (bf16[576,512]{1,0:T(8,128)(2,1)}, bf16[576,512]{1,0:T(8,128)(2,1)}, u32[]{:S(2)}, u32[]{:S(2)}) collective-permute-start(bf16[576,512]{1,0:T(8,128)(2,1)} %get-tuple-element.33), channel_id=1, source_target_pairs={{0,1},{1,0},{2,3},{3,2},{4,5},{5,4},{6,7},{7,6},{8,9},{9,8},{10,11... | collective-permute-start | bytes 1769480 | tf_op jit(solution)/shard_map/ppermute | solution.py:290
  7.6 41.4 %copy-start = (bf16[1024,576]{0,1:T(8,128)(2,1)S(1)}, bf16[1024,576]{0,1:T(8,128)(2,1)}, u32[]{:S(2)}) copy-start(bf16[1024,576]{0,1:T(8,128)(2,1)} %param.6) | copy-start | bytes 3538948
  7.6 4.2 %collective-permute-start = (bf16[4,80,128]{2,1,0:T(8,128)(2,1)S(1)}, bf16[4,80,128]{2,1,0:T(8,128)(2,1)S(1)}, u32[]{:S(2)}, u32[]{:S(2)}) collective-permute-start(bf16[4,80,128]{2,1,0:T(8,128)(2,1)S(1)} %pad_maximum_fusion), channel_id=1, source_target_pairs={{0,4},{4,0},{8,12},{12,8},{16,20},{20,16},{24,28},{28,24},{1,5},{5... | collective-permute-start | bytes 245768 | tf_op jit(solution)/shard_map/ppermute | solution.py:290
  9.2 30.4 %collective-permute-start.4 = (bf16[4,592,128]{2,1,0:T(8,128)(2,1)}, bf16[4,592,128]{2,1,0:T(8,128)(2,1)}, u32[]{:S(2)}, u32[]{:S(2)}) collective-permute-start(bf16[4,592,128]{2,1,0:T(8,128)(2,1)} %table.1.refs_0_), channel_id=1, source_target_pairs={{0,2},{1,3},{2,0},{3,1},{4,6},{5,7},{6,4},{7,5},{8,10},{9,11},{10,... | collective-permute-start | bytes 1818632 | tf_op jit(solution)/shard_map/ppermute | solution.py:290
  11.9 22.3 %collective-permute-start.1 = (bf16[8,80,128]{2,1,0:T(8,128)(2,1)S(1)}, bf16[8,80,128]{2,1,0:T(8,128)(2,1)S(1)}, u32[]{:S(2)}, u32[]{:S(2)}) collective-permute-start(bf16[8,80,128]{2,1,0:T(8,128)(2,1)S(1)} %maximum_select_fusion.2), channel_id=1, source_target_pairs={{0,8},{4,12},{8,0},{12,4},{16,24},{20,28},{24,16},{28,20},{1,9},{5... | collective-permute-start | bytes 491528 | tf_op jit(solution)/shard_map/ppermute | solution.py:290
  12.5 37.0 %collective-permute-start.3 = (bf16[4,592,128]{2,1,0:T(8,128)(2,1)}, bf16[4,592,128]{2,1,0:T(8,128)(2,1)}, u32[]{:S(2)}, u32[]{:S(2)}) collective-permute-start(bf16[4,592,128]{2,1,0:T(8,128)(2,1)} %table.1.refs_0_), channel_id=1, source_target_pairs={{0,16},{4,20},{8,24},{12,28},{16,0},{20,4},{24,8},{28,12},{1,17},{... | collective-permute-start | bytes 1818632 | tf_op jit(solution)/shard_map/ppermute | solution.py:290
  30.8 17.5 %collective-permute-start.13 = (bf16[576,512]{1,0:T(8,128)(2,1)}, bf16[576,512]{1,0:T(8,128)(2,1)}, u32[]{:S(2)}, u32[]{:S(2)}) collective-permute-start(bf16[576,512]{1,0:T(8,128)(2,1)} %get-tuple-element.20), channel_id=1, source_target_pairs={{0,1},{1,0},{2,3},{3,2},{4,5},{5,4},{6,7},{7,6},{8,9},{9,8},{10,11... | collective-permute-start | bytes 1769480 | tf_op jit(solution)/shard_map/ppermute | solution.py:290
  30.8 17.5 %collective-permute-start.11 = (bf16[576,512]{1,0:T(8,128)(2,1)}, bf16[576,512]{1,0:T(8,128)(2,1)}, u32[]{:S(2)}, u32[]{:S(2)}) collective-permute-start(bf16[576,512]{1,0:T(8,128)(2,1)} %collective-permute-done.9.refs_5_), channel_id=1, source_target_pairs={{0,8},{4,12},{8,0},{12,4},{16,24},{20,28},{24,16},{28,20},{1,9},{5... | collective-permute-start | bytes 1769480 | tf_op jit(solution)/shard_map/ppermute | solution.py:290
  34.2 15.3 %copy-start.4 = (bf16[16,80,128]{2,1,0:T(8,128)(2,1)}, bf16[16,80,128]{2,1,0:T(8,128)(2,1)S(1)}, u32[]{:S(2)}) copy-start(bf16[16,80,128]{2,1,0:T(8,128)(2,1)S(1)} %maximum_select_fusion.1) | copy-start | bytes 983044
  34.2 14.8 %collective-permute-start.2 = (bf16[16,80,128]{2,1,0:T(8,128)(2,1)S(1)}, bf16[16,80,128]{2,1,0:T(8,128)(2,1)S(1)}, u32[]{:S(2)}, u32[]{:S(2)}) collective-permute-start(bf16[16,80,128]{2,1,0:T(8,128)(2,1)S(1)} %maximum_select_fusion.1), channel_id=1, source_target_pairs={{0,16},{4,20},{8,24},{12,28},{16,0},{20,4},{24,8},{28,12},{1,17},{... | collective-permute-start | bytes 983048 | tf_op jit(solution)/shard_map/ppermute | solution.py:290
  39.7 19.0 %collective-permute-start.5 = (bf16[4,592,128]{2,1,0:T(8,128)(2,1)}, bf16[4,592,128]{2,1,0:T(8,128)(2,1)}, u32[]{:S(2)}, u32[]{:S(2)}) collective-permute-start(bf16[4,592,128]{2,1,0:T(8,128)(2,1)} %collective-permute-done.4.refs_0_), channel_id=1, source_target_pairs={{0,16},{4,20},{8,24},{12,28},{16,0},{20,4},{24,8},{28,12},{1,17},{... | collective-permute-start | bytes 1818632 | tf_op jit(solution)/shard_map/ppermute | solution.py:290
  48.3 13.3 %collective-permute-start.15 = (bf16[576,512]{1,0:T(8,128)(2,1)}, bf16[576,512]{1,0:T(8,128)(2,1)}, u32[]{:S(2)}, u32[]{:S(2)}) collective-permute-start(bf16[576,512]{1,0:T(8,128)(2,1)} %collective-permute-done.13.refs_9_), channel_id=1, source_target_pairs={{0,8},{4,12},{8,0},{12,4},{16,24},{20,28},{24,16},{28,20},{1,9},{5... | collective-permute-start | bytes 1769480 | tf_op jit(solution)/shard_map/ppermute | solution.py:290
  49.0 13.6 %collective-permute-start.6 = (bf16[576,1024]{1,0:T(8,128)(2,1)S(1)}, bf16[576,1024]{1,0:T(8,128)(2,1)S(1)}, u32[]{:S(2)}, u32[]{:S(2)}) collective-permute-start(bf16[576,1024]{1,0:T(8,128)(2,1)S(1)} %bitcast.29), channel_id=1, source_target_pairs={{0,4},{4,0},{8,12},{12,8},{16,20},{20,16},{24,28},{28,24},{1,5},{5... | collective-permute-start | bytes 3538952 | tf_op jit(solution)/shard_map/ppermute | solution.py:290
  49.0 0.7 copy-start.5
  49.0 12.6 %collective-permute-start.10 = (bf16[576,512]{1,0:T(8,128)(2,1)}, bf16[576,512]{1,0:T(8,128)(2,1)}, u32[]{:S(2)}, u32[]{:S(2)}) collective-permute-start(bf16[576,512]{1,0:T(8,128)(2,1)} %collective-permute-done.9.refs_5_), channel_id=1, source_target_pairs={{0,4},{4,0},{8,12},{12,8},{16,20},{20,16},{24,28},{28,24},{1,5},{5... | collective-permute-start | bytes 1769480 | tf_op jit(solution)/shard_map/ppermute | solution.py:290
  49.7 14.2 %collective-permute-start.8 = (bf16[576,1024]{1,0:T(8,128)(2,1)S(1)}, bf16[576,1024]{1,0:T(8,128)(2,1)}, u32[]{:S(2)}, u32[]{:S(2)}) collective-permute-start(bf16[576,1024]{1,0:T(8,128)(2,1)S(1)} %collective-permute-done.7.refs_3_), channel_id=1, source_target_pairs={{0,4},{4,0},{8,12},{12,8},{16,20},{20,16},{24,28},{28,24},{1,5},{5... | collective-permute-start | bytes 3538952 | tf_op jit(solution)/shard_map/ppermute | solution.py:290
  50.2 1.6 %copy-start.1 = (bf16[4096,128]{1,0:T(8,128)(2,1)S(1)}, bf16[4096,128]{1,0:T(8,128)(2,1)}, u32[]{:S(2)}) copy-start(bf16[4096,128]{1,0:T(8,128)(2,1)} %keys_ref.1) | copy-start | bytes 3145732
  58.7 3.9 %collective-permute-start.14 = (bf16[576,512]{1,0:T(8,128)(2,1)}, bf16[576,512]{1,0:T(8,128)(2,1)}, u32[]{:S(2)}, u32[]{:S(2)}) collective-permute-start(bf16[576,512]{1,0:T(8,128)(2,1)} %collective-permute-done.13.refs_9_), channel_id=1, source_target_pairs={{0,4},{4,0},{8,12},{12,8},{16,20},{20,16},{24,28},{28,24},{1,5},{5... | collective-permute-start | bytes 1769480 | tf_op jit(solution)/shard_map/ppermute | solution.py:290
  61.6 2.3 %collective-permute-start.12 = (bf16[576,512]{1,0:T(8,128)(2,1)}, bf16[576,512]{1,0:T(8,128)(2,1)}, u32[]{:S(2)}, u32[]{:S(2)}) collective-permute-start(bf16[576,512]{1,0:T(8,128)(2,1)} %collective-permute-done.11.refs_7_), channel_id=1, source_target_pairs={{0,4},{4,0},{8,12},{12,8},{16,20},{20,16},{24,28},{28,24},{1,5},{5... | collective-permute-start | bytes 1769480 | tf_op jit(solution)/shard_map/ppermute | solution.py:290
  61.6 3.2 %collective-permute-start.16 = (bf16[576,512]{1,0:T(8,128)(2,1)}, bf16[576,512]{1,0:T(8,128)(2,1)}, u32[]{:S(2)}, u32[]{:S(2)}) collective-permute-start(bf16[576,512]{1,0:T(8,128)(2,1)} %collective-permute-done.15.refs_11_), channel_id=1, source_target_pairs={{0,4},{4,0},{8,12},{12,8},{16,20},{20,16},{24,28},{28,24},{1,5},{5... | collective-permute-start | bytes 1769480 | tf_op jit(solution)/shard_map/ppermute | solution.py:290
  71.7 8.8 %collective-permute-start.18 = (bf16[272,512]{1,0:T(8,128)(2,1)S(1)}, bf16[272,512]{1,0:T(8,128)(2,1)S(1)}, u32[]{:S(2)}, u32[]{:S(2)}) collective-permute-start(bf16[272,512]{1,0:T(8,128)(2,1)S(1)} %get-tuple-element.24), channel_id=1, source_target_pairs={{0,16},{4,20},{8,24},{12,28},{16,0},{20,4},{24,8},{28,12},{1,17},{... | collective-permute-start | bytes 835592 | tf_op jit(solution)/shard_map/ppermute | solution.py:290
  80.7 15.1 %collective-permute-start.19 = (bf16[272,512]{1,0:T(8,128)(2,1)S(1)}, bf16[272,512]{1,0:T(8,128)(2,1)S(1)}, u32[]{:S(2)}, u32[]{:S(2)}) collective-permute-start(bf16[272,512]{1,0:T(8,128)(2,1)S(1)} %combine.3), channel_id=1, source_target_pairs={{0,2},{1,3},{2,0},{3,1},{4,6},{5,7},{6,4},{7,5},{8,10},{9,11},{10,... | collective-permute-start | bytes 835592 | tf_op jit(solution)/shard_map/ppermute | solution.py:290
  83.0 14.1 %collective-permute-start.17 = (bf16[272,512]{1,0:T(8,128)(2,1)S(1)}, bf16[272,512]{1,0:T(8,128)(2,1)S(1)}, u32[]{:S(2)}, u32[]{:S(2)}) collective-permute-start(bf16[272,512]{1,0:T(8,128)(2,1)S(1)} %get-tuple-element.23), channel_id=1, source_target_pairs={{0,16},{4,20},{8,24},{12,28},{16,0},{20,4},{24,8},{28,12},{1,17},{... | collective-permute-start | bytes 835592 | tf_op jit(solution)/shard_map/ppermute | solution.py:290
  95.8 12.9 %collective-permute-start.21 = (bf16[528,512]{1,0:T(8,128)(2,1)S(1)}, bf16[528,512]{1,0:T(8,128)(2,1)S(1)}, u32[]{:S(2)}, u32[]{:S(2)}) collective-permute-start(bf16[528,512]{1,0:T(8,128)(2,1)S(1)} %attend.6), channel_id=1, source_target_pairs={{0,16},{4,20},{8,24},{12,28},{16,0},{20,4},{24,8},{28,12},{1,17},{... | collective-permute-start | bytes 1622024 | tf_op jit(solution)/shard_map/ppermute | solution.py:290
  97.3 13.7 %collective-permute-start.20 = (bf16[272,512]{1,0:T(8,128)(2,1)S(1)}, bf16[272,512]{1,0:T(8,128)(2,1)S(1)}, u32[]{:S(2)}, u32[]{:S(2)}) collective-permute-start(bf16[272,512]{1,0:T(8,128)(2,1)S(1)} %combine.2), channel_id=1, source_target_pairs={{0,2},{1,3},{2,0},{3,1},{4,6},{5,7},{6,4},{7,5},{8,10},{9,11},{10,... | collective-permute-start | bytes 835592 | tf_op jit(solution)/shard_map/ppermute | solution.py:290

commit v4 on v3

--- a/solution.py
+++ b/solution.py
@@ -77,47 +77,47 @@
     return jnp.concatenate(three(total) + three(peak) + [pad], axis=0).astype(jnp.bfloat16)
 
 
-def attend_kernel(blocks, shards, per, width, masked, parts, where_ref, *refs):
+def attend_kernel(places, blocks, per, width, sizes, masked, parts, *refs):
+    shards = len(places)
     packs, slabs = refs[:blocks], refs[blocks : blocks + shards]
-    outs, keys = refs[blocks + shards : -1], refs[-1]
+    outs, keys, table = refs[blocks + shards : -2], refs[-2], refs[-1]
     some = per // parts
     rows = blocks * per
     span = RUN * RUN
-    his = packs[0].shape[1] - width
-    hi_at = lax.broadcasted_iota(jnp.int32, (his, LANES), 0)
-    lane_at = lax.broadcasted_iota(jnp.int32, (RUN, span), 1).astype(jnp.float32)
-    tables = [
-        packs[row // per][row % per, width:, :].astype(jnp.float32) for row in range(rows)
-    ]
-    valid, begin = [], 0
-    for shard in range(shards):
-        runs = slabs[shard].shape[1] // RUN
-        own = [
-            jnp.sum(jnp.where(hi_at == where_ref[2 * shard], table, 0.0), axis=0, keepdims=True)
-            for table in tables
-        ]
-        line = jnp.concatenate(own, axis=0)
-        line = pltpu.roll(line, where_ref[2 * shard + 1], 1)
-        column = jnp.transpose(line)[:runs, :]
-        base = (lax.broadcasted_iota(jnp.int32, column.shape, 0) % RUN * RUN).astype(jnp.float32)
-        target = jnp.where(column > 0.0, base + column - 1.0, -1.0)
-        valid.append(column)
-        for at in range(runs // RUN):
+    here, plane = lax.axis_index("ctx"), lax.axis_index("row")
+    planes, tokens = sizes
+    for i, pack in enumerate(packs):
+        table[i * per : (i + 1) * per] = pack[:, width:, :].astype(jnp.float32)
+    spare = [jnp.zeros((-rows % 8, LANES), jnp.float32)] * (rows % 8 > 0)
+    lane = lax.broadcasted_iota(jnp.int32, (rows + -rows % 8, LANES), 1)
+    base = (lane % RUN * RUN - 1).astype(jnp.float32)
+    spread = lax.broadcasted_iota(jnp.int32, (RUN, span), 1).astype(jnp.float32)
+    targets, begin = [], 0
+    for slab, (core, across, mask, offset) in zip(slabs, places):
+        start = ((here ^ mask ^ core) * planes + (plane ^ across)) * (tokens // RUN) + offset // RUN
+        row, shift = start // LANES, (LANES - start % LANES + begin) % LANES
+        line = [table[i, pl.ds(row, 1), :] for i in range(rows)]
+        line = pltpu.roll(jnp.concatenate(line + spare, axis=0), shift, 1)
+        tile = line if begin % LANES == 0 else jnp.where(lane >= begin % LANES, line, tile)
+        begin += slab.shape[1] // RUN
+        if begin % LANES == 0:
+            targets.append(jnp.transpose(jnp.where(tile > 0.0, base + tile, -1.0)))
+    slot = 0
+    for slab in slabs:
+        for at in range(0, slab.shape[1], span):
+            target = targets[slot // LANES][slot % LANES : slot % LANES + RUN, :]
             hits = [
-                (lane_at == target[at * RUN : (at + 1) * RUN, row : row + 1])
-                .astype(jnp.float32)
-                .astype(jnp.bfloat16)
-                for row in range(rows)
+                (spread == target[:, i : i + 1]).astype(jnp.float32).astype(jnp.bfloat16)
+                for i in range(rows)
             ]
             picked = lax.dot_general(
                 jnp.concatenate(hits, axis=0),
-                slabs[shard][:, at * span : (at + 1) * span],
+                slab[:, at : at + span],
                 (((1,), (1,)), ((), ())),
                 preferred_element_type=jnp.float32,
             ).astype(jnp.bfloat16)
-            start = begin + at * RUN
-            keys[:, start : start + RUN, :] = picked.reshape(rows, RUN, width)
-        begin += runs
+            keys[:, slot : slot + RUN, :] = picked.reshape(rows, RUN, width)
+            slot += RUN
     for first in range(0, rows, BATCH):
         group = range(first, min(first + BATCH, rows))
         logits = [
@@ -131,7 +131,7 @@
         done = []
         for row, scores in zip(group, logits):
             if masked:
-                known = jnp.concatenate([v[:, row : row + 1] for v in valid], axis=0) > 0.0
+                known = jnp.concatenate([t[:, row : row + 1] for t in targets], axis=0) >= 0.0
                 known = jnp.broadcast_to(known, scores.shape)
                 scores = jnp.where(known, scores, -1e30)
             top = jnp.max(scores, axis=0, keepdims=True)
@@ -155,22 +155,24 @@
             out[some * heads :, at * LANES : (at + 1) * LANES] = aux_tile(total, peak)
 
 
-def attend(packs, slabs, where, width, masked, parts):
-    blocks, shards = len(packs), len(slabs)
-    per, _, heads = packs[0].shape
+def attend(packs, slabs, places, width, sizes, masked, parts):
+    blocks = len(packs)
+    per, tall, heads = packs[0].shape
     slots = sum(slab.shape[1] for slab in slabs) // RUN
-    rows = blocks * per
     out = VMEM((per // parts * heads + AUX, LATENT), jnp.bfloat16)
     return pl.pallas_call(
-        functools.partial(attend_kernel, blocks, shards, per, width, masked, parts),
+        functools.partial(attend_kernel, places, blocks, per, width, sizes, masked, parts),
         out_shape=[out] * (blocks * parts),
-        in_specs=[pl.BlockSpec(memory_space=pltpu.SMEM)] + whole_vmem(blocks + shards),
+        in_specs=whole_vmem(blocks + len(slabs)),
         out_specs=whole_vmem(blocks * parts),
-        scratch_shapes=[pltpu.VMEM((rows, slots, width), jnp.bfloat16)],
+        scratch_shapes=[
+            VMEM((blocks * per, slots, width), jnp.bfloat16),
+            VMEM((blocks * per, tall - width, LANES), jnp.float32),
+        ],
         compiler_params=params(14),
         cost_estimate=TINY,
         name="attend",
-    )(where, *near(packs), *near(slabs))
+    )(*near(packs), *near(slabs))
 
 
 def combine_kernel(begins, rows, heads, last, *refs):
@@ -230,7 +232,7 @@
     )(*near(parts), *more)
 
 
-def index_kernel(heads, meta_ref, keys_ref, out_ref, gate_scr):
+def index_kernel(heads, per, meta_ref, keys_ref, out_ref, gate_scr):
     rows = meta_ref.shape[0]
     tokens = keys_ref.shape[0]
 
@@ -245,25 +247,31 @@
             for i in range(8):
                 gate_scr[first + i] = jnp.broadcast_to(turned[:heads, i : i + 1], (heads, LANES))
 
-    for first in range(0, rows, 8):
-        queries = jnp.concatenate([meta_ref[first + i, :heads, :] for i in range(8)], axis=0)
+    for first in range(0, rows, 2 * per):
+        queries = jnp.concatenate([meta_ref[first + i, :heads, :] for i in range(2 * per)], axis=0)
         logits = lax.dot_general(
             queries, keys_ref[...], (((1,), (1,)), ((), ())), preferred_element_type=jnp.float32
         )
         lines = []
-        for i in range(8):
+        for i in range(2 * per):
             gate = jnp.concatenate([gate_scr[first + i]] * (tokens // LANES), axis=1)
             terms = jnp.maximum(logits[i * heads : (i + 1) * heads, :], 0.0) * gate
             lines.append(jnp.sum(terms, axis=0, keepdims=True))
-        out_ref[first : first + 8, :] = jnp.concatenate(lines, axis=0)
-
-
-def index_block(meta, index_keys, heads):
+        here = lax.axis_index("ctx")
+        ours, mates = lines[:per], lines[per:]
+        group = jnp.where(
+            here % 2 == 0, jnp.concatenate(ours + mates, axis=0), jnp.concatenate(mates + ours, axis=0)
+        )
+        place = (here // 2) ^ (first // (2 * per))
+        out_ref[pl.ds(pl.multiple_of(place * 2 * per, 2 * per), 2 * per), :] = group
+
+
+def index_block(meta, index_keys, heads, per):
     rows, tall, size = meta.shape
     tokens = index_keys.shape[0]
     block = 512
     return pl.pallas_call(
-        functools.partial(index_kernel, heads),
+        functools.partial(index_kernel, heads, per),
         grid=(tokens // block,),
         out_shape=jax.ShapeDtypeStruct((rows, tokens), jnp.float32),
         in_specs=[
@@ -290,7 +298,6 @@
         return lax.ppermute(array, axis, [(i, i ^ mask) for i in range(size)])
 
     def body(latent_cache, index_keys, query_latent, index_query, index_gates, selected):
-        here, plane = lax.axis_index("ctx"), lax.axis_index("row")
         per, _, width = query_latent.shape
         heads = query_latent.shape[1]
         tokens = latent_cache.shape[0]
@@ -310,8 +317,7 @@
         bit = 1
         while bit < columns:
             other = swap(meta, "ctx", bit)
-            low, high = jnp.concatenate([meta, other]), jnp.concatenate([other, meta])
-            meta = jnp.where(here & bit == 0, low, high)
+            meta = jnp.concatenate([meta, other])
             bit *= 2
 
         packed = with_table(query, selected, all_runs // LANES)
@@ -322,7 +328,7 @@
         }
         near_queries = list(groups[0].values()) + list(starts.values())
         far_queries = [pack for group in groups.values() for pack in group.values()]
-        index_scores = index_block(after(meta, *near_queries), index_keys, index_query.shape[1])
+        index_scores = index_block(after(meta, *near_queries), index_keys, index_query.shape[1], per)
 
         half = tokens // 2
         pieces, sent, shown = [(0, 0, slab)], [], []
@@ -331,7 +337,7 @@
                 piece = slab[:, offset : offset + half]
                 sent.append(swap(after(piece, *sent[-1:]), "row", across))
                 pieces.append((across, offset, sent[-1]))
-        slabs, where = [], []
+        slabs, places = [], []
         for across, offset, piece in pieces:
             for mask in token_columns:
                 one = piece
@@ -343,21 +349,18 @@
                     if core and mask and offset:
                         one = after(one, index_scores, *far_queries)
                     slabs.append(swap(one, "ctx", 1) if core else one)
-                    start = (here ^ mask ^ core) * planes + (plane ^ across)
-                    start = (start * tokens + offset) // RUN
-                    where += [start // LANES, (-start) % LANES]
-        where = jnp.stack(where).astype(jnp.int32)
-
-        parts, last = [], after(where, index_scores)
+                    places.append((core, across, mask, offset))
+
+        parts, last = [], [index_scores]
         split = 2
         some = per // split
         for across in row_planes[1:] + row_planes[:1]:
             mine = []
             for mask in reversed(row_columns):
-                done = attend(
-                    [groups[across][mask]], slabs, last, width, masked, split if across else 1
-                )
-                last = after(where, *done)
+                pack = after(groups[across][mask], *last)
+                sizes = (planes, tokens)
+                done = attend([pack], slabs, places, width, sizes, masked, split if across else 1)
+                last = list(done)
                 first = [] if across else [back[0] for back in parts]
                 mine.append([swap(after(a, *first), "ctx", mask) if mask else a for a in done])
             if across:
@@ -366,7 +369,7 @@
                     rows = range(i * some, (i + 1) * some)
                     mixed = combine([part[i] for part in mine], [rows[0]] * len(mine), rows, heads)
                     back.append(swap(after(mixed, *back), "row", across))
-                    last = after(where, *done, mixed) if i == 0 else last
+                    last = last + [mixed] if i == 0 else last
                 parts.append(back)
             else:
                 own = [part[0] for part in mine]

time: 112 us -> 108 us (0.964)
  Pallas kernels: 39 us -> 27 us
  waiting for transfers between devices: 43.8 us -> 54.1 us
  local copies, waits for them, and re-layouts: 2.85 us -> 1.36 us
  other arithmetic: 1.54 us -> 0.08 us
    pallas_call x5, Pallas kernels: 34.7 us -> 23.6 us  [the longest x4 16.7 us: attend(): pl.pallas_call(functools.partial(attend_kernel, places, blocks, per, widt...]
    ppermute x22, waiting for transfers between devices: 43.8 us -> 54.1 us  [swap(): return lax.ppermute(array, axis, [(i, i ^ mask) for i in range(size)])]
    select_n x3 -> x0, other arithmetic: 1.53 us -> none  [body(): meta = jnp.where(here & bit == 0, low, high)]
  transfers between devices with their start and end apart: 22 -> 22, of which waited for: 11 -> 13; matrix products, arithmetic and copies ran while one was open for 4% -> 1% of each run, Pallas kernels for 27% -> 20%
where the time goes in v4:
time: 108 us
  waiting for transfers between devices  54.1 us (50%)
  Pallas kernels  27 us (25%)
  starting transfers between devices  24.9 us (23%)
  local copies, waits for them, and re-layouts  1.36 us (1%)
    ppermute x22, waiting for transfers between devices, swap(): return lax.ppermute(array, axis, [(i, i ^ mask) for i in range(size)])  54.1 us
    ppermute x22, starting transfers between devices, swap(): return lax.ppermute(array, axis, [(i, i ^ mask) for i in range(size)])  24.9 us
    pallas_call x4, Pallas kernels, attend(): pl.pallas_call(functools.partial(attend_kernel, places, blocks, per, widt...  16.7 us
    pallas_call x1, Pallas kernels, index_block(): pl.pallas_call(functools.partial(index_kernel, heads, per), grid=(tokens...  6.87 us
    pallas_call x2, Pallas kernels, finish(): pl.pallas_call(functools.partial(combine_kernel, begins, rows, heads, Tru...  2.23 us
  transfers between devices with their start and end apart: 22, of which 13 were waited for; matrix products, arithmetic and copies ran while one was open for 1% of the time, Pallas kernels for 20%

profile of v4, /device:TPU:0, one launch (start us, length us, event | category | flops | bytes accessed | tf_op | source)
XLA Modules:
  0.0 108.2 jit_solution(8117203658703710295)
XLA Ops:
  0.7 3.0 %collective-permute-start.7 = (bf16[576,1024]{1,0:T(8,128)(2,1)}, bf16[576,1024]{1,0:T(8,128)(2,1)S(1)}, u32[]{:S(2)}, u32[]{:S(2)}) collective-permute-start(bf16[576,1024]{1,0:T(8,128)(2,1)} %bitcast.3), channel_id=1, source_target_pairs={{0,8},{4,12},{8,0},{12,4},{16,24},{20,28},{24,16},{28,20},{1,9},{5... | collective-permute-start | bytes 3538952 | tf_op jit(solution)/shard_map/ppermute | solution.py:298
  3.7 1.3 %fusion = (bf16[576,512]{1,0:T(8,128)(2,1)S(1)}, bf16[576,512]{1,0:T(8,128)(2,1)S(1)}) fusion(bf16[576,1024]{1,0:T(8,128)(2,1)} %bitcast.4), kind=kLoop, calls=%fused_computation.4 | loop fusion | bytes 2359296 | tf_op jit(solution)/shard_map/slice | solution.py:337
  5.0 1.6 %collective-permute-start.9 = (bf16[576,512]{1,0:T(8,128)(2,1)S(1)}, bf16[576,512]{1,0:T(8,128)(2,1)S(1)}, u32[]{:S(2)}, u32[]{:S(2)}) collective-permute-start(bf16[576,512]{1,0:T(8,128)(2,1)S(1)} %get-tuple-element.33), channel_id=1, source_target_pairs={{0,1},{1,0},{2,3},{3,2},{4,5},{5,4},{6,7},{7,6},{8,9},{9,8},{10,11... | collective-permute-start | bytes 1769480 | tf_op jit(solution)/shard_map/ppermute | solution.py:298
  6.7 0.0 copy-start
  6.7 0.1 collective-permute-start.2
  6.8 0.7 table.1.refs_0_
  7.5 2.6 %collective-permute-start = (bf16[4,592,128]{2,1,0:T(8,128)(2,1)S(1)}, bf16[4,592,128]{2,1,0:T(8,128)(2,1)S(1)}, u32[]{:S(2)}, u32[]{:S(2)}) collective-permute-start(bf16[4,592,128]{2,1,0:T(8,128)(2,1)S(1)} %table.1.refs_0_), channel_id=1, source_target_pairs={{0,2},{1,3},{2,0},{3,1},{4,6},{5,7},{6,4},{7,5},{8,10},{9,11},{10,... | collective-permute-start | bytes 1818632 | tf_op jit(solution)/shard_map/ppermute | solution.py:298
  10.1 0.6 collective-permute-start.3
  10.7 1.5 %collective-permute-start.5 = (bf16[4,592,128]{2,1,0:T(8,128)(2,1)S(1)}, bf16[4,592,128]{2,1,0:T(8,128)(2,1)S(1)}, u32[]{:S(2)}, u32[]{:S(2)}) collective-permute-start(bf16[4,592,128]{2,1,0:T(8,128)(2,1)S(1)} %table.1.refs_0_), channel_id=1, source_target_pairs={{0,16},{4,20},{8,24},{12,28},{16,0},{20,4},{24,8},{28,12},{1,17},{... | collective-permute-start | bytes 1818632 | tf_op jit(solution)/shard_map/ppermute | solution.py:298
  12.2 18.1 %collective-permute-done.9.refs_5_ = bf16[576,512]{1,0:T(8,128)(2,1)S(1)} collective-permute-done((bf16[576,512]{1,0:T(8,128)(2,1)S(1)}, bf16[576,512]{1,0:T(8,128)(2,1)S(1)}, u32[]{:S(2)}, u32[]{:S(2)}) %collective-permute-start.9) | collective-permute-done | bytes 589856 | tf_op jit(solution)/shard_map/ppermute | solution.py:298
  30.3 0.3 collective-permute-done.7.refs_3_
  30.7 2.1 %collective-permute-start.11 = (bf16[576,512]{1,0:T(8,128)(2,1)S(1)}, bf16[576,512]{1,0:T(8,128)(2,1)S(1)}, u32[]{:S(2)}, u32[]{:S(2)}) collective-permute-start(bf16[576,512]{1,0:T(8,128)(2,1)S(1)} %collective-permute-done.9.refs_5_), channel_id=1, source_target_pairs={{0,8},{4,12},{8,0},{12,4},{16,24},{20,28},{24,16},{28,20},{1,9},{5... | collective-permute-start | bytes 1769480 | tf_op jit(solution)/shard_map/ppermute | solution.py:298
  32.7 1.5 %collective-permute-done.3 = bf16[8,80,128]{2,1,0:T(8,128)(2,1)S(1)} collective-permute-done((bf16[8,80,128]{2,1,0:T(8,128)(2,1)S(1)}, bf16[8,80,128]{2,1,0:T(8,128)(2,1)S(1)}, u32[]{:S(2)}, u32[]{:S(2)}) %collective-permute-start.3) | collective-permute-done | bytes 163872 | tf_op jit(solution)/shard_map/ppermute | solution.py:298
  34.2 2.1 %collective-permute-start.4 = (bf16[16,80,128]{2,1,0:T(8,128)(2,1)S(1)}, bf16[16,80,128]{2,1,0:T(8,128)(2,1)S(1)}, u32[]{:S(2)}, u32[]{:S(2)}) collective-permute-start(bf16[16,80,128]{2,1,0:T(8,128)(2,1)S(1)} %pad_maximum_fusion.1), channel_id=1, source_target_pairs={{0,16},{4,20},{8,24},{12,28},{16,0},{20,4},{24,8},{28,12},{1,17},{... | collective-permute-start | bytes 983048 | tf_op jit(solution)/shard_map/ppermute | solution.py:298
  36.4 1.2 %collective-permute-done.refs_0_ = bf16[4,592,128]{2,1,0:T(8,128)(2,1)S(1)} collective-permute-done((bf16[4,592,128]{2,1,0:T(8,128)(2,1)S(1)}, bf16[4,592,128]{2,1,0:T(8,128)(2,1)S(1)}, u32[]{:S(2)}, u32[]{:S(2)}) %collective-permute-start) | collective-permute-done | bytes 606240 | tf_op jit(solution)/shard_map/ppermute | solution.py:298
  37.6 1.5 %collective-permute-start.1 = (bf16[4,592,128]{2,1,0:T(8,128)(2,1)S(1)}, bf16[4,592,128]{2,1,0:T(8,128)(2,1)S(1)}, u32[]{:S(2)}, u32[]{:S(2)}) collective-permute-start(bf16[4,592,128]{2,1,0:T(8,128)(2,1)S(1)} %collective-permute-done.refs_0_), channel_id=1, source_target_pairs={{0,16},{4,20},{8,24},{12,28},{16,0},{20,4},{24,8},{28,12},{1,17},{... | collective-permute-start | bytes 1818632 | tf_op jit(solution)/shard_map/ppermute | solution.py:298
  39.1 7.6 %collective-permute-done.13.refs_9_ = bf16[576,512]{1,0:T(8,128)(2,1)S(1)} collective-permute-done((bf16[576,512]{1,0:T(8,128)(2,1)S(1)}, bf16[576,512]{1,0:T(8,128)(2,1)S(1)}, u32[]{:S(2)}, u32[]{:S(2)}) %collective-permute-start.13) | collective-permute-done | bytes 589856 | tf_op jit(solution)/shard_map/ppermute | solution.py:298
  46.7 1.0 collective-permute-start.15
  47.8 0.5 collective-permute-start.10
  48.3 0.1 collective-permute-start.8
  48.4 6.9 %index.1 = f32[32,4096]{1,0:T(8,128)} custom-call(bf16[32,80,128]{2,1,0:T(8,128)(2,1)S(1)} %pad_maximum_fusion.meta_ref, bf16[4096,128]{1,0:T(8,128)(2,1)S(1)} %copy-done.1), custom_call_target="tpu_custom_call" | custom-call | flops 1000 | bytes 1000 | tf_op jit(solution)/shard_map/index/pallas_call | solution.py:273
  55.3 0.1 collective-permute-done.1.refs_0_
  55.3 0.4 collective-permute-start.14
  55.7 4.7 %collective-permute-done.15.refs_11_ = bf16[576,512]{1,0:T(8,128)(2,1)S(1)} collective-permute-done((bf16[576,512]{1,0:T(8,128)(2,1)S(1)}, bf16[576,512]{1,0:T(8,128)(2,1)S(1)}, u32[]{:S(2)}, u32[]{:S(2)}) %collective-permute-start.15) | collective-permute-done | bytes 589856 | tf_op jit(solution)/shard_map/ppermute | solution.py:298
  60.4 0.0 collective-permute-start.12
  60.4 0.0 collective-permute-done.10.refs_6_
  60.4 0.5 collective-permute-start.16
  60.9 0.0 collective-permute-done.6.refs_2_
  60.9 0.0 collective-permute-done.14.refs_10_
  60.9 1.5 %collective-permute-done.12.refs_8_ = bf16[576,512]{1,0:T(8,128)(2,1)S(1)} collective-permute-done((bf16[576,512]{1,0:T(8,128)(2,1)S(1)}, bf16[576,512]{1,0:T(8,128)(2,1)S(1)}, u32[]{:S(2)}, u32[]{:S(2)}) %collective-permute-start.12) | collective-permute-done | bytes 589856 | tf_op jit(solution)/shard_map/ppermute | solution.py:298
  62.4 0.8 collective-permute-done.16.refs_12_
  63.2 4.1 %attend.4 = (bf16[272,512]{1,0:T(8,128)(2,1)S(1)}, bf16[272,512]{1,0:T(8,128)(2,1)S(1)}) custom-call(bf16[4,592,128]{2,1,0:T(8,128)(2,1)S(1)} %collective-permute-done.1.refs_0_, bf16[576,1024]{1,0:T(8,128)(2,1)S(1)} %bitcast.6, bf16[576,1024]{1,0:T(8,128)(2,1)S(1)} %collective-permute-done.6.refs_2_, bf16[576,1024]{1,0:T(8,128)(2,1)S(1)} %collective-permute-done.7.refs_3_, ...), custom_call_target="tpu_custom_call" | custom-call | flops 1000 | bytes 1000 | tf_op jit(solution)/shard_map/attend/pallas_call | solution.py:163
  67.4 1.5 %collective-permute-start.18 = (bf16[272,512]{1,0:T(8,128)(2,1)S(1)}, bf16[272,512]{1,0:T(8,128)(2,1)S(1)}, u32[]{:S(2)}, u32[]{:S(2)}) collective-permute-start(bf16[272,512]{1,0:T(8,128)(2,1)S(1)} %get-tuple-element.24), channel_id=1, source_target_pairs={{0,16},{4,20},{8,24},{12,28},{16,0},{20,4},{24,8},{28,12},{1,17},{... | collective-permute-start | bytes 835592 | tf_op jit(solution)/shard_map/ppermute | solution.py:298
  68.9 4.1 %attend.5 = (bf16[272,512]{1,0:T(8,128)(2,1)S(1)}, bf16[272,512]{1,0:T(8,128)(2,1)S(1)}) custom-call(bf16[4,592,128]{2,1,0:T(8,128)(2,1)S(1)} %collective-permute-done.refs_0_, bf16[576,1024]{1,0:T(8,128)(2,1)S(1)} %bitcast.7, bf16[576,1024]{1,0:T(8,128)(2,1)S(1)} %collective-permute-done.6.refs_2_, bf16[576,1024]{1,0:T(8,128)(2,1)S(1)} %collective-permute-done.7.refs_3_, ...), custom_call_target="tpu_custom_call" | custom-call | flops 1000 | bytes 1000 | tf_op jit(solution)/shard_map/attend/pallas_call | solution.py:163
  73.0 3.1 %collective-permute-done.18.refs_0_ = bf16[272,512]{1,0:T(8,128)(2,1)S(1)} collective-permute-done((bf16[272,512]{1,0:T(8,128)(2,1)S(1)}, bf16[272,512]{1,0:T(8,128)(2,1)S(1)}, u32[]{:S(2)}, u32[]{:S(2)}) %collective-permute-start.18) | collective-permute-done | bytes 278560 | tf_op jit(solution)/shard_map/ppermute | solution.py:298
  76.1 0.3 combine.3
  76.4 2.6 %collective-permute-start.19 = (bf16[272,512]{1,0:T(8,128)(2,1)S(1)}, bf16[272,512]{1,0:T(8,128)(2,1)S(1)}, u32[]{:S(2)}, u32[]{:S(2)}) collective-permute-start(bf16[272,512]{1,0:T(8,128)(2,1)S(1)} %combine.3), channel_id=1, source_target_pairs={{0,2},{1,3},{2,0},{3,1},{4,6},{5,7},{6,4},{7,5},{8,10},{9,11},{10,... | collective-permute-start | bytes 835592 | tf_op jit(solution)/shard_map/ppermute | solution.py:298
  79.0 1.5 %collective-permute-start.17 = (bf16[272,512]{1,0:T(8,128)(2,1)S(1)}, bf16[272,512]{1,0:T(8,128)(2,1)S(1)}, u32[]{:S(2)}, u32[]{:S(2)}) collective-permute-start(bf16[272,512]{1,0:T(8,128)(2,1)S(1)} %get-tuple-element.23), channel_id=1, source_target_pairs={{0,16},{4,20},{8,24},{12,28},{16,0},{20,4},{24,8},{28,12},{1,17},{... | collective-permute-start | bytes 835592 | tf_op jit(solution)/shard_map/ppermute | solution.py:298
  80.5 4.1 %attend.6 = bf16[528,512]{1,0:T(8,128)(2,1)S(1)} custom-call(bf16[4,592,128]{2,1,0:T(8,128)(2,1)S(1)} %collective-permute-done.5.refs_0_, bf16[576,1024]{1,0:T(8,128)(2,1)S(1)} %bitcast.8, bf16[576,1024]{1,0:T(8,128)(2,1)S(1)} %collective-permute-done.6.refs_2_, bf16[576,1024]{1,0:T(8,128)(2,1)S(1)} %collective-permute-done.7.refs_3_, ...), custom_call_target="tpu_custom_call" | custom-call | flops 1000 | bytes 1000 | tf_op jit(solution)/shard_map/attend/pallas_call | solution.py:163
  84.7 6.5 %collective-permute-done.19.refs_0_ = bf16[272,512]{1,0:T(8,128)(2,1)S(1)} collective-permute-done((bf16[272,512]{1,0:T(8,128)(2,1)S(1)}, bf16[272,512]{1,0:T(8,128)(2,1)S(1)}, u32[]{:S(2)}, u32[]{:S(2)}) %collective-permute-start.19) | collective-permute-done | bytes 278560 | tf_op jit(solution)/shard_map/ppermute | solution.py:298
  91.2 1.5 %collective-permute-start.21 = (bf16[528,512]{1,0:T(8,128)(2,1)S(1)}, bf16[528,512]{1,0:T(8,128)(2,1)S(1)}, u32[]{:S(2)}, u32[]{:S(2)}) collective-permute-start(bf16[528,512]{1,0:T(8,128)(2,1)S(1)} %attend.6), channel_id=1, source_target_pairs={{0,16},{4,20},{8,24},{12,28},{16,0},{20,4},{24,8},{28,12},{1,17},{... | collective-permute-start | bytes 1622024 | tf_op jit(solution)/shard_map/ppermute | solution.py:298
  92.7 0.3 combine.2
  92.9 0.1 collective-permute-start.20
  93.0 4.3 %attend.7.refs_2_ = bf16[528,512]{1,0:T(8,128)(2,1)S(1)} custom-call(bf16[4,592,128]{2,1,0:T(8,128)(2,1)S(1)} %table.1.refs_0_, bf16[576,1024]{1,0:T(8,128)(2,1)S(1)} %bitcast.9, bf16[576,1024]{1,0:T(8,128)(2,1)S(1)} %collective-permute-done.6.refs_2_, bf16[576,1024]{1,0:T(8,128)(2,1)S(1)} %collective-permute-done.7.refs_3_, ...), custom_call_target="tpu_custom_call" | custom-call | flops 1000 | bytes 1000 | tf_op jit(solution)/shard_map/attend/pallas_call | solution.py:163
  97.3 7.0 %collective-permute-done.21.refs_1_ = bf16[528,512]{1,0:T(8,128)(2,1)S(1)} collective-permute-done((bf16[528,512]{1,0:T(8,128)(2,1)S(1)}, bf16[528,512]{1,0:T(8,128)(2,1)S(1)}, u32[]{:S(2)}, u32[]{:S(2)}) %collective-permute-start.21) | collective-permute-done | bytes 540704 | tf_op jit(solution)/shard_map/ppermute | solution.py:298
  104.3 1.1 %finish.2.refs_3_ = bf16[4,128,512]{2,1,0:T(8,128)(2,1)} custom-call(bf16[272,512]{1,0:T(8,128)(2,1)S(1)} %collective-permute-done.19.refs_0_, bf16[528,512]{1,0:T(8,128)(2,1)S(1)} %collective-permute-done.21.refs_1_, bf16[528,512]{1,0:T(8,128)(2,1)S(1)} %attend.7.refs_2_), custom_call_target="tpu_custom_call" | custom-call | flops 1000 | bytes 60000000 | tf_op jit(solution)/shard_map/finish/pallas_call | solution.py:222
  105.4 1.6 %collective-permute-done.20.refs_0_ = bf16[272,512]{1,0:T(8,128)(2,1)S(1)} collective-permute-done((bf16[272,512]{1,0:T(8,128)(2,1)S(1)}, bf16[272,512]{1,0:T(8,128)(2,1)S(1)}, u32[]{:S(2)}, u32[]{:S(2)}) %collective-permute-start.20) | collective-permute-done | bytes 278560 | tf_op jit(solution)/shard_map/ppermute | solution.py:298
  107.1 1.1 %finish.3 = bf16[4,128,512]{2,1,0:T(8,128)(2,1)} custom-call(bf16[272,512]{1,0:T(8,128)(2,1)S(1)} %collective-permute-done.20.refs_0_, bf16[528,512]{1,0:T(8,128)(2,1)S(1)} %collective-permute-done.21.refs_1_, bf16[528,512]{1,0:T(8,128)(2,1)S(1)} %attend.7.refs_2_, bf16[4,128,512]{2,1,0:T(8,128)(2,1)} %finish.2.refs_3_), custom_call_target="tpu_custom_call", output_to_operand_aliasing={{}: (3, {})} | custom-call | flops 1000 | bytes 1000 | tf_op jit(solution)/shard_map/finish/pallas_call | solution.py:222
  (25 shorter events, 0.1 us)
Async XLA Ops:
  0.6 6.0 %copy-start.5 = (bf16[4,64]{1,0:T(4,128)(2,1)S(1)}, bf16[4,64]{1,0:T(4,128)(2,1)}, u32[]{:S(2)}) copy-start(bf16[4,64]{1,0:T(4,128)(2,1)} %param.10) | copy-start | bytes 1540
  0.6 6.0 %copy-start.4 = (bf16[4,64,128]{2,1,0:T(8,128)(2,1)S(1)}, bf16[4,64,128]{2,1,0:T(8,128)(2,1)}, u32[]{:S(2)}) copy-start(bf16[4,64,128]{2,1,0:T(8,128)(2,1)} %param.9) | copy-start | bytes 196612
  0.7 6.1 %copy-start.2 = (bf16[4,128,576]{1,2,0:T(8,128)(2,1)S(1)}, bf16[4,128,576]{1,2,0:T(8,128)(2,1)}, u32[]{:S(2)}) copy-start(bf16[4,128,576]{1,2,0:T(8,128)(2,1)} %param.8) | copy-start | bytes 1769476
  0.7 6.1 %copy-start.3 = (s32[4,2048]{1,0:T(4,128)S(1)}, s32[4,2048]{1,0:T(4,128)}, u32[]{:S(2)}) copy-start(s32[4,2048]{1,0:T(4,128)} %selected_ref.1) | copy-start | bytes 98308
  0.7 30.0 %collective-permute-start.7 = (bf16[576,1024]{1,0:T(8,128)(2,1)}, bf16[576,1024]{1,0:T(8,128)(2,1)S(1)}, u32[]{:S(2)}, u32[]{:S(2)}) collective-permute-start(bf16[576,1024]{1,0:T(8,128)(2,1)} %bitcast.3), channel_id=1, source_target_pairs={{0,8},{4,12},{8,0},{12,4},{16,24},{20,28},{24,16},{28,20},{1,9},{5... | collective-permute-start | bytes 3538952 | tf_op jit(solution)/shard_map/ppermute | solution.py:298
  5.0 25.3 %collective-permute-start.9 = (bf16[576,512]{1,0:T(8,128)(2,1)S(1)}, bf16[576,512]{1,0:T(8,128)(2,1)S(1)}, u32[]{:S(2)}, u32[]{:S(2)}) collective-permute-start(bf16[576,512]{1,0:T(8,128)(2,1)S(1)} %get-tuple-element.33), channel_id=1, source_target_pairs={{0,1},{1,0},{2,3},{3,2},{4,5},{5,4},{6,7},{7,6},{8,9},{9,8},{10,11... | collective-permute-start | bytes 1769480 | tf_op jit(solution)/shard_map/ppermute | solution.py:298
  6.7 41.1 %copy-start = (bf16[1024,576]{0,1:T(8,128)(2,1)S(1)}, bf16[1024,576]{0,1:T(8,128)(2,1)}, u32[]{:S(2)}) copy-start(bf16[1024,576]{0,1:T(8,128)(2,1)} %param.6) | copy-start | bytes 3538948
  6.7 3.4 %collective-permute-start.2 = (bf16[4,80,128]{2,1,0:T(8,128)(2,1)S(1)}, bf16[4,80,128]{2,1,0:T(8,128)(2,1)S(1)}, u32[]{:S(2)}, u32[]{:S(2)}) collective-permute-start(bf16[4,80,128]{2,1,0:T(8,128)(2,1)S(1)} %pad_maximum_fusion.3), channel_id=1, source_target_pairs={{0,4},{4,0},{8,12},{12,8},{16,20},{20,16},{24,28},{28,24},{1,5},{5... | collective-permute-start | bytes 245768 | tf_op jit(solution)/shard_map/ppermute | solution.py:298
  7.5 40.9 %copy-start.1 = (bf16[4096,128]{1,0:T(8,128)(2,1)S(1)}, bf16[4096,128]{1,0:T(8,128)(2,1)}, u32[]{:S(2)}) copy-start(bf16[4096,128]{1,0:T(8,128)(2,1)} %keys_ref.1) | copy-start | bytes 3145732
  7.5 30.1 %collective-permute-start = (bf16[4,592,128]{2,1,0:T(8,128)(2,1)S(1)}, bf16[4,592,128]{2,1,0:T(8,128)(2,1)S(1)}, u32[]{:S(2)}, u32[]{:S(2)}) collective-permute-start(bf16[4,592,128]{2,1,0:T(8,128)(2,1)S(1)} %table.1.refs_0_), channel_id=1, source_target_pairs={{0,2},{1,3},{2,0},{3,1},{4,6},{5,7},{6,4},{7,5},{8,10},{9,11},{10,... | collective-permute-start | bytes 1818632 | tf_op jit(solution)/shard_map/ppermute | solution.py:298
  10.1 24.1 %collective-permute-start.3 = (bf16[8,80,128]{2,1,0:T(8,128)(2,1)S(1)}, bf16[8,80,128]{2,1,0:T(8,128)(2,1)S(1)}, u32[]{:S(2)}, u32[]{:S(2)}) collective-permute-start(bf16[8,80,128]{2,1,0:T(8,128)(2,1)S(1)} %pad_maximum_fusion.2), channel_id=1, source_target_pairs={{0,8},{4,12},{8,0},{12,4},{16,24},{20,28},{24,16},{28,20},{1,9},{5... | collective-permute-start | bytes 491528 | tf_op jit(solution)/shard_map/ppermute | solution.py:298
  10.7 37.6 %collective-permute-start.5 = (bf16[4,592,128]{2,1,0:T(8,128)(2,1)S(1)}, bf16[4,592,128]{2,1,0:T(8,128)(2,1)S(1)}, u32[]{:S(2)}, u32[]{:S(2)}) collective-permute-start(bf16[4,592,128]{2,1,0:T(8,128)(2,1)S(1)} %table.1.refs_0_), channel_id=1, source_target_pairs={{0,16},{4,20},{8,24},{12,28},{16,0},{20,4},{24,8},{28,12},{1,17},{... | collective-permute-start | bytes 1818632 | tf_op jit(solution)/shard_map/ppermute | solution.py:298
  30.3 16.4 %collective-permute-start.13 = (bf16[576,512]{1,0:T(8,128)(2,1)S(1)}, bf16[576,512]{1,0:T(8,128)(2,1)S(1)}, u32[]{:S(2)}, u32[]{:S(2)}) collective-permute-start(bf16[576,512]{1,0:T(8,128)(2,1)S(1)} %get-tuple-element.20), channel_id=1, source_target_pairs={{0,1},{1,0},{2,3},{3,2},{4,5},{5,4},{6,7},{7,6},{8,9},{9,8},{10,11... | collective-permute-start | bytes 1769480 | tf_op jit(solution)/shard_map/ppermute | solution.py:298
  30.7 16.0 %collective-permute-start.11 = (bf16[576,512]{1,0:T(8,128)(2,1)S(1)}, bf16[576,512]{1,0:T(8,128)(2,1)S(1)}, u32[]{:S(2)}, u32[]{:S(2)}) collective-permute-start(bf16[576,512]{1,0:T(8,128)(2,1)S(1)} %collective-permute-done.9.refs_5_), channel_id=1, source_target_pairs={{0,8},{4,12},{8,0},{12,4},{16,24},{20,28},{24,16},{28,20},{1,9},{5... | collective-permute-start | bytes 1769480 | tf_op jit(solution)/shard_map/ppermute | solution.py:298
  34.2 13.5 %collective-permute-start.4 = (bf16[16,80,128]{2,1,0:T(8,128)(2,1)S(1)}, bf16[16,80,128]{2,1,0:T(8,128)(2,1)S(1)}, u32[]{:S(2)}, u32[]{:S(2)}) collective-permute-start(bf16[16,80,128]{2,1,0:T(8,128)(2,1)S(1)} %pad_maximum_fusion.1), channel_id=1, source_target_pairs={{0,16},{4,20},{8,24},{12,28},{16,0},{20,4},{24,8},{28,12},{1,17},{... | collective-permute-start | bytes 983048 | tf_op jit(solution)/shard_map/ppermute | solution.py:298
  37.6 17.8 %collective-permute-start.1 = (bf16[4,592,128]{2,1,0:T(8,128)(2,1)S(1)}, bf16[4,592,128]{2,1,0:T(8,128)(2,1)S(1)}, u32[]{:S(2)}, u32[]{:S(2)}) collective-permute-start(bf16[4,592,128]{2,1,0:T(8,128)(2,1)S(1)} %collective-permute-done.refs_0_), channel_id=1, source_target_pairs={{0,16},{4,20},{8,24},{12,28},{16,0},{20,4},{24,8},{28,12},{1,17},{... | collective-permute-start | bytes 1818632 | tf_op jit(solution)/shard_map/ppermute | solution.py:298
  46.7 13.6 %collective-permute-start.15 = (bf16[576,512]{1,0:T(8,128)(2,1)S(1)}, bf16[576,512]{1,0:T(8,128)(2,1)S(1)}, u32[]{:S(2)}, u32[]{:S(2)}) collective-permute-start(bf16[576,512]{1,0:T(8,128)(2,1)S(1)} %collective-permute-done.13.refs_9_), channel_id=1, source_target_pairs={{0,8},{4,12},{8,0},{12,4},{16,24},{20,28},{24,16},{28,20},{1,9},{5... | collective-permute-start | bytes 1769480 | tf_op jit(solution)/shard_map/ppermute | solution.py:298
  47.7 13.1 %collective-permute-start.6 = (bf16[576,1024]{1,0:T(8,128)(2,1)S(1)}, bf16[576,1024]{1,0:T(8,128)(2,1)S(1)}, u32[]{:S(2)}, u32[]{:S(2)}) collective-permute-start(bf16[576,1024]{1,0:T(8,128)(2,1)S(1)} %bitcast.5), channel_id=1, source_target_pairs={{0,4},{4,0},{8,12},{12,8},{16,20},{20,16},{24,28},{28,24},{1,5},{5... | collective-permute-start | bytes 3538952 | tf_op jit(solution)/shard_map/ppermute | solution.py:298
  47.8 12.6 %collective-permute-start.10 = (bf16[576,512]{1,0:T(8,128)(2,1)S(1)}, bf16[576,512]{1,0:T(8,128)(2,1)S(1)}, u32[]{:S(2)}, u32[]{:S(2)}) collective-permute-start(bf16[576,512]{1,0:T(8,128)(2,1)S(1)} %collective-permute-done.9.refs_5_), channel_id=1, source_target_pairs={{0,4},{4,0},{8,12},{12,8},{16,20},{20,16},{24,28},{28,24},{1,5},{5... | collective-permute-start | bytes 1769480 | tf_op jit(solution)/shard_map/ppermute | solution.py:298
  48.3 14.1 %collective-permute-start.8 = (bf16[576,1024]{1,0:T(8,128)(2,1)S(1)}, bf16[576,1024]{1,0:T(8,128)(2,1)S(1)}, u32[]{:S(2)}, u32[]{:S(2)}) collective-permute-start(bf16[576,1024]{1,0:T(8,128)(2,1)S(1)} %collective-permute-done.7.refs_3_), channel_id=1, source_target_pairs={{0,4},{4,0},{8,12},{12,8},{16,20},{20,16},{24,28},{28,24},{1,5},{5... | collective-permute-start | bytes 3538952 | tf_op jit(solution)/shard_map/ppermute | solution.py:298
  55.3 5.5 %collective-permute-start.14 = (bf16[576,512]{1,0:T(8,128)(2,1)S(1)}, bf16[576,512]{1,0:T(8,128)(2,1)S(1)}, u32[]{:S(2)}, u32[]{:S(2)}) collective-permute-start(bf16[576,512]{1,0:T(8,128)(2,1)S(1)} %collective-permute-done.13.refs_9_), channel_id=1, source_target_pairs={{0,4},{4,0},{8,12},{12,8},{16,20},{20,16},{24,28},{28,24},{1,5},{5... | collective-permute-start | bytes 1769480 | tf_op jit(solution)/shard_map/ppermute | solution.py:298
  60.4 2.0 %collective-permute-start.12 = (bf16[576,512]{1,0:T(8,128)(2,1)S(1)}, bf16[576,512]{1,0:T(8,128)(2,1)S(1)}, u32[]{:S(2)}, u32[]{:S(2)}) collective-permute-start(bf16[576,512]{1,0:T(8,128)(2,1)S(1)} %collective-permute-done.11.refs_7_), channel_id=1, source_target_pairs={{0,4},{4,0},{8,12},{12,8},{16,20},{20,16},{24,28},{28,24},{1,5},{5... | collective-permute-start | bytes 1769480 | tf_op jit(solution)/shard_map/ppermute | solution.py:298
  60.4 2.8 %collective-permute-start.16 = (bf16[576,512]{1,0:T(8,128)(2,1)S(1)}, bf16[576,512]{1,0:T(8,128)(2,1)S(1)}, u32[]{:S(2)}, u32[]{:S(2)}) collective-permute-start(bf16[576,512]{1,0:T(8,128)(2,1)S(1)} %collective-permute-done.15.refs_11_), channel_id=1, source_target_pairs={{0,4},{4,0},{8,12},{12,8},{16,20},{20,16},{24,28},{28,24},{1,5},{5... | collective-permute-start | bytes 1769480 | tf_op jit(solution)/shard_map/ppermute | solution.py:298
  67.4 8.8 %collective-permute-start.18 = (bf16[272,512]{1,0:T(8,128)(2,1)S(1)}, bf16[272,512]{1,0:T(8,128)(2,1)S(1)}, u32[]{:S(2)}, u32[]{:S(2)}) collective-permute-start(bf16[272,512]{1,0:T(8,128)(2,1)S(1)} %get-tuple-element.24), channel_id=1, source_target_pairs={{0,16},{4,20},{8,24},{12,28},{16,0},{20,4},{24,8},{28,12},{1,17},{... | collective-permute-start | bytes 835592 | tf_op jit(solution)/shard_map/ppermute | solution.py:298
  76.4 14.8 %collective-permute-start.19 = (bf16[272,512]{1,0:T(8,128)(2,1)S(1)}, bf16[272,512]{1,0:T(8,128)(2,1)S(1)}, u32[]{:S(2)}, u32[]{:S(2)}) collective-permute-start(bf16[272,512]{1,0:T(8,128)(2,1)S(1)} %combine.3), channel_id=1, source_target_pairs={{0,2},{1,3},{2,0},{3,1},{4,6},{5,7},{6,4},{7,5},{8,10},{9,11},{10,... | collective-permute-start | bytes 835592 | tf_op jit(solution)/shard_map/ppermute | solution.py:298
  79.0 13.7 %collective-permute-start.17 = (bf16[272,512]{1,0:T(8,128)(2,1)S(1)}, bf16[272,512]{1,0:T(8,128)(2,1)S(1)}, u32[]{:S(2)}, u32[]{:S(2)}) collective-permute-start(bf16[272,512]{1,0:T(8,128)(2,1)S(1)} %get-tuple-element.23), channel_id=1, source_target_pairs={{0,16},{4,20},{8,24},{12,28},{16,0},{20,4},{24,8},{28,12},{1,17},{... | collective-permute-start | bytes 835592 | tf_op jit(solution)/shard_map/ppermute | solution.py:298
  91.2 13.1 %collective-permute-start.21 = (bf16[528,512]{1,0:T(8,128)(2,1)S(1)}, bf16[528,512]{1,0:T(8,128)(2,1)S(1)}, u32[]{:S(2)}, u32[]{:S(2)}) collective-permute-start(bf16[528,512]{1,0:T(8,128)(2,1)S(1)} %attend.6), channel_id=1, source_target_pairs={{0,16},{4,20},{8,24},{12,28},{16,0},{20,4},{24,8},{28,12},{1,17},{... | collective-permute-start | bytes 1622024 | tf_op jit(solution)/shard_map/ppermute | solution.py:298
  92.9 14.1 %collective-permute-start.20 = (bf16[272,512]{1,0:T(8,128)(2,1)S(1)}, bf16[272,512]{1,0:T(8,128)(2,1)S(1)}, u32[]{:S(2)}, u32[]{:S(2)}) collective-permute-start(bf16[272,512]{1,0:T(8,128)(2,1)S(1)} %combine.2), channel_id=1, source_target_pairs={{0,2},{1,3},{2,0},{3,1},{4,6},{5,7},{6,4},{7,5},{8,10},{9,11},{10,... | collective-permute-start | bytes 835592 | tf_op jit(solution)/shard_map/ppermute | solution.py:298

commit v5 on v4

--- a/solution.py
+++ b/solution.py
@@ -78,7 +78,7 @@
 
 
 def attend_kernel(places, blocks, per, width, sizes, masked, parts, *refs):
-    shards = len(places)
+    shards = 1 + max(array for array, *_ in places)
     packs, slabs = refs[:blocks], refs[blocks : blocks + shards]
     outs, keys, table = refs[blocks + shards : -2], refs[-2], refs[-1]
     some = per // parts
@@ -93,18 +93,18 @@
     base = (lane % RUN * RUN - 1).astype(jnp.float32)
     spread = lax.broadcasted_iota(jnp.int32, (RUN, span), 1).astype(jnp.float32)
     targets, begin = [], 0
-    for slab, (core, across, mask, offset) in zip(slabs, places):
+    for _, _, count, core, across, mask, offset in places:
         start = ((here ^ mask ^ core) * planes + (plane ^ across)) * (tokens // RUN) + offset // RUN
         row, shift = start // LANES, (LANES - start % LANES + begin) % LANES
         line = [table[i, pl.ds(row, 1), :] for i in range(rows)]
         line = pltpu.roll(jnp.concatenate(line + spare, axis=0), shift, 1)
         tile = line if begin % LANES == 0 else jnp.where(lane >= begin % LANES, line, tile)
-        begin += slab.shape[1] // RUN
+        begin += count // RUN
         if begin % LANES == 0:
             targets.append(jnp.transpose(jnp.where(tile > 0.0, base + tile, -1.0)))
     slot = 0
-    for slab in slabs:
-        for at in range(0, slab.shape[1], span):
+    for array, lanes, count, *_ in places:
+        for at in range(lanes, lanes + count, span):
             target = targets[slot // LANES][slot % LANES : slot % LANES + RUN, :]
             hits = [
                 (spread == target[:, i : i + 1]).astype(jnp.float32).astype(jnp.bfloat16)
@@ -112,7 +112,7 @@
             ]
             picked = lax.dot_general(
                 jnp.concatenate(hits, axis=0),
-                slab[:, at : at + span],
+                slabs[array][:, at : at + span],
                 (((1,), (1,)), ((), ())),
                 preferred_element_type=jnp.float32,
             ).astype(jnp.bfloat16)
@@ -158,7 +158,7 @@
 def attend(packs, slabs, places, width, sizes, masked, parts):
     blocks = len(packs)
     per, tall, heads = packs[0].shape
-    slots = sum(slab.shape[1] for slab in slabs) // RUN
+    slots = sum(count for _, _, count, *_ in places) // RUN
     out = VMEM((per // parts * heads + AUX, LATENT), jnp.bfloat16)
     return pl.pallas_call(
         functools.partial(attend_kernel, places, blocks, per, width, sizes, masked, parts),
@@ -232,7 +232,7 @@
     )(*near(parts), *more)
 
 
-def index_kernel(heads, per, meta_ref, keys_ref, out_ref, gate_scr):
+def index_kernel(heads, per, masks, meta_ref, keys_ref, out_ref, gate_scr):
     rows = meta_ref.shape[0]
     tokens = keys_ref.shape[0]
 
@@ -262,16 +262,16 @@
         group = jnp.where(
             here % 2 == 0, jnp.concatenate(ours + mates, axis=0), jnp.concatenate(mates + ours, axis=0)
         )
-        place = (here // 2) ^ (first // (2 * per))
+        place = (here ^ masks[first // (2 * per)]) // 2
         out_ref[pl.ds(pl.multiple_of(place * 2 * per, 2 * per), 2 * per), :] = group
 
 
-def index_block(meta, index_keys, heads, per):
+def index_block(meta, index_keys, heads, per, masks):
     rows, tall, size = meta.shape
     tokens = index_keys.shape[0]
     block = 512
     return pl.pallas_call(
-        functools.partial(index_kernel, heads, per),
+        functools.partial(index_kernel, heads, per, masks),
         grid=(tokens // block,),
         out_shape=jax.ShapeDtypeStruct((rows, tokens), jnp.float32),
         in_specs=[
@@ -314,11 +314,7 @@
             index_gates[:, None, :], ((0, 0), (0, AUX - 1), (0, LANES - index_gates.shape[1]))
         )
         meta = jnp.concatenate([index_query, gate_rows], axis=1)
-        bit = 1
-        while bit < columns:
-            other = swap(meta, "ctx", bit)
-            meta = jnp.concatenate([meta, other])
-            bit *= 2
+        meta = jnp.concatenate([meta, swap(meta, "ctx", 1)])
 
         packed = with_table(query, selected, all_runs // LANES)
         starts = {across: swap(packed, "row", across) if across else packed for across in row_planes}
@@ -326,15 +322,12 @@
             across: {mask: swap(start, "ctx", mask) if mask else start for mask in row_columns}
             for across, start in starts.items()
         }
-        near_queries = list(groups[0].values()) + list(starts.values())
         far_queries = [pack for group in groups.values() for pack in group.values()]
-        index_scores = index_block(after(meta, *near_queries), index_keys, index_query.shape[1], per)
-
-        half = tokens // 2
+        half, quarter = tokens // 2, tokens // 4
         pieces, sent, shown = [(0, 0, slab)], [], []
         for across in token_planes[1:]:
-            for offset in (0, half):
-                piece = slab[:, offset : offset + half]
+            for offset, count in ((0, half), (half, quarter)):
+                piece = slab[:, offset : offset + count]
                 sent.append(swap(after(piece, *sent[-1:]), "row", across))
                 pieces.append((across, offset, sent[-1]))
         slabs, places = [], []
@@ -347,17 +340,31 @@
                     shown.append(one)
                 for core in (0, 1):
                     if core and mask and offset:
-                        one = after(one, index_scores, *far_queries)
+                        one = after(one, *far_queries)
+                    places.append((len(slabs), 0, piece.shape[1], core, across, mask, offset))
                     slabs.append(swap(one, "ctx", 1) if core else one)
-                    places.append((core, across, mask, offset))
-
-        parts, last = [], [index_scores]
+        for across in token_planes[1:]:
+            first = half + quarter
+            both = [held[:, first:] for held in (slab, *shown[:1])]
+            both = swap(jnp.concatenate(both, axis=1), "row", across)
+            for core in (0, 1):
+                for i, mask in enumerate(token_columns):
+                    places.append((len(slabs), i * quarter, quarter, core, across, mask, first))
+                slabs.append(swap(both, "ctx", 1) if core else both)
+
+        masks = [0]
+        for bit in [1 << k for k in range(2, columns.bit_length() - 1)] + token_columns[1:]:
+            meta = after(meta, *(shown[-1:] if bit in token_columns else far_queries))
+            meta = jnp.concatenate([meta, swap(meta, "ctx", bit)])
+            masks += [mask ^ bit for mask in masks]
+
+        parts, last = [], []
         split = 2
         some = per // split
         for across in row_planes[1:] + row_planes[:1]:
             mine = []
             for mask in reversed(row_columns):
-                pack = after(groups[across][mask], *last)
+                pack = after(groups[across][mask], *last) if last else groups[across][mask]
                 sizes = (planes, tokens)
                 done = attend([pack], slabs, places, width, sizes, masked, split if across else 1)
                 last = list(done)
@@ -368,11 +375,12 @@
                 for i in range(split):
                     rows = range(i * some, (i + 1) * some)
                     mixed = combine([part[i] for part in mine], [rows[0]] * len(mine), rows, heads)
-                    back.append(swap(after(mixed, *back), "row", across))
-                    last = last + [mixed] if i == 0 else last
+                    back.append(swap(mixed, "row", across))
+                    last = last + [mixed, meta] if i == 0 else last
                 parts.append(back)
             else:
                 own = [part[0] for part in mine]
+        index_scores = index_block(after(meta, *last), index_keys, index_query.shape[1], per, masks)
         attended = None
         for i in range(split):
             rows = range(i * some, (i + 1) * some)

time: 108 us -> 105 us (0.972)
  waiting for transfers between devices: 54.1 us -> 52.2 us
  starting transfers between devices: 24.9 us -> 23.5 us
    ppermute x22 -> x24, waiting for transfers between devices: 54.1 us -> 52.2 us  [swap(): return lax.ppermute(array, axis, [(i, i ^ mask) for i in range(size)])]
    ppermute x22 -> x24, starting transfers between devices: 24.9 us -> 23.5 us  [swap(): return lax.ppermute(array, axis, [(i, i ^ mask) for i in range(size)])]
  transfers between devices with their start and end apart: 22 -> 24, of which waited for: 13 -> 12; matrix products, arithmetic and copies ran while one was open for 1% -> 1% of each run, Pallas kernels for 20% -> 25%
where the time goes in v5:
time: 105 us
  waiting for transfers between devices  52.2 us (50%)
  Pallas kernels  27 us (26%)
  starting transfers between devices  23.5 us (22%)
  local copies, waits for them, and re-layouts  1.32 us (1%)
    ppermute x24, waiting for transfers between devices, swap(): return lax.ppermute(array, axis, [(i, i ^ mask) for i in range(size)])  52.2 us
    ppermute x24, starting transfers between devices, swap(): return lax.ppermute(array, axis, [(i, i ^ mask) for i in range(size)])  23.5 us
    pallas_call x4, Pallas kernels, attend(): pl.pallas_call(functools.partial(attend_kernel, places, blocks, per, widt...  16.7 us
    pallas_call x1, Pallas kernels, index_block(): pl.pallas_call(functools.partial(index_kernel, heads, per, masks), grid=(...  6.87 us
    pallas_call x2, Pallas kernels, finish(): pl.pallas_call(functools.partial(combine_kernel, begins, rows, heads, Tru...  2.23 us
  transfers between devices with their start and end apart: 24, of which 12 were waited for; matrix products, arithmetic and copies ran while one was open for 1% of the time, Pallas kernels for 25%

profile of v5, /device:TPU:0, one launch (start us, length us, event | category | flops | bytes accessed | tf_op | source)
XLA Modules:
  0.0 104.9 jit_solution(3120902816259680531)
XLA Ops:
  0.7 3.0 %collective-permute-start.3 = (bf16[576,1024]{1,0:T(8,128)(2,1)}, bf16[576,1024]{1,0:T(8,128)(2,1)S(1)}, u32[]{:S(2)}, u32[]{:S(2)}) collective-permute-start(bf16[576,1024]{1,0:T(8,128)(2,1)} %bitcast.3), channel_id=1, source_target_pairs={{0,8},{4,12},{8,0},{12,4},{16,24},{20,28},{24,16},{28,20},{1,9},{5... | collective-permute-start | bytes 3538952 | tf_op jit(solution)/shard_map/ppermute | solution.py:298
  3.7 1.1 %slice.16 = bf16[576,512]{1,0:T(8,128)(2,1)S(1)} slice(bf16[576,1024]{1,0:T(8,128)(2,1)} %bitcast.4), slice={[0:576], [0:512]} | slice | bytes 1179648 | tf_op jit(solution)/shard_map/slice | solution.py:330
  4.8 1.6 %collective-permute-start.5 = (bf16[576,512]{1,0:T(8,128)(2,1)S(1)}, bf16[576,512]{1,0:T(8,128)(2,1)S(1)}, u32[]{:S(2)}, u32[]{:S(2)}) collective-permute-start(bf16[576,512]{1,0:T(8,128)(2,1)S(1)} %slice.16), channel_id=1, source_target_pairs={{0,1},{1,0},{2,3},{3,2},{4,5},{5,4},{6,7},{7,6},{8,9},{9,8},{10,11... | collective-permute-start | bytes 1769480 | tf_op jit(solution)/shard_map/ppermute | solution.py:298
  6.5 0.7 table.1.refs_0_
  7.1 2.6 %collective-permute-start = (bf16[4,592,128]{2,1,0:T(8,128)(2,1)S(1)}, bf16[4,592,128]{2,1,0:T(8,128)(2,1)S(1)}, u32[]{:S(2)}, u32[]{:S(2)}) collective-permute-start(bf16[4,592,128]{2,1,0:T(8,128)(2,1)S(1)} %table.1.refs_0_), channel_id=1, source_target_pairs={{0,2},{1,3},{2,0},{3,1},{4,6},{5,7},{6,4},{7,5},{8,10},{9,11},{10,... | collective-permute-start | bytes 1818632 | tf_op jit(solution)/shard_map/ppermute | solution.py:298
  9.7 1.5 %collective-permute-start.12 = (bf16[4,592,128]{2,1,0:T(8,128)(2,1)S(1)}, bf16[4,592,128]{2,1,0:T(8,128)(2,1)S(1)}, u32[]{:S(2)}, u32[]{:S(2)}) collective-permute-start(bf16[4,592,128]{2,1,0:T(8,128)(2,1)S(1)} %table.1.refs_0_), channel_id=1, source_target_pairs={{0,16},{4,20},{8,24},{12,28},{16,0},{20,4},{24,8},{28,12},{1,17},{... | collective-permute-start | bytes 1818632 | tf_op jit(solution)/shard_map/ppermute | solution.py:298
  11.3 20.2 %collective-permute-done.5.refs_5_ = bf16[576,512]{1,0:T(8,128)(2,1)S(1)} collective-permute-done((bf16[576,512]{1,0:T(8,128)(2,1)S(1)}, bf16[576,512]{1,0:T(8,128)(2,1)S(1)}, u32[]{:S(2)}, u32[]{:S(2)}) %collective-permute-start.5) | collective-permute-done | bytes 589856 | tf_op jit(solution)/shard_map/ppermute | solution.py:298
  31.5 0.5 collective-permute-start.7
  32.1 1.2 %collective-permute-start.9 = (bf16[576,256]{1,0:T(8,128)(2,1)S(1)}, bf16[576,256]{1,0:T(8,128)(2,1)S(1)}, u32[]{:S(2)}, u32[]{:S(2)}) collective-permute-start(bf16[576,256]{1,0:T(8,128)(2,1)S(1)} %get-tuple-element.18), channel_id=1, source_target_pairs={{0,1},{1,0},{2,3},{3,2},{4,5},{5,4},{6,7},{7,6},{8,9},{9,8},{10,11... | collective-permute-start | bytes 884744 | tf_op jit(solution)/shard_map/ppermute | solution.py:298
  33.3 2.8 %collective-permute-done.refs_0_ = bf16[4,592,128]{2,1,0:T(8,128)(2,1)S(1)} collective-permute-done((bf16[4,592,128]{2,1,0:T(8,128)(2,1)S(1)}, bf16[4,592,128]{2,1,0:T(8,128)(2,1)S(1)}, u32[]{:S(2)}, u32[]{:S(2)}) %collective-permute-start) | collective-permute-done | bytes 606240 | tf_op jit(solution)/shard_map/ppermute | solution.py:298
  36.0 1.5 %collective-permute-start.1 = (bf16[4,592,128]{2,1,0:T(8,128)(2,1)S(1)}, bf16[4,592,128]{2,1,0:T(8,128)(2,1)S(1)}, u32[]{:S(2)}, u32[]{:S(2)}) collective-permute-start(bf16[4,592,128]{2,1,0:T(8,128)(2,1)S(1)} %collective-permute-done.refs_0_), channel_id=1, source_target_pairs={{0,16},{4,20},{8,24},{12,28},{16,0},{20,4},{24,8},{28,12},{1,17},{... | collective-permute-start | bytes 1818632 | tf_op jit(solution)/shard_map/ppermute | solution.py:298
  37.6 0.1 collective-permute-start.19
  37.7 1.3 %collective-permute-done.19 = bf16[4,80,128]{2,1,0:T(8,128)(2,1)S(1)} collective-permute-done((bf16[4,80,128]{2,1,0:T(8,128)(2,1)S(1)}, bf16[4,80,128]{2,1,0:T(8,128)(2,1)S(1)}, u32[]{:S(2)}, u32[]{:S(2)}) %collective-permute-start.19) | collective-permute-done | bytes 81952 | tf_op jit(solution)/shard_map/ppermute | solution.py:298
  38.9 0.2 collective-permute-start.2
  39.2 1.9 %collective-permute-done.9.refs_9_ = bf16[576,256]{1,0:T(8,128)(2,1)S(1)} collective-permute-done((bf16[576,256]{1,0:T(8,128)(2,1)S(1)}, bf16[576,256]{1,0:T(8,128)(2,1)S(1)}, u32[]{:S(2)}, u32[]{:S(2)}) %collective-permute-start.9) | collective-permute-done | bytes 294944 | tf_op jit(solution)/shard_map/ppermute | solution.py:298
  41.1 0.0 collective-permute-start.10
  41.1 0.0 collective-permute-done.12.refs_0_
  41.1 0.0 collective-permute-start.14
  41.1 4.3 %collective-permute-done.7.refs_7_ = bf16[576,512]{1,0:T(8,128)(2,1)S(1)} collective-permute-done((bf16[576,512]{1,0:T(8,128)(2,1)S(1)}, bf16[576,512]{1,0:T(8,128)(2,1)S(1)}, u32[]{:S(2)}, u32[]{:S(2)}) %collective-permute-start.7) | collective-permute-done | bytes 589856 | tf_op jit(solution)/shard_map/ppermute | solution.py:298
  45.4 0.5 collective-permute-start.6
  45.9 1.4 %collective-permute-done.1.refs_0_ = bf16[4,592,128]{2,1,0:T(8,128)(2,1)S(1)} collective-permute-done((bf16[4,592,128]{2,1,0:T(8,128)(2,1)S(1)}, bf16[4,592,128]{2,1,0:T(8,128)(2,1)S(1)}, u32[]{:S(2)}, u32[]{:S(2)}) %collective-permute-start.1) | collective-permute-done | bytes 606240 | tf_op jit(solution)/shard_map/ppermute | solution.py:298
  47.3 0.5 collective-permute-start.11
  47.8 9.0 %collective-permute-done.14.refs_13_ = bf16[576,512]{1,0:T(8,128)(2,1)S(1)} collective-permute-done((bf16[576,512]{1,0:T(8,128)(2,1)S(1)}, bf16[576,512]{1,0:T(8,128)(2,1)S(1)}, u32[]{:S(2)}, u32[]{:S(2)}) %collective-permute-start.14) | collective-permute-done | bytes 589856 | tf_op jit(solution)/shard_map/ppermute | solution.py:298
  56.8 0.0 collective-permute-start.15
  56.8 0.5 collective-permute-start.8
  57.4 0.1 collective-permute-start.13
  57.5 1.4 %collective-permute-start.20 = (bf16[8,80,128]{2,1,0:T(8,128)(2,1)S(1)}, bf16[8,80,128]{2,1,0:T(8,128)(2,1)S(1)}, u32[]{:S(2)}, u32[]{:S(2)}) collective-permute-start(bf16[8,80,128]{2,1,0:T(8,128)(2,1)S(1)} %pad_maximum_fusion.2), channel_id=1, source_target_pairs={{0,16},{4,20},{8,24},{12,28},{16,0},{20,4},{24,8},{28,12},{1,17},{... | collective-permute-start | bytes 491528 | tf_op jit(solution)/shard_map/ppermute | solution.py:298
  58.9 1.2 %collective-permute-done.13.refs_12_ = bf16[576,256]{1,0:T(8,128)(2,1)S(1)} collective-permute-done((bf16[576,256]{1,0:T(8,128)(2,1)S(1)}, bf16[576,256]{1,0:T(8,128)(2,1)S(1)}, u32[]{:S(2)}, u32[]{:S(2)}) %collective-permute-start.13) | collective-permute-done | bytes 294944 | tf_op jit(solution)/shard_map/ppermute | solution.py:298
  60.1 4.1 %attend.4 = (bf16[272,512]{1,0:T(8,128)(2,1)S(1)}, bf16[272,512]{1,0:T(8,128)(2,1)S(1)}) custom-call(bf16[4,592,128]{2,1,0:T(8,128)(2,1)S(1)} %collective-permute-done.1.refs_0_, bf16[576,1024]{1,0:T(8,128)(2,1)S(1)} %bitcast.7, bf16[576,1024]{1,0:T(8,128)(2,1)S(1)} %collective-permute-done.2.refs_2_, bf16[576,1024]{1,0:T(8,128)(2,1)S(1)} %collective-permute-done.3.refs_3_, ...), custom_call_target="tpu_custom_call" | custom-call | flops 1000 | bytes 1000 | tf_op jit(solution)/shard_map/attend/pallas_call | solution.py:163
  64.3 1.4 %collective-permute-start.18 = (bf16[272,512]{1,0:T(8,128)(2,1)S(1)}, bf16[272,512]{1,0:T(8,128)(2,1)S(1)}, u32[]{:S(2)}, u32[]{:S(2)}) collective-permute-start(bf16[272,512]{1,0:T(8,128)(2,1)S(1)} %get-tuple-element.22), channel_id=1, source_target_pairs={{0,16},{4,20},{8,24},{12,28},{16,0},{20,4},{24,8},{28,12},{1,17},{... | collective-permute-start | bytes 835592 | tf_op jit(solution)/shard_map/ppermute | solution.py:298
  65.7 1.2 %collective-permute-start.21 = (bf16[16,80,128]{2,1,0:T(8,128)(2,1)S(1)}, bf16[16,80,128]{2,1,0:T(8,128)(2,1)S(1)}, u32[]{:S(2)}, u32[]{:S(2)}) collective-permute-start(bf16[16,80,128]{2,1,0:T(8,128)(2,1)S(1)} %pad_maximum_fusion.1), channel_id=1, source_target_pairs={{0,8},{4,12},{8,0},{12,4},{16,24},{20,28},{24,16},{28,20},{1,9},{5... | collective-permute-start | bytes 983048 | tf_op jit(solution)/shard_map/ppermute | solution.py:298
  66.9 4.1 %attend.5 = (bf16[272,512]{1,0:T(8,128)(2,1)S(1)}, bf16[272,512]{1,0:T(8,128)(2,1)S(1)}) custom-call(bf16[4,592,128]{2,1,0:T(8,128)(2,1)S(1)} %collective-permute-done.refs_0_, bf16[576,1024]{1,0:T(8,128)(2,1)S(1)} %bitcast.8, bf16[576,1024]{1,0:T(8,128)(2,1)S(1)} %collective-permute-done.2.refs_2_, bf16[576,1024]{1,0:T(8,128)(2,1)S(1)} %collective-permute-done.3.refs_3_, ...), custom_call_target="tpu_custom_call" | custom-call | flops 1000 | bytes 1000 | tf_op jit(solution)/shard_map/attend/pallas_call | solution.py:163
  71.1 2.0 %collective-permute-done.18.refs_0_ = bf16[272,512]{1,0:T(8,128)(2,1)S(1)} collective-permute-done((bf16[272,512]{1,0:T(8,128)(2,1)S(1)}, bf16[272,512]{1,0:T(8,128)(2,1)S(1)}, u32[]{:S(2)}, u32[]{:S(2)}) %collective-permute-start.18) | collective-permute-done | bytes 278560 | tf_op jit(solution)/shard_map/ppermute | solution.py:298
  73.0 0.3 combine.3
  73.3 2.5 %collective-permute-start.22 = (bf16[272,512]{1,0:T(8,128)(2,1)S(1)}, bf16[272,512]{1,0:T(8,128)(2,1)S(1)}, u32[]{:S(2)}, u32[]{:S(2)}) collective-permute-start(bf16[272,512]{1,0:T(8,128)(2,1)S(1)} %combine.3), channel_id=1, source_target_pairs={{0,2},{1,3},{2,0},{3,1},{4,6},{5,7},{6,4},{7,5},{8,10},{9,11},{10,... | collective-permute-start | bytes 835592 | tf_op jit(solution)/shard_map/ppermute | solution.py:298
  75.8 1.6 %collective-permute-start.16 = (bf16[272,512]{1,0:T(8,128)(2,1)S(1)}, bf16[272,512]{1,0:T(8,128)(2,1)S(1)}, u32[]{:S(2)}, u32[]{:S(2)}) collective-permute-start(bf16[272,512]{1,0:T(8,128)(2,1)S(1)} %get-tuple-element.21), channel_id=1, source_target_pairs={{0,16},{4,20},{8,24},{12,28},{16,0},{20,4},{24,8},{28,12},{1,17},{... | collective-permute-start | bytes 835592 | tf_op jit(solution)/shard_map/ppermute | solution.py:298
  77.5 4.3 %attend.6 = bf16[528,512]{1,0:T(8,128)(2,1)S(1)} custom-call(bf16[4,592,128]{2,1,0:T(8,128)(2,1)S(1)} %collective-permute-done.12.refs_0_, bf16[576,1024]{1,0:T(8,128)(2,1)S(1)} %bitcast.9, bf16[576,1024]{1,0:T(8,128)(2,1)S(1)} %collective-permute-done.2.refs_2_, bf16[576,1024]{1,0:T(8,128)(2,1)S(1)} %collective-permute-done.3.refs_3_, ...), custom_call_target="tpu_custom_call" | custom-call | flops 1000 | bytes 1000 | tf_op jit(solution)/shard_map/attend/pallas_call | solution.py:163
  81.8 6.3 %collective-permute-done.22.refs_0_ = bf16[272,512]{1,0:T(8,128)(2,1)S(1)} collective-permute-done((bf16[272,512]{1,0:T(8,128)(2,1)S(1)}, bf16[272,512]{1,0:T(8,128)(2,1)S(1)}, u32[]{:S(2)}, u32[]{:S(2)}) %collective-permute-start.22) | collective-permute-done | bytes 278560 | tf_op jit(solution)/shard_map/ppermute | solution.py:298
  88.1 1.4 %collective-permute-start.23 = (bf16[528,512]{1,0:T(8,128)(2,1)S(1)}, bf16[528,512]{1,0:T(8,128)(2,1)S(1)}, u32[]{:S(2)}, u32[]{:S(2)}) collective-permute-start(bf16[528,512]{1,0:T(8,128)(2,1)S(1)} %attend.6), channel_id=1, source_target_pairs={{0,16},{4,20},{8,24},{12,28},{16,0},{20,4},{24,8},{28,12},{1,17},{... | collective-permute-start | bytes 1622024 | tf_op jit(solution)/shard_map/ppermute | solution.py:298
  89.5 0.3 combine.2
  89.7 0.0 copy-start.1
  89.7 0.1 collective-permute-start.17
  89.8 4.1 %attend.7.refs_2_ = bf16[528,512]{1,0:T(8,128)(2,1)S(1)} custom-call(bf16[4,592,128]{2,1,0:T(8,128)(2,1)S(1)} %table.1.refs_0_, bf16[576,1024]{1,0:T(8,128)(2,1)S(1)} %bitcast.10, bf16[576,1024]{1,0:T(8,128)(2,1)S(1)} %collective-permute-done.2.refs_2_, bf16[576,1024]{1,0:T(8,128)(2,1)S(1)} %collective-permute-done.3.refs_3_, ...), custom_call_target="tpu_custom_call" | custom-call | flops 1000 | bytes 1000 | tf_op jit(solution)/shard_map/attend/pallas_call | solution.py:163
  94.0 6.9 %index.1 = f32[32,4096]{1,0:T(8,128)} custom-call(bf16[32,80,128]{2,1,0:T(8,128)(2,1)S(1)} %constant_dynamic-update-slice_fusion.meta_ref, bf16[4096,128]{1,0:T(8,128)(2,1)S(1)} %copy-done.1), custom_call_target="tpu_custom_call" | custom-call | flops 1000 | bytes 1000 | tf_op jit(solution)/shard_map/index/pallas_call | solution.py:273
  100.8 0.4 collective-permute-done.23.refs_1_
  101.2 1.1 %finish.2.refs_3_ = bf16[4,128,512]{2,1,0:T(8,128)(2,1)} custom-call(bf16[272,512]{1,0:T(8,128)(2,1)S(1)} %collective-permute-done.22.refs_0_, bf16[528,512]{1,0:T(8,128)(2,1)S(1)} %collective-permute-done.23.refs_1_, bf16[528,512]{1,0:T(8,128)(2,1)S(1)} %attend.7.refs_2_), custom_call_target="tpu_custom_call" | custom-call | flops 1000 | bytes 60000000 | tf_op jit(solution)/shard_map/finish/pallas_call | solution.py:222
  102.3 1.4 %collective-permute-done.17.refs_0_ = bf16[272,512]{1,0:T(8,128)(2,1)S(1)} collective-permute-done((bf16[272,512]{1,0:T(8,128)(2,1)S(1)}, bf16[272,512]{1,0:T(8,128)(2,1)S(1)}, u32[]{:S(2)}, u32[]{:S(2)}) %collective-permute-start.17) | collective-permute-done | bytes 278560 | tf_op jit(solution)/shard_map/ppermute | solution.py:298
  103.7 1.1 %finish.3 = bf16[4,128,512]{2,1,0:T(8,128)(2,1)} custom-call(bf16[272,512]{1,0:T(8,128)(2,1)S(1)} %collective-permute-done.17.refs_0_, bf16[528,512]{1,0:T(8,128)(2,1)S(1)} %collective-permute-done.23.refs_1_, bf16[528,512]{1,0:T(8,128)(2,1)S(1)} %attend.7.refs_2_, bf16[4,128,512]{2,1,0:T(8,128)(2,1)} %finish.2.refs_3_), custom_call_target="tpu_custom_call", output_to_operand_aliasing={{}: (3, {})} | custom-call | flops 1000 | bytes 1000 | tf_op jit(solution)/shard_map/finish/pallas_call | solution.py:222
  (33 shorter events, 0.3 us)
Async XLA Ops:
  0.6 5.8 %copy-start.3 = (s32[4,2048]{1,0:T(4,128)S(1)}, s32[4,2048]{1,0:T(4,128)}, u32[]{:S(2)}) copy-start(s32[4,2048]{1,0:T(4,128)} %selected_ref.1) | copy-start | bytes 98308
  0.6 5.8 %copy-start.2 = (bf16[4,128,576]{1,2,0:T(8,128)(2,1)S(1)}, bf16[4,128,576]{1,2,0:T(8,128)(2,1)}, u32[]{:S(2)}) copy-start(bf16[4,128,576]{1,2,0:T(8,128)(2,1)} %param.8) | copy-start | bytes 1769476
  0.7 10.6 %copy-start.5 = (bf16[4,64]{1,0:T(4,128)(2,1)S(1)}, bf16[4,64]{1,0:T(4,128)(2,1)}, u32[]{:S(2)}) copy-start(bf16[4,64]{1,0:T(4,128)(2,1)} %param.10) | copy-start | bytes 1540
  0.7 31.4 %copy-start = (bf16[1024,576]{0,1:T(8,128)(2,1)S(1)}, bf16[1024,576]{0,1:T(8,128)(2,1)}, u32[]{:S(2)}) copy-start(bf16[1024,576]{0,1:T(8,128)(2,1)} %param.6) | copy-start | bytes 3538948
  0.7 30.8 %collective-permute-start.3 = (bf16[576,1024]{1,0:T(8,128)(2,1)}, bf16[576,1024]{1,0:T(8,128)(2,1)S(1)}, u32[]{:S(2)}, u32[]{:S(2)}) collective-permute-start(bf16[576,1024]{1,0:T(8,128)(2,1)} %bitcast.3), channel_id=1, source_target_pairs={{0,8},{4,12},{8,0},{12,4},{16,24},{20,28},{24,16},{28,20},{1,9},{5... | collective-permute-start | bytes 3538952 | tf_op jit(solution)/shard_map/ppermute | solution.py:298
  4.8 26.7 %collective-permute-start.5 = (bf16[576,512]{1,0:T(8,128)(2,1)S(1)}, bf16[576,512]{1,0:T(8,128)(2,1)S(1)}, u32[]{:S(2)}, u32[]{:S(2)}) collective-permute-start(bf16[576,512]{1,0:T(8,128)(2,1)S(1)} %slice.16), channel_id=1, source_target_pairs={{0,1},{1,0},{2,3},{3,2},{4,5},{5,4},{6,7},{7,6},{8,9},{9,8},{10,11... | collective-permute-start | bytes 1769480 | tf_op jit(solution)/shard_map/ppermute | solution.py:298
  6.5 31.1 %copy-start.4 = (bf16[4,64,128]{2,1,0:T(8,128)(2,1)S(1)}, bf16[4,64,128]{2,1,0:T(8,128)(2,1)}, u32[]{:S(2)}) copy-start(bf16[4,64,128]{2,1,0:T(8,128)(2,1)} %param.9) | copy-start | bytes 196612
  7.1 28.9 %collective-permute-start = (bf16[4,592,128]{2,1,0:T(8,128)(2,1)S(1)}, bf16[4,592,128]{2,1,0:T(8,128)(2,1)S(1)}, u32[]{:S(2)}, u32[]{:S(2)}) collective-permute-start(bf16[4,592,128]{2,1,0:T(8,128)(2,1)S(1)} %table.1.refs_0_), channel_id=1, source_target_pairs={{0,2},{1,3},{2,0},{3,1},{4,6},{5,7},{6,4},{7,5},{8,10},{9,11},{10,... | collective-permute-start | bytes 1818632 | tf_op jit(solution)/shard_map/ppermute | solution.py:298
  9.7 31.4 %collective-permute-start.12 = (bf16[4,592,128]{2,1,0:T(8,128)(2,1)S(1)}, bf16[4,592,128]{2,1,0:T(8,128)(2,1)S(1)}, u32[]{:S(2)}, u32[]{:S(2)}) collective-permute-start(bf16[4,592,128]{2,1,0:T(8,128)(2,1)S(1)} %table.1.refs_0_), channel_id=1, source_target_pairs={{0,16},{4,20},{8,24},{12,28},{16,0},{20,4},{24,8},{28,12},{1,17},{... | collective-permute-start | bytes 1818632 | tf_op jit(solution)/shard_map/ppermute | solution.py:298
  31.5 13.9 %collective-permute-start.7 = (bf16[576,512]{1,0:T(8,128)(2,1)S(1)}, bf16[576,512]{1,0:T(8,128)(2,1)S(1)}, u32[]{:S(2)}, u32[]{:S(2)}) collective-permute-start(bf16[576,512]{1,0:T(8,128)(2,1)S(1)} %collective-permute-done.5.refs_5_), channel_id=1, source_target_pairs={{0,8},{4,12},{8,0},{12,4},{16,24},{20,28},{24,16},{28,20},{1,9},{5... | collective-permute-start | bytes 1769480 | tf_op jit(solution)/shard_map/ppermute | solution.py:298
  32.1 9.0 %collective-permute-start.9 = (bf16[576,256]{1,0:T(8,128)(2,1)S(1)}, bf16[576,256]{1,0:T(8,128)(2,1)S(1)}, u32[]{:S(2)}, u32[]{:S(2)}) collective-permute-start(bf16[576,256]{1,0:T(8,128)(2,1)S(1)} %get-tuple-element.18), channel_id=1, source_target_pairs={{0,1},{1,0},{2,3},{3,2},{4,5},{5,4},{6,7},{7,6},{8,9},{9,8},{10,11... | collective-permute-start | bytes 884744 | tf_op jit(solution)/shard_map/ppermute | solution.py:298
  36.0 11.2 %collective-permute-start.1 = (bf16[4,592,128]{2,1,0:T(8,128)(2,1)S(1)}, bf16[4,592,128]{2,1,0:T(8,128)(2,1)S(1)}, u32[]{:S(2)}, u32[]{:S(2)}) collective-permute-start(bf16[4,592,128]{2,1,0:T(8,128)(2,1)S(1)} %collective-permute-done.refs_0_), channel_id=1, source_target_pairs={{0,16},{4,20},{8,24},{12,28},{16,0},{20,4},{24,8},{28,12},{1,17},{... | collective-permute-start | bytes 1818632 | tf_op jit(solution)/shard_map/ppermute | solution.py:298
  37.6 1.3 %collective-permute-start.19 = (bf16[4,80,128]{2,1,0:T(8,128)(2,1)S(1)}, bf16[4,80,128]{2,1,0:T(8,128)(2,1)S(1)}, u32[]{:S(2)}, u32[]{:S(2)}) collective-permute-start(bf16[4,80,128]{2,1,0:T(8,128)(2,1)S(1)} %pad_maximum_fusion.3), channel_id=1, source_target_pairs={{0,4},{4,0},{8,12},{12,8},{16,20},{20,16},{24,28},{28,24},{1,5},{5... | collective-permute-start | bytes 245768 | tf_op jit(solution)/shard_map/ppermute | solution.py:298
  38.9 18.5 %collective-permute-start.2 = (bf16[576,1024]{1,0:T(8,128)(2,1)S(1)}, bf16[576,1024]{1,0:T(8,128)(2,1)S(1)}, u32[]{:S(2)}, u32[]{:S(2)}) collective-permute-start(bf16[576,1024]{1,0:T(8,128)(2,1)S(1)} %bitcast.6), channel_id=1, source_target_pairs={{0,4},{4,0},{8,12},{12,8},{16,20},{20,16},{24,28},{28,24},{1,5},{5... | collective-permute-start | bytes 3538952 | tf_op jit(solution)/shard_map/ppermute | solution.py:298
  41.1 4.3 %collective-permute-start.10 = (bf16[576,256]{1,0:T(8,128)(2,1)S(1)}, bf16[576,256]{1,0:T(8,128)(2,1)S(1)}, u32[]{:S(2)}, u32[]{:S(2)}) collective-permute-start(bf16[576,256]{1,0:T(8,128)(2,1)S(1)} %collective-permute-done.9.refs_9_), channel_id=1, source_target_pairs={{0,4},{4,0},{8,12},{12,8},{16,20},{20,16},{24,28},{28,24},{1,5},{5... | collective-permute-start | bytes 884744 | tf_op jit(solution)/shard_map/ppermute | solution.py:298
  41.1 15.7 %collective-permute-start.14 = (bf16[576,512]{1,0:T(8,128)(2,1)S(1)}, bf16[576,512]{1,0:T(8,128)(2,1)S(1)}, u32[]{:S(2)}, u32[]{:S(2)}) collective-permute-start(bf16[576,512]{1,0:T(8,128)(2,1)S(1)} %pad_maximum_fusion), channel_id=1, source_target_pairs={{0,1},{1,0},{2,3},{3,2},{4,5},{5,4},{6,7},{7,6},{8,9},{9,8},{10,11... | collective-permute-start | bytes 1769480 | tf_op jit(solution)/shard_map/ppermute | solution.py:298
  45.4 14.7 %collective-permute-start.4 = (bf16[576,1024]{1,0:T(8,128)(2,1)S(1)}, bf16[576,1024]{1,0:T(8,128)(2,1)S(1)}, u32[]{:S(2)}, u32[]{:S(2)}) collective-permute-start(bf16[576,1024]{1,0:T(8,128)(2,1)S(1)} %collective-permute-done.3.refs_3_), channel_id=1, source_target_pairs={{0,4},{4,0},{8,12},{12,8},{16,20},{20,16},{24,28},{28,24},{1,5},{5... | collective-permute-start | bytes 3538952 | tf_op jit(solution)/shard_map/ppermute | solution.py:298
  45.4 12.0 %collective-permute-start.6 = (bf16[576,512]{1,0:T(8,128)(2,1)S(1)}, bf16[576,512]{1,0:T(8,128)(2,1)S(1)}, u32[]{:S(2)}, u32[]{:S(2)}) collective-permute-start(bf16[576,512]{1,0:T(8,128)(2,1)S(1)} %collective-permute-done.5.refs_5_), channel_id=1, source_target_pairs={{0,4},{4,0},{8,12},{12,8},{16,20},{20,16},{24,28},{28,24},{1,5},{5... | collective-permute-start | bytes 1769480 | tf_op jit(solution)/shard_map/ppermute | solution.py:298
  47.3 9.6 %collective-permute-start.11 = (bf16[576,256]{1,0:T(8,128)(2,1)S(1)}, bf16[576,256]{1,0:T(8,128)(2,1)S(1)}, u32[]{:S(2)}, u32[]{:S(2)}) collective-permute-start(bf16[576,256]{1,0:T(8,128)(2,1)S(1)} %collective-permute-done.9.refs_9_), channel_id=1, source_target_pairs={{0,8},{4,12},{8,0},{12,4},{16,24},{20,28},{24,16},{28,20},{1,9},{5... | collective-permute-start | bytes 884744 | tf_op jit(solution)/shard_map/ppermute | solution.py:298
  56.8 3.3 %collective-permute-start.15 = (bf16[576,512]{1,0:T(8,128)(2,1)S(1)}, bf16[576,512]{1,0:T(8,128)(2,1)S(1)}, u32[]{:S(2)}, u32[]{:S(2)}) collective-permute-start(bf16[576,512]{1,0:T(8,128)(2,1)S(1)} %collective-permute-done.14.refs_13_), channel_id=1, source_target_pairs={{0,4},{4,0},{8,12},{12,8},{16,20},{20,16},{24,28},{28,24},{1,5},{5... | collective-permute-start | bytes 1769480 | tf_op jit(solution)/shard_map/ppermute | solution.py:298
  56.8 3.3 %collective-permute-start.8 = (bf16[576,512]{1,0:T(8,128)(2,1)S(1)}, bf16[576,512]{1,0:T(8,128)(2,1)S(1)}, u32[]{:S(2)}, u32[]{:S(2)}) collective-permute-start(bf16[576,512]{1,0:T(8,128)(2,1)S(1)} %collective-permute-done.7.refs_7_), channel_id=1, source_target_pairs={{0,4},{4,0},{8,12},{12,8},{16,20},{20,16},{24,28},{28,24},{1,5},{5... | collective-permute-start | bytes 1769480 | tf_op jit(solution)/shard_map/ppermute | solution.py:298
  57.4 2.8 %collective-permute-start.13 = (bf16[576,256]{1,0:T(8,128)(2,1)S(1)}, bf16[576,256]{1,0:T(8,128)(2,1)S(1)}, u32[]{:S(2)}, u32[]{:S(2)}) collective-permute-start(bf16[576,256]{1,0:T(8,128)(2,1)S(1)} %collective-permute-done.11.refs_11_), channel_id=1, source_target_pairs={{0,4},{4,0},{8,12},{12,8},{16,20},{20,16},{24,28},{28,24},{1,5},{5... | collective-permute-start | bytes 884744 | tf_op jit(solution)/shard_map/ppermute | solution.py:298
  57.5 8.2 %collective-permute-start.20 = (bf16[8,80,128]{2,1,0:T(8,128)(2,1)S(1)}, bf16[8,80,128]{2,1,0:T(8,128)(2,1)S(1)}, u32[]{:S(2)}, u32[]{:S(2)}) collective-permute-start(bf16[8,80,128]{2,1,0:T(8,128)(2,1)S(1)} %pad_maximum_fusion.2), channel_id=1, source_target_pairs={{0,16},{4,20},{8,24},{12,28},{16,0},{20,4},{24,8},{28,12},{1,17},{... | collective-permute-start | bytes 491528 | tf_op jit(solution)/shard_map/ppermute | solution.py:298
  64.3 8.8 %collective-permute-start.18 = (bf16[272,512]{1,0:T(8,128)(2,1)S(1)}, bf16[272,512]{1,0:T(8,128)(2,1)S(1)}, u32[]{:S(2)}, u32[]{:S(2)}) collective-permute-start(bf16[272,512]{1,0:T(8,128)(2,1)S(1)} %get-tuple-element.22), channel_id=1, source_target_pairs={{0,16},{4,20},{8,24},{12,28},{16,0},{20,4},{24,8},{28,12},{1,17},{... | collective-permute-start | bytes 835592 | tf_op jit(solution)/shard_map/ppermute | solution.py:298
  65.7 11.7 %collective-permute-start.21 = (bf16[16,80,128]{2,1,0:T(8,128)(2,1)S(1)}, bf16[16,80,128]{2,1,0:T(8,128)(2,1)S(1)}, u32[]{:S(2)}, u32[]{:S(2)}) collective-permute-start(bf16[16,80,128]{2,1,0:T(8,128)(2,1)S(1)} %pad_maximum_fusion.1), channel_id=1, source_target_pairs={{0,8},{4,12},{8,0},{12,4},{16,24},{20,28},{24,16},{28,20},{1,9},{5... | collective-permute-start | bytes 983048 | tf_op jit(solution)/shard_map/ppermute | solution.py:298
  73.3 14.8 %collective-permute-start.22 = (bf16[272,512]{1,0:T(8,128)(2,1)S(1)}, bf16[272,512]{1,0:T(8,128)(2,1)S(1)}, u32[]{:S(2)}, u32[]{:S(2)}) collective-permute-start(bf16[272,512]{1,0:T(8,128)(2,1)S(1)} %combine.3), channel_id=1, source_target_pairs={{0,2},{1,3},{2,0},{3,1},{4,6},{5,7},{6,4},{7,5},{8,10},{9,11},{10,... | collective-permute-start | bytes 835592 | tf_op jit(solution)/shard_map/ppermute | solution.py:298
  75.8 13.6 %collective-permute-start.16 = (bf16[272,512]{1,0:T(8,128)(2,1)S(1)}, bf16[272,512]{1,0:T(8,128)(2,1)S(1)}, u32[]{:S(2)}, u32[]{:S(2)}) collective-permute-start(bf16[272,512]{1,0:T(8,128)(2,1)S(1)} %get-tuple-element.21), channel_id=1, source_target_pairs={{0,16},{4,20},{8,24},{12,28},{16,0},{20,4},{24,8},{28,12},{1,17},{... | collective-permute-start | bytes 835592 | tf_op jit(solution)/shard_map/ppermute | solution.py:298
  88.1 13.1 %collective-permute-start.23 = (bf16[528,512]{1,0:T(8,128)(2,1)S(1)}, bf16[528,512]{1,0:T(8,128)(2,1)S(1)}, u32[]{:S(2)}, u32[]{:S(2)}) collective-permute-start(bf16[528,512]{1,0:T(8,128)(2,1)S(1)} %attend.6), channel_id=1, source_target_pairs={{0,16},{4,20},{8,24},{12,28},{16,0},{20,4},{24,8},{28,12},{1,17},{... | collective-permute-start | bytes 1622024 | tf_op jit(solution)/shard_map/ppermute | solution.py:298
  89.7 4.2 %copy-start.1 = (bf16[4096,128]{1,0:T(8,128)(2,1)S(1)}, bf16[4096,128]{1,0:T(8,128)(2,1)}, u32[]{:S(2)}) copy-start(bf16[4096,128]{1,0:T(8,128)(2,1)} %keys_ref.1) | copy-start | bytes 3145732
  89.7 14.0 %collective-permute-start.17 = (bf16[272,512]{1,0:T(8,128)(2,1)S(1)}, bf16[272,512]{1,0:T(8,128)(2,1)S(1)}, u32[]{:S(2)}, u32[]{:S(2)}) collective-permute-start(bf16[272,512]{1,0:T(8,128)(2,1)S(1)} %combine.2), channel_id=1, source_target_pairs={{0,2},{1,3},{2,0},{3,1},{4,6},{5,7},{6,4},{7,5},{8,10},{9,11},{10,... | collective-permute-start | bytes 835592 | tf_op jit(solution)/shard_map/ppermute | solution.py:298

commit v6 on v5

--- a/solution.py
+++ b/solution.py
@@ -240,7 +240,7 @@
     def _():
         for first in range(0, rows, 8):
             lines = jnp.concatenate(
-                [meta_ref[first + i, heads : heads + 8, :].astype(jnp.float32)[:1] for i in range(8)],
+                [meta_ref[first + i, heads : heads + AUX, :].astype(jnp.float32)[:1] for i in range(8)],
                 axis=0,
             )
             turned = jnp.transpose(lines)

time: 105 us -> 105 us (level)
  no operation moved by 1% of the time
where the time goes in v6:
time: 105 us
  waiting for transfers between devices  52.2 us (50%)
  Pallas kernels  27 us (26%)
  starting transfers between devices  23.5 us (22%)
  local copies, waits for them, and re-layouts  1.32 us (1%)
    ppermute x24, waiting for transfers between devices, swap(): return lax.ppermute(array, axis, [(i, i ^ mask) for i in range(size)])  52.2 us
    ppermute x24, starting transfers between devices, swap(): return lax.ppermute(array, axis, [(i, i ^ mask) for i in range(size)])  23.5 us
    pallas_call x4, Pallas kernels, attend(): pl.pallas_call(functools.partial(attend_kernel, places, blocks, per, widt...  16.7 us
    pallas_call x1, Pallas kernels, index_block(): pl.pallas_call(functools.partial(index_kernel, heads, per, masks), grid=(...  6.87 us
    pallas_call x2, Pallas kernels, finish(): pl.pallas_call(functools.partial(combine_kernel, begins, rows, heads, Tru...  2.23 us
  transfers between devices with their start and end apart: 24, of which 12 were waited for; matrix products, arithmetic and copies ran while one was open for 1% of the time, Pallas kernels for 25%

profile of v6, /device:TPU:0, one launch (start us, length us, event | category | flops | bytes accessed | tf_op | source)
XLA Modules:
  0.0 104.9 jit_solution(3120902816259680531)
XLA Ops:
  0.7 3.0 %collective-permute-start.3 = (bf16[576,1024]{1,0:T(8,128)(2,1)}, bf16[576,1024]{1,0:T(8,128)(2,1)S(1)}, u32[]{:S(2)}, u32[]{:S(2)}) collective-permute-start(bf16[576,1024]{1,0:T(8,128)(2,1)} %bitcast.3), channel_id=1, source_target_pairs={{0,8},{4,12},{8,0},{12,4},{16,24},{20,28},{24,16},{28,20},{1,9},{5... | collective-permute-start | bytes 3538952 | tf_op jit(solution)/shard_map/ppermute | solution.py:298
  3.7 1.1 %slice.16 = bf16[576,512]{1,0:T(8,128)(2,1)S(1)} slice(bf16[576,1024]{1,0:T(8,128)(2,1)} %bitcast.4), slice={[0:576], [0:512]} | slice | bytes 1179648 | tf_op jit(solution)/shard_map/slice | solution.py:330
  4.8 1.6 %collective-permute-start.5 = (bf16[576,512]{1,0:T(8,128)(2,1)S(1)}, bf16[576,512]{1,0:T(8,128)(2,1)S(1)}, u32[]{:S(2)}, u32[]{:S(2)}) collective-permute-start(bf16[576,512]{1,0:T(8,128)(2,1)S(1)} %slice.16), channel_id=1, source_target_pairs={{0,1},{1,0},{2,3},{3,2},{4,5},{5,4},{6,7},{7,6},{8,9},{9,8},{10,11... | collective-permute-start | bytes 1769480 | tf_op jit(solution)/shard_map/ppermute | solution.py:298
  6.5 0.7 table.1.refs_0_
  7.1 2.6 %collective-permute-start = (bf16[4,592,128]{2,1,0:T(8,128)(2,1)S(1)}, bf16[4,592,128]{2,1,0:T(8,128)(2,1)S(1)}, u32[]{:S(2)}, u32[]{:S(2)}) collective-permute-start(bf16[4,592,128]{2,1,0:T(8,128)(2,1)S(1)} %table.1.refs_0_), channel_id=1, source_target_pairs={{0,2},{1,3},{2,0},{3,1},{4,6},{5,7},{6,4},{7,5},{8,10},{9,11},{10,... | collective-permute-start | bytes 1818632 | tf_op jit(solution)/shard_map/ppermute | solution.py:298
  9.7 1.5 %collective-permute-start.12 = (bf16[4,592,128]{2,1,0:T(8,128)(2,1)S(1)}, bf16[4,592,128]{2,1,0:T(8,128)(2,1)S(1)}, u32[]{:S(2)}, u32[]{:S(2)}) collective-permute-start(bf16[4,592,128]{2,1,0:T(8,128)(2,1)S(1)} %table.1.refs_0_), channel_id=1, source_target_pairs={{0,16},{4,20},{8,24},{12,28},{16,0},{20,4},{24,8},{28,12},{1,17},{... | collective-permute-start | bytes 1818632 | tf_op jit(solution)/shard_map/ppermute | solution.py:298
  11.3 20.2 %collective-permute-done.5.refs_5_ = bf16[576,512]{1,0:T(8,128)(2,1)S(1)} collective-permute-done((bf16[576,512]{1,0:T(8,128)(2,1)S(1)}, bf16[576,512]{1,0:T(8,128)(2,1)S(1)}, u32[]{:S(2)}, u32[]{:S(2)}) %collective-permute-start.5) | collective-permute-done | bytes 589856 | tf_op jit(solution)/shard_map/ppermute | solution.py:298
  31.5 0.5 collective-permute-start.7
  32.1 1.2 %collective-permute-start.9 = (bf16[576,256]{1,0:T(8,128)(2,1)S(1)}, bf16[576,256]{1,0:T(8,128)(2,1)S(1)}, u32[]{:S(2)}, u32[]{:S(2)}) collective-permute-start(bf16[576,256]{1,0:T(8,128)(2,1)S(1)} %get-tuple-element.18), channel_id=1, source_target_pairs={{0,1},{1,0},{2,3},{3,2},{4,5},{5,4},{6,7},{7,6},{8,9},{9,8},{10,11... | collective-permute-start | bytes 884744 | tf_op jit(solution)/shard_map/ppermute | solution.py:298
  33.3 2.8 %collective-permute-done.refs_0_ = bf16[4,592,128]{2,1,0:T(8,128)(2,1)S(1)} collective-permute-done((bf16[4,592,128]{2,1,0:T(8,128)(2,1)S(1)}, bf16[4,592,128]{2,1,0:T(8,128)(2,1)S(1)}, u32[]{:S(2)}, u32[]{:S(2)}) %collective-permute-start) | collective-permute-done | bytes 606240 | tf_op jit(solution)/shard_map/ppermute | solution.py:298
  36.0 1.5 %collective-permute-start.1 = (bf16[4,592,128]{2,1,0:T(8,128)(2,1)S(1)}, bf16[4,592,128]{2,1,0:T(8,128)(2,1)S(1)}, u32[]{:S(2)}, u32[]{:S(2)}) collective-permute-start(bf16[4,592,128]{2,1,0:T(8,128)(2,1)S(1)} %collective-permute-done.refs_0_), channel_id=1, source_target_pairs={{0,16},{4,20},{8,24},{12,28},{16,0},{20,4},{24,8},{28,12},{1,17},{... | collective-permute-start | bytes 1818632 | tf_op jit(solution)/shard_map/ppermute | solution.py:298
  37.6 0.1 collective-permute-start.19
  37.7 1.3 %collective-permute-done.19 = bf16[4,80,128]{2,1,0:T(8,128)(2,1)S(1)} collective-permute-done((bf16[4,80,128]{2,1,0:T(8,128)(2,1)S(1)}, bf16[4,80,128]{2,1,0:T(8,128)(2,1)S(1)}, u32[]{:S(2)}, u32[]{:S(2)}) %collective-permute-start.19) | collective-permute-done | bytes 81952 | tf_op jit(solution)/shard_map/ppermute | solution.py:298
  38.9 0.2 collective-permute-start.2
  39.2 1.9 %collective-permute-done.9.refs_9_ = bf16[576,256]{1,0:T(8,128)(2,1)S(1)} collective-permute-done((bf16[576,256]{1,0:T(8,128)(2,1)S(1)}, bf16[576,256]{1,0:T(8,128)(2,1)S(1)}, u32[]{:S(2)}, u32[]{:S(2)}) %collective-permute-start.9) | collective-permute-done | bytes 294944 | tf_op jit(solution)/shard_map/ppermute | solution.py:298
  41.1 0.0 collective-permute-start.10
  41.1 0.0 collective-permute-done.12.refs_0_
  41.1 0.0 collective-permute-start.14
  41.1 4.3 %collective-permute-done.7.refs_7_ = bf16[576,512]{1,0:T(8,128)(2,1)S(1)} collective-permute-done((bf16[576,512]{1,0:T(8,128)(2,1)S(1)}, bf16[576,512]{1,0:T(8,128)(2,1)S(1)}, u32[]{:S(2)}, u32[]{:S(2)}) %collective-permute-start.7) | collective-permute-done | bytes 589856 | tf_op jit(solution)/shard_map/ppermute | solution.py:298
  45.4 0.5 collective-permute-start.6
  45.9 1.4 %collective-permute-done.1.refs_0_ = bf16[4,592,128]{2,1,0:T(8,128)(2,1)S(1)} collective-permute-done((bf16[4,592,128]{2,1,0:T(8,128)(2,1)S(1)}, bf16[4,592,128]{2,1,0:T(8,128)(2,1)S(1)}, u32[]{:S(2)}, u32[]{:S(2)}) %collective-permute-start.1) | collective-permute-done | bytes 606240 | tf_op jit(solution)/shard_map/ppermute | solution.py:298
  47.3 0.5 collective-permute-start.11
  47.8 9.0 %collective-permute-done.14.refs_13_ = bf16[576,512]{1,0:T(8,128)(2,1)S(1)} collective-permute-done((bf16[576,512]{1,0:T(8,128)(2,1)S(1)}, bf16[576,512]{1,0:T(8,128)(2,1)S(1)}, u32[]{:S(2)}, u32[]{:S(2)}) %collective-permute-start.14) | collective-permute-done | bytes 589856 | tf_op jit(solution)/shard_map/ppermute | solution.py:298
  56.8 0.0 collective-permute-start.15
  56.8 0.5 collective-permute-start.8
  57.4 0.1 collective-permute-start.13
  57.5 1.4 %collective-permute-start.20 = (bf16[8,80,128]{2,1,0:T(8,128)(2,1)S(1)}, bf16[8,80,128]{2,1,0:T(8,128)(2,1)S(1)}, u32[]{:S(2)}, u32[]{:S(2)}) collective-permute-start(bf16[8,80,128]{2,1,0:T(8,128)(2,1)S(1)} %pad_maximum_fusion.2), channel_id=1, source_target_pairs={{0,16},{4,20},{8,24},{12,28},{16,0},{20,4},{24,8},{28,12},{1,17},{... | collective-permute-start | bytes 491528 | tf_op jit(solution)/shard_map/ppermute | solution.py:298
  58.9 1.2 %collective-permute-done.13.refs_12_ = bf16[576,256]{1,0:T(8,128)(2,1)S(1)} collective-permute-done((bf16[576,256]{1,0:T(8,128)(2,1)S(1)}, bf16[576,256]{1,0:T(8,128)(2,1)S(1)}, u32[]{:S(2)}, u32[]{:S(2)}) %collective-permute-start.13) | collective-permute-done | bytes 294944 | tf_op jit(solution)/shard_map/ppermute | solution.py:298
  60.1 4.1 %attend.4 = (bf16[272,512]{1,0:T(8,128)(2,1)S(1)}, bf16[272,512]{1,0:T(8,128)(2,1)S(1)}) custom-call(bf16[4,592,128]{2,1,0:T(8,128)(2,1)S(1)} %collective-permute-done.1.refs_0_, bf16[576,1024]{1,0:T(8,128)(2,1)S(1)} %bitcast.7, bf16[576,1024]{1,0:T(8,128)(2,1)S(1)} %collective-permute-done.2.refs_2_, bf16[576,1024]{1,0:T(8,128)(2,1)S(1)} %collective-permute-done.3.refs_3_, ...), custom_call_target="tpu_custom_call" | custom-call | flops 1000 | bytes 1000 | tf_op jit(solution)/shard_map/attend/pallas_call | solution.py:163
  64.3 1.4 %collective-permute-start.18 = (bf16[272,512]{1,0:T(8,128)(2,1)S(1)}, bf16[272,512]{1,0:T(8,128)(2,1)S(1)}, u32[]{:S(2)}, u32[]{:S(2)}) collective-permute-start(bf16[272,512]{1,0:T(8,128)(2,1)S(1)} %get-tuple-element.22), channel_id=1, source_target_pairs={{0,16},{4,20},{8,24},{12,28},{16,0},{20,4},{24,8},{28,12},{1,17},{... | collective-permute-start | bytes 835592 | tf_op jit(solution)/shard_map/ppermute | solution.py:298
  65.7 1.2 %collective-permute-start.21 = (bf16[16,80,128]{2,1,0:T(8,128)(2,1)S(1)}, bf16[16,80,128]{2,1,0:T(8,128)(2,1)S(1)}, u32[]{:S(2)}, u32[]{:S(2)}) collective-permute-start(bf16[16,80,128]{2,1,0:T(8,128)(2,1)S(1)} %pad_maximum_fusion.1), channel_id=1, source_target_pairs={{0,8},{4,12},{8,0},{12,4},{16,24},{20,28},{24,16},{28,20},{1,9},{5... | collective-permute-start | bytes 983048 | tf_op jit(solution)/shard_map/ppermute | solution.py:298
  66.9 4.1 %attend.5 = (bf16[272,512]{1,0:T(8,128)(2,1)S(1)}, bf16[272,512]{1,0:T(8,128)(2,1)S(1)}) custom-call(bf16[4,592,128]{2,1,0:T(8,128)(2,1)S(1)} %collective-permute-done.refs_0_, bf16[576,1024]{1,0:T(8,128)(2,1)S(1)} %bitcast.8, bf16[576,1024]{1,0:T(8,128)(2,1)S(1)} %collective-permute-done.2.refs_2_, bf16[576,1024]{1,0:T(8,128)(2,1)S(1)} %collective-permute-done.3.refs_3_, ...), custom_call_target="tpu_custom_call" | custom-call | flops 1000 | bytes 1000 | tf_op jit(solution)/shard_map/attend/pallas_call | solution.py:163
  71.1 2.0 %collective-permute-done.18.refs_0_ = bf16[272,512]{1,0:T(8,128)(2,1)S(1)} collective-permute-done((bf16[272,512]{1,0:T(8,128)(2,1)S(1)}, bf16[272,512]{1,0:T(8,128)(2,1)S(1)}, u32[]{:S(2)}, u32[]{:S(2)}) %collective-permute-start.18) | collective-permute-done | bytes 278560 | tf_op jit(solution)/shard_map/ppermute | solution.py:298
  73.0 0.3 combine.3
  73.3 2.5 %collective-permute-start.22 = (bf16[272,512]{1,0:T(8,128)(2,1)S(1)}, bf16[272,512]{1,0:T(8,128)(2,1)S(1)}, u32[]{:S(2)}, u32[]{:S(2)}) collective-permute-start(bf16[272,512]{1,0:T(8,128)(2,1)S(1)} %combine.3), channel_id=1, source_target_pairs={{0,2},{1,3},{2,0},{3,1},{4,6},{5,7},{6,4},{7,5},{8,10},{9,11},{10,... | collective-permute-start | bytes 835592 | tf_op jit(solution)/shard_map/ppermute | solution.py:298
  75.8 1.6 %collective-permute-start.16 = (bf16[272,512]{1,0:T(8,128)(2,1)S(1)}, bf16[272,512]{1,0:T(8,128)(2,1)S(1)}, u32[]{:S(2)}, u32[]{:S(2)}) collective-permute-start(bf16[272,512]{1,0:T(8,128)(2,1)S(1)} %get-tuple-element.21), channel_id=1, source_target_pairs={{0,16},{4,20},{8,24},{12,28},{16,0},{20,4},{24,8},{28,12},{1,17},{... | collective-permute-start | bytes 835592 | tf_op jit(solution)/shard_map/ppermute | solution.py:298
  77.5 4.3 %attend.6 = bf16[528,512]{1,0:T(8,128)(2,1)S(1)} custom-call(bf16[4,592,128]{2,1,0:T(8,128)(2,1)S(1)} %collective-permute-done.12.refs_0_, bf16[576,1024]{1,0:T(8,128)(2,1)S(1)} %bitcast.9, bf16[576,1024]{1,0:T(8,128)(2,1)S(1)} %collective-permute-done.2.refs_2_, bf16[576,1024]{1,0:T(8,128)(2,1)S(1)} %collective-permute-done.3.refs_3_, ...), custom_call_target="tpu_custom_call" | custom-call | flops 1000 | bytes 1000 | tf_op jit(solution)/shard_map/attend/pallas_call | solution.py:163
  81.8 6.3 %collective-permute-done.22.refs_0_ = bf16[272,512]{1,0:T(8,128)(2,1)S(1)} collective-permute-done((bf16[272,512]{1,0:T(8,128)(2,1)S(1)}, bf16[272,512]{1,0:T(8,128)(2,1)S(1)}, u32[]{:S(2)}, u32[]{:S(2)}) %collective-permute-start.22) | collective-permute-done | bytes 278560 | tf_op jit(solution)/shard_map/ppermute | solution.py:298
  88.1 1.4 %collective-permute-start.23 = (bf16[528,512]{1,0:T(8,128)(2,1)S(1)}, bf16[528,512]{1,0:T(8,128)(2,1)S(1)}, u32[]{:S(2)}, u32[]{:S(2)}) collective-permute-start(bf16[528,512]{1,0:T(8,128)(2,1)S(1)} %attend.6), channel_id=1, source_target_pairs={{0,16},{4,20},{8,24},{12,28},{16,0},{20,4},{24,8},{28,12},{1,17},{... | collective-permute-start | bytes 1622024 | tf_op jit(solution)/shard_map/ppermute | solution.py:298
  89.5 0.3 combine.2
  89.7 0.0 copy-start.1
  89.7 0.1 collective-permute-start.17
  89.8 4.1 %attend.7.refs_2_ = bf16[528,512]{1,0:T(8,128)(2,1)S(1)} custom-call(bf16[4,592,128]{2,1,0:T(8,128)(2,1)S(1)} %table.1.refs_0_, bf16[576,1024]{1,0:T(8,128)(2,1)S(1)} %bitcast.10, bf16[576,1024]{1,0:T(8,128)(2,1)S(1)} %collective-permute-done.2.refs_2_, bf16[576,1024]{1,0:T(8,128)(2,1)S(1)} %collective-permute-done.3.refs_3_, ...), custom_call_target="tpu_custom_call" | custom-call | flops 1000 | bytes 1000 | tf_op jit(solution)/shard_map/attend/pallas_call | solution.py:163
  94.0 6.9 %index.1 = f32[32,4096]{1,0:T(8,128)} custom-call(bf16[32,80,128]{2,1,0:T(8,128)(2,1)S(1)} %constant_dynamic-update-slice_fusion.meta_ref, bf16[4096,128]{1,0:T(8,128)(2,1)S(1)} %copy-done.1), custom_call_target="tpu_custom_call" | custom-call | flops 1000 | bytes 1000 | tf_op jit(solution)/shard_map/index/pallas_call | solution.py:273
  100.8 0.4 collective-permute-done.23.refs_1_
  101.2 1.1 %finish.2.refs_3_ = bf16[4,128,512]{2,1,0:T(8,128)(2,1)} custom-call(bf16[272,512]{1,0:T(8,128)(2,1)S(1)} %collective-permute-done.22.refs_0_, bf16[528,512]{1,0:T(8,128)(2,1)S(1)} %collective-permute-done.23.refs_1_, bf16[528,512]{1,0:T(8,128)(2,1)S(1)} %attend.7.refs_2_), custom_call_target="tpu_custom_call" | custom-call | flops 1000 | bytes 60000000 | tf_op jit(solution)/shard_map/finish/pallas_call | solution.py:222
  102.3 1.4 %collective-permute-done.17.refs_0_ = bf16[272,512]{1,0:T(8,128)(2,1)S(1)} collective-permute-done((bf16[272,512]{1,0:T(8,128)(2,1)S(1)}, bf16[272,512]{1,0:T(8,128)(2,1)S(1)}, u32[]{:S(2)}, u32[]{:S(2)}) %collective-permute-start.17) | collective-permute-done | bytes 278560 | tf_op jit(solution)/shard_map/ppermute | solution.py:298
  103.7 1.1 %finish.3 = bf16[4,128,512]{2,1,0:T(8,128)(2,1)} custom-call(bf16[272,512]{1,0:T(8,128)(2,1)S(1)} %collective-permute-done.17.refs_0_, bf16[528,512]{1,0:T(8,128)(2,1)S(1)} %collective-permute-done.23.refs_1_, bf16[528,512]{1,0:T(8,128)(2,1)S(1)} %attend.7.refs_2_, bf16[4,128,512]{2,1,0:T(8,128)(2,1)} %finish.2.refs_3_), custom_call_target="tpu_custom_call", output_to_operand_aliasing={{}: (3, {})} | custom-call | flops 1000 | bytes 1000 | tf_op jit(solution)/shard_map/finish/pallas_call | solution.py:222
  (33 shorter events, 0.3 us)
Async XLA Ops:
  0.6 5.8 %copy-start.3 = (s32[4,2048]{1,0:T(4,128)S(1)}, s32[4,2048]{1,0:T(4,128)}, u32[]{:S(2)}) copy-start(s32[4,2048]{1,0:T(4,128)} %selected_ref.1) | copy-start | bytes 98308
  0.6 5.8 %copy-start.2 = (bf16[4,128,576]{1,2,0:T(8,128)(2,1)S(1)}, bf16[4,128,576]{1,2,0:T(8,128)(2,1)}, u32[]{:S(2)}) copy-start(bf16[4,128,576]{1,2,0:T(8,128)(2,1)} %param.8) | copy-start | bytes 1769476
  0.7 10.6 %copy-start.5 = (bf16[4,64]{1,0:T(4,128)(2,1)S(1)}, bf16[4,64]{1,0:T(4,128)(2,1)}, u32[]{:S(2)}) copy-start(bf16[4,64]{1,0:T(4,128)(2,1)} %param.10) | copy-start | bytes 1540
  0.7 31.4 %copy-start = (bf16[1024,576]{0,1:T(8,128)(2,1)S(1)}, bf16[1024,576]{0,1:T(8,128)(2,1)}, u32[]{:S(2)}) copy-start(bf16[1024,576]{0,1:T(8,128)(2,1)} %param.6) | copy-start | bytes 3538948
  0.7 30.8 %collective-permute-start.3 = (bf16[576,1024]{1,0:T(8,128)(2,1)}, bf16[576,1024]{1,0:T(8,128)(2,1)S(1)}, u32[]{:S(2)}, u32[]{:S(2)}) collective-permute-start(bf16[576,1024]{1,0:T(8,128)(2,1)} %bitcast.3), channel_id=1, source_target_pairs={{0,8},{4,12},{8,0},{12,4},{16,24},{20,28},{24,16},{28,20},{1,9},{5... | collective-permute-start | bytes 3538952 | tf_op jit(solution)/shard_map/ppermute | solution.py:298
  4.8 26.7 %collective-permute-start.5 = (bf16[576,512]{1,0:T(8,128)(2,1)S(1)}, bf16[576,512]{1,0:T(8,128)(2,1)S(1)}, u32[]{:S(2)}, u32[]{:S(2)}) collective-permute-start(bf16[576,512]{1,0:T(8,128)(2,1)S(1)} %slice.16), channel_id=1, source_target_pairs={{0,1},{1,0},{2,3},{3,2},{4,5},{5,4},{6,7},{7,6},{8,9},{9,8},{10,11... | collective-permute-start | bytes 1769480 | tf_op jit(solution)/shard_map/ppermute | solution.py:298
  6.5 31.1 %copy-start.4 = (bf16[4,64,128]{2,1,0:T(8,128)(2,1)S(1)}, bf16[4,64,128]{2,1,0:T(8,128)(2,1)}, u32[]{:S(2)}) copy-start(bf16[4,64,128]{2,1,0:T(8,128)(2,1)} %param.9) | copy-start | bytes 196612
  7.1 28.9 %collective-permute-start = (bf16[4,592,128]{2,1,0:T(8,128)(2,1)S(1)}, bf16[4,592,128]{2,1,0:T(8,128)(2,1)S(1)}, u32[]{:S(2)}, u32[]{:S(2)}) collective-permute-start(bf16[4,592,128]{2,1,0:T(8,128)(2,1)S(1)} %table.1.refs_0_), channel_id=1, source_target_pairs={{0,2},{1,3},{2,0},{3,1},{4,6},{5,7},{6,4},{7,5},{8,10},{9,11},{10,... | collective-permute-start | bytes 1818632 | tf_op jit(solution)/shard_map/ppermute | solution.py:298
  9.7 31.4 %collective-permute-start.12 = (bf16[4,592,128]{2,1,0:T(8,128)(2,1)S(1)}, bf16[4,592,128]{2,1,0:T(8,128)(2,1)S(1)}, u32[]{:S(2)}, u32[]{:S(2)}) collective-permute-start(bf16[4,592,128]{2,1,0:T(8,128)(2,1)S(1)} %table.1.refs_0_), channel_id=1, source_target_pairs={{0,16},{4,20},{8,24},{12,28},{16,0},{20,4},{24,8},{28,12},{1,17},{... | collective-permute-start | bytes 1818632 | tf_op jit(solution)/shard_map/ppermute | solution.py:298
  31.5 13.9 %collective-permute-start.7 = (bf16[576,512]{1,0:T(8,128)(2,1)S(1)}, bf16[576,512]{1,0:T(8,128)(2,1)S(1)}, u32[]{:S(2)}, u32[]{:S(2)}) collective-permute-start(bf16[576,512]{1,0:T(8,128)(2,1)S(1)} %collective-permute-done.5.refs_5_), channel_id=1, source_target_pairs={{0,8},{4,12},{8,0},{12,4},{16,24},{20,28},{24,16},{28,20},{1,9},{5... | collective-permute-start | bytes 1769480 | tf_op jit(solution)/shard_map/ppermute | solution.py:298
  32.1 9.0 %collective-permute-start.9 = (bf16[576,256]{1,0:T(8,128)(2,1)S(1)}, bf16[576,256]{1,0:T(8,128)(2,1)S(1)}, u32[]{:S(2)}, u32[]{:S(2)}) collective-permute-start(bf16[576,256]{1,0:T(8,128)(2,1)S(1)} %get-tuple-element.18), channel_id=1, source_target_pairs={{0,1},{1,0},{2,3},{3,2},{4,5},{5,4},{6,7},{7,6},{8,9},{9,8},{10,11... | collective-permute-start | bytes 884744 | tf_op jit(solution)/shard_map/ppermute | solution.py:298
  36.0 11.2 %collective-permute-start.1 = (bf16[4,592,128]{2,1,0:T(8,128)(2,1)S(1)}, bf16[4,592,128]{2,1,0:T(8,128)(2,1)S(1)}, u32[]{:S(2)}, u32[]{:S(2)}) collective-permute-start(bf16[4,592,128]{2,1,0:T(8,128)(2,1)S(1)} %collective-permute-done.refs_0_), channel_id=1, source_target_pairs={{0,16},{4,20},{8,24},{12,28},{16,0},{20,4},{24,8},{28,12},{1,17},{... | collective-permute-start | bytes 1818632 | tf_op jit(solution)/shard_map/ppermute | solution.py:298
  37.6 1.3 %collective-permute-start.19 = (bf16[4,80,128]{2,1,0:T(8,128)(2,1)S(1)}, bf16[4,80,128]{2,1,0:T(8,128)(2,1)S(1)}, u32[]{:S(2)}, u32[]{:S(2)}) collective-permute-start(bf16[4,80,128]{2,1,0:T(8,128)(2,1)S(1)} %pad_maximum_fusion.3), channel_id=1, source_target_pairs={{0,4},{4,0},{8,12},{12,8},{16,20},{20,16},{24,28},{28,24},{1,5},{5... | collective-permute-start | bytes 245768 | tf_op jit(solution)/shard_map/ppermute | solution.py:298
  38.9 18.5 %collective-permute-start.2 = (bf16[576,1024]{1,0:T(8,128)(2,1)S(1)}, bf16[576,1024]{1,0:T(8,128)(2,1)S(1)}, u32[]{:S(2)}, u32[]{:S(2)}) collective-permute-start(bf16[576,1024]{1,0:T(8,128)(2,1)S(1)} %bitcast.6), channel_id=1, source_target_pairs={{0,4},{4,0},{8,12},{12,8},{16,20},{20,16},{24,28},{28,24},{1,5},{5... | collective-permute-start | bytes 3538952 | tf_op jit(solution)/shard_map/ppermute | solution.py:298
  41.1 4.3 %collective-permute-start.10 = (bf16[576,256]{1,0:T(8,128)(2,1)S(1)}, bf16[576,256]{1,0:T(8,128)(2,1)S(1)}, u32[]{:S(2)}, u32[]{:S(2)}) collective-permute-start(bf16[576,256]{1,0:T(8,128)(2,1)S(1)} %collective-permute-done.9.refs_9_), channel_id=1, source_target_pairs={{0,4},{4,0},{8,12},{12,8},{16,20},{20,16},{24,28},{28,24},{1,5},{5... | collective-permute-start | bytes 884744 | tf_op jit(solution)/shard_map/ppermute | solution.py:298
  41.1 15.7 %collective-permute-start.14 = (bf16[576,512]{1,0:T(8,128)(2,1)S(1)}, bf16[576,512]{1,0:T(8,128)(2,1)S(1)}, u32[]{:S(2)}, u32[]{:S(2)}) collective-permute-start(bf16[576,512]{1,0:T(8,128)(2,1)S(1)} %pad_maximum_fusion), channel_id=1, source_target_pairs={{0,1},{1,0},{2,3},{3,2},{4,5},{5,4},{6,7},{7,6},{8,9},{9,8},{10,11... | collective-permute-start | bytes 1769480 | tf_op jit(solution)/shard_map/ppermute | solution.py:298
  45.4 14.7 %collective-permute-start.4 = (bf16[576,1024]{1,0:T(8,128)(2,1)S(1)}, bf16[576,1024]{1,0:T(8,128)(2,1)S(1)}, u32[]{:S(2)}, u32[]{:S(2)}) collective-permute-start(bf16[576,1024]{1,0:T(8,128)(2,1)S(1)} %collective-permute-done.3.refs_3_), channel_id=1, source_target_pairs={{0,4},{4,0},{8,12},{12,8},{16,20},{20,16},{24,28},{28,24},{1,5},{5... | collective-permute-start | bytes 3538952 | tf_op jit(solution)/shard_map/ppermute | solution.py:298
  45.4 12.0 %collective-permute-start.6 = (bf16[576,512]{1,0:T(8,128)(2,1)S(1)}, bf16[576,512]{1,0:T(8,128)(2,1)S(1)}, u32[]{:S(2)}, u32[]{:S(2)}) collective-permute-start(bf16[576,512]{1,0:T(8,128)(2,1)S(1)} %collective-permute-done.5.refs_5_), channel_id=1, source_target_pairs={{0,4},{4,0},{8,12},{12,8},{16,20},{20,16},{24,28},{28,24},{1,5},{5... | collective-permute-start | bytes 1769480 | tf_op jit(solution)/shard_map/ppermute | solution.py:298
  47.3 9.6 %collective-permute-start.11 = (bf16[576,256]{1,0:T(8,128)(2,1)S(1)}, bf16[576,256]{1,0:T(8,128)(2,1)S(1)}, u32[]{:S(2)}, u32[]{:S(2)}) collective-permute-start(bf16[576,256]{1,0:T(8,128)(2,1)S(1)} %collective-permute-done.9.refs_9_), channel_id=1, source_target_pairs={{0,8},{4,12},{8,0},{12,4},{16,24},{20,28},{24,16},{28,20},{1,9},{5... | collective-permute-start | bytes 884744 | tf_op jit(solution)/shard_map/ppermute | solution.py:298
  56.8 3.3 %collective-permute-start.15 = (bf16[576,512]{1,0:T(8,128)(2,1)S(1)}, bf16[576,512]{1,0:T(8,128)(2,1)S(1)}, u32[]{:S(2)}, u32[]{:S(2)}) collective-permute-start(bf16[576,512]{1,0:T(8,128)(2,1)S(1)} %collective-permute-done.14.refs_13_), channel_id=1, source_target_pairs={{0,4},{4,0},{8,12},{12,8},{16,20},{20,16},{24,28},{28,24},{1,5},{5... | collective-permute-start | bytes 1769480 | tf_op jit(solution)/shard_map/ppermute | solution.py:298
  56.8 3.3 %collective-permute-start.8 = (bf16[576,512]{1,0:T(8,128)(2,1)S(1)}, bf16[576,512]{1,0:T(8,128)(2,1)S(1)}, u32[]{:S(2)}, u32[]{:S(2)}) collective-permute-start(bf16[576,512]{1,0:T(8,128)(2,1)S(1)} %collective-permute-done.7.refs_7_), channel_id=1, source_target_pairs={{0,4},{4,0},{8,12},{12,8},{16,20},{20,16},{24,28},{28,24},{1,5},{5... | collective-permute-start | bytes 1769480 | tf_op jit(solution)/shard_map/ppermute | solution.py:298
  57.4 2.8 %collective-permute-start.13 = (bf16[576,256]{1,0:T(8,128)(2,1)S(1)}, bf16[576,256]{1,0:T(8,128)(2,1)S(1)}, u32[]{:S(2)}, u32[]{:S(2)}) collective-permute-start(bf16[576,256]{1,0:T(8,128)(2,1)S(1)} %collective-permute-done.11.refs_11_), channel_id=1, source_target_pairs={{0,4},{4,0},{8,12},{12,8},{16,20},{20,16},{24,28},{28,24},{1,5},{5... | collective-permute-start | bytes 884744 | tf_op jit(solution)/shard_map/ppermute | solution.py:298
  57.5 8.2 %collective-permute-start.20 = (bf16[8,80,128]{2,1,0:T(8,128)(2,1)S(1)}, bf16[8,80,128]{2,1,0:T(8,128)(2,1)S(1)}, u32[]{:S(2)}, u32[]{:S(2)}) collective-permute-start(bf16[8,80,128]{2,1,0:T(8,128)(2,1)S(1)} %pad_maximum_fusion.2), channel_id=1, source_target_pairs={{0,16},{4,20},{8,24},{12,28},{16,0},{20,4},{24,8},{28,12},{1,17},{... | collective-permute-start | bytes 491528 | tf_op jit(solution)/shard_map/ppermute | solution.py:298
  64.3 8.8 %collective-permute-start.18 = (bf16[272,512]{1,0:T(8,128)(2,1)S(1)}, bf16[272,512]{1,0:T(8,128)(2,1)S(1)}, u32[]{:S(2)}, u32[]{:S(2)}) collective-permute-start(bf16[272,512]{1,0:T(8,128)(2,1)S(1)} %get-tuple-element.22), channel_id=1, source_target_pairs={{0,16},{4,20},{8,24},{12,28},{16,0},{20,4},{24,8},{28,12},{1,17},{... | collective-permute-start | bytes 835592 | tf_op jit(solution)/shard_map/ppermute | solution.py:298
  65.7 11.7 %collective-permute-start.21 = (bf16[16,80,128]{2,1,0:T(8,128)(2,1)S(1)}, bf16[16,80,128]{2,1,0:T(8,128)(2,1)S(1)}, u32[]{:S(2)}, u32[]{:S(2)}) collective-permute-start(bf16[16,80,128]{2,1,0:T(8,128)(2,1)S(1)} %pad_maximum_fusion.1), channel_id=1, source_target_pairs={{0,8},{4,12},{8,0},{12,4},{16,24},{20,28},{24,16},{28,20},{1,9},{5... | collective-permute-start | bytes 983048 | tf_op jit(solution)/shard_map/ppermute | solution.py:298
  73.3 14.8 %collective-permute-start.22 = (bf16[272,512]{1,0:T(8,128)(2,1)S(1)}, bf16[272,512]{1,0:T(8,128)(2,1)S(1)}, u32[]{:S(2)}, u32[]{:S(2)}) collective-permute-start(bf16[272,512]{1,0:T(8,128)(2,1)S(1)} %combine.3), channel_id=1, source_target_pairs={{0,2},{1,3},{2,0},{3,1},{4,6},{5,7},{6,4},{7,5},{8,10},{9,11},{10,... | collective-permute-start | bytes 835592 | tf_op jit(solution)/shard_map/ppermute | solution.py:298
  75.8 13.6 %collective-permute-start.16 = (bf16[272,512]{1,0:T(8,128)(2,1)S(1)}, bf16[272,512]{1,0:T(8,128)(2,1)S(1)}, u32[]{:S(2)}, u32[]{:S(2)}) collective-permute-start(bf16[272,512]{1,0:T(8,128)(2,1)S(1)} %get-tuple-element.21), channel_id=1, source_target_pairs={{0,16},{4,20},{8,24},{12,28},{16,0},{20,4},{24,8},{28,12},{1,17},{... | collective-permute-start | bytes 835592 | tf_op jit(solution)/shard_map/ppermute | solution.py:298
  88.1 13.1 %collective-permute-start.23 = (bf16[528,512]{1,0:T(8,128)(2,1)S(1)}, bf16[528,512]{1,0:T(8,128)(2,1)S(1)}, u32[]{:S(2)}, u32[]{:S(2)}) collective-permute-start(bf16[528,512]{1,0:T(8,128)(2,1)S(1)} %attend.6), channel_id=1, source_target_pairs={{0,16},{4,20},{8,24},{12,28},{16,0},{20,4},{24,8},{28,12},{1,17},{... | collective-permute-start | bytes 1622024 | tf_op jit(solution)/shard_map/ppermute | solution.py:298
  89.7 4.2 %copy-start.1 = (bf16[4096,128]{1,0:T(8,128)(2,1)S(1)}, bf16[4096,128]{1,0:T(8,128)(2,1)}, u32[]{:S(2)}) copy-start(bf16[4096,128]{1,0:T(8,128)(2,1)} %keys_ref.1) | copy-start | bytes 3145732
  89.7 14.0 %collective-permute-start.17 = (bf16[272,512]{1,0:T(8,128)(2,1)S(1)}, bf16[272,512]{1,0:T(8,128)(2,1)S(1)}, u32[]{:S(2)}, u32[]{:S(2)}) collective-permute-start(bf16[272,512]{1,0:T(8,128)(2,1)S(1)} %combine.2), channel_id=1, source_target_pairs={{0,2},{1,3},{2,0},{3,1},{4,6},{5,7},{6,4},{7,5},{8,10},{9,11},{10,... | collective-permute-start | bytes 835592 | tf_op jit(solution)/shard_map/ppermute | solution.py:298

commit v7 on v6

--- a/solution.py
+++ b/solution.py
@@ -359,7 +359,7 @@
             masks += [mask ^ bit for mask in masks]
 
         parts, last = [], []
-        split = 2
+        split, halves = 2, []
         some = per // split
         for across in row_planes[1:] + row_planes[:1]:
             mine = []
@@ -368,18 +368,22 @@
                 sizes = (planes, tokens)
                 done = attend([pack], slabs, places, width, sizes, masked, split if across else 1)
                 last = list(done)
-                first = [] if across else [back[0] for back in parts]
-                mine.append([swap(after(a, *first), "ctx", mask) if mask else a for a in done])
+                mine.append([swap(a, "ctx", mask) if mask else a for a in done] if across else done)
             if across:
                 back = []
                 for i in range(split):
                     rows = range(i * some, (i + 1) * some)
                     mixed = combine([part[i] for part in mine], [rows[0]] * len(mine), rows, heads)
                     back.append(swap(mixed, "row", across))
+                    halves.append(mixed)
                     last = last + [mixed, meta] if i == 0 else last
                 parts.append(back)
             else:
-                own = [part[0] for part in mine]
+                waits = [back[0] for back in parts] + halves + [part[0] for part in mine]
+                own = [
+                    swap(after(part[0], *waits), "ctx", mask) if mask else part[0]
+                    for mask, part in zip(reversed(row_columns), mine)
+                ]
         index_scores = index_block(after(meta, *last), index_keys, index_query.shape[1], per, masks)
         attended = None
         for i in range(split):

time: 105 us -> 105 us (level)
  waiting for transfers between devices: 52.2 us -> 50.9 us
  starting transfers between devices: 23.5 us -> 24.7 us
    ppermute x24, waiting for transfers between devices: 52.2 us -> 50.9 us  [swap(): return lax.ppermute(array, axis, [(i, i ^ mask) for i in range(size)])]
    ppermute x24, starting transfers between devices: 23.5 us -> 24.7 us  [swap(): return lax.ppermute(array, axis, [(i, i ^ mask) for i in range(size)])]
  transfers between devices with their start and end apart: 24 -> 24, of which waited for: 12 -> 13; matrix products, arithmetic and copies ran while one was open for 1% -> 1% of each run, Pallas kernels for 25% -> 25%
where the time goes in v7:
time: 105 us
  waiting for transfers between devices  50.9 us (48%)
  Pallas kernels  27 us (26%)
  starting transfers between devices  24.7 us (24%)
  local copies, waits for them, and re-layouts  1.32 us (1%)
    ppermute x24, waiting for transfers between devices, swap(): return lax.ppermute(array, axis, [(i, i ^ mask) for i in range(size)])  50.9 us
    ppermute x24, starting transfers between devices, swap(): return lax.ppermute(array, axis, [(i, i ^ mask) for i in range(size)])  24.7 us
    pallas_call x4, Pallas kernels, attend(): pl.pallas_call(functools.partial(attend_kernel, places, blocks, per, widt...  16.7 us
    pallas_call x1, Pallas kernels, index_block(): pl.pallas_call(functools.partial(index_kernel, heads, per, masks), grid=(...  6.84 us
    pallas_call x2, Pallas kernels, finish(): pl.pallas_call(functools.partial(combine_kernel, begins, rows, heads, Tru...  2.23 us
  transfers between devices with their start and end apart: 24, of which 13 were waited for; matrix products, arithmetic and copies ran while one was open for 1% of the time, Pallas kernels for 25%

profile of v7, /device:TPU:0, one launch (start us, length us, event | category | flops | bytes accessed | tf_op | source)
XLA Modules:
  0.0 104.7 jit_solution(17486246204507875108)
XLA Ops:
  0.7 3.0 %collective-permute-start.3 = (bf16[576,1024]{1,0:T(8,128)(2,1)}, bf16[576,1024]{1,0:T(8,128)(2,1)S(1)}, u32[]{:S(2)}, u32[]{:S(2)}) collective-permute-start(bf16[576,1024]{1,0:T(8,128)(2,1)} %bitcast.3), channel_id=1, source_target_pairs={{0,8},{4,12},{8,0},{12,4},{16,24},{20,28},{24,16},{28,20},{1,9},{5... | collective-permute-start | bytes 3538952 | tf_op jit(solution)/shard_map/ppermute | solution.py:298
  3.7 1.1 %slice.16 = bf16[576,512]{1,0:T(8,128)(2,1)S(1)} slice(bf16[576,1024]{1,0:T(8,128)(2,1)} %bitcast.4), slice={[0:576], [0:512]} | slice | bytes 1179648 | tf_op jit(solution)/shard_map/slice | solution.py:330
  4.8 1.6 %collective-permute-start.5 = (bf16[576,512]{1,0:T(8,128)(2,1)S(1)}, bf16[576,512]{1,0:T(8,128)(2,1)S(1)}, u32[]{:S(2)}, u32[]{:S(2)}) collective-permute-start(bf16[576,512]{1,0:T(8,128)(2,1)S(1)} %slice.16), channel_id=1, source_target_pairs={{0,1},{1,0},{2,3},{3,2},{4,5},{5,4},{6,7},{7,6},{8,9},{9,8},{10,11... | collective-permute-start | bytes 1769480 | tf_op jit(solution)/shard_map/ppermute | solution.py:298
  6.5 0.7 table.1.refs_0_
  7.1 2.6 %collective-permute-start = (bf16[4,592,128]{2,1,0:T(8,128)(2,1)S(1)}, bf16[4,592,128]{2,1,0:T(8,128)(2,1)S(1)}, u32[]{:S(2)}, u32[]{:S(2)}) collective-permute-start(bf16[4,592,128]{2,1,0:T(8,128)(2,1)S(1)} %table.1.refs_0_), channel_id=1, source_target_pairs={{0,2},{1,3},{2,0},{3,1},{4,6},{5,7},{6,4},{7,5},{8,10},{9,11},{10,... | collective-permute-start | bytes 1818632 | tf_op jit(solution)/shard_map/ppermute | solution.py:298
  9.7 1.5 %collective-permute-start.12 = (bf16[4,592,128]{2,1,0:T(8,128)(2,1)S(1)}, bf16[4,592,128]{2,1,0:T(8,128)(2,1)S(1)}, u32[]{:S(2)}, u32[]{:S(2)}) collective-permute-start(bf16[4,592,128]{2,1,0:T(8,128)(2,1)S(1)} %table.1.refs_0_), channel_id=1, source_target_pairs={{0,16},{4,20},{8,24},{12,28},{16,0},{20,4},{24,8},{28,12},{1,17},{... | collective-permute-start | bytes 1818632 | tf_op jit(solution)/shard_map/ppermute | solution.py:298
  11.3 20.2 %collective-permute-done.5.refs_5_ = bf16[576,512]{1,0:T(8,128)(2,1)S(1)} collective-permute-done((bf16[576,512]{1,0:T(8,128)(2,1)S(1)}, bf16[576,512]{1,0:T(8,128)(2,1)S(1)}, u32[]{:S(2)}, u32[]{:S(2)}) %collective-permute-start.5) | collective-permute-done | bytes 589856 | tf_op jit(solution)/shard_map/ppermute | solution.py:298
  31.5 0.0 collective-permute-done.3.refs_3_
  31.5 0.5 collective-permute-start.7
  32.1 1.2 %collective-permute-start.9 = (bf16[576,256]{1,0:T(8,128)(2,1)S(1)}, bf16[576,256]{1,0:T(8,128)(2,1)S(1)}, u32[]{:S(2)}, u32[]{:S(2)}) collective-permute-start(bf16[576,256]{1,0:T(8,128)(2,1)S(1)} %get-tuple-element.18), channel_id=1, source_target_pairs={{0,1},{1,0},{2,3},{3,2},{4,5},{5,4},{6,7},{7,6},{8,9},{9,8},{10,11... | collective-permute-start | bytes 884744 | tf_op jit(solution)/shard_map/ppermute | solution.py:298
  33.3 2.8 %collective-permute-done.refs_0_ = bf16[4,592,128]{2,1,0:T(8,128)(2,1)S(1)} collective-permute-done((bf16[4,592,128]{2,1,0:T(8,128)(2,1)S(1)}, bf16[4,592,128]{2,1,0:T(8,128)(2,1)S(1)}, u32[]{:S(2)}, u32[]{:S(2)}) %collective-permute-start) | collective-permute-done | bytes 606240 | tf_op jit(solution)/shard_map/ppermute | solution.py:298
  36.0 1.5 %collective-permute-start.1 = (bf16[4,592,128]{2,1,0:T(8,128)(2,1)S(1)}, bf16[4,592,128]{2,1,0:T(8,128)(2,1)S(1)}, u32[]{:S(2)}, u32[]{:S(2)}) collective-permute-start(bf16[4,592,128]{2,1,0:T(8,128)(2,1)S(1)} %collective-permute-done.refs_0_), channel_id=1, source_target_pairs={{0,16},{4,20},{8,24},{12,28},{16,0},{20,4},{24,8},{28,12},{1,17},{... | collective-permute-start | bytes 1818632 | tf_op jit(solution)/shard_map/ppermute | solution.py:298
  37.6 0.1 collective-permute-start.19
  37.7 1.3 %collective-permute-done.19 = bf16[4,80,128]{2,1,0:T(8,128)(2,1)S(1)} collective-permute-done((bf16[4,80,128]{2,1,0:T(8,128)(2,1)S(1)}, bf16[4,80,128]{2,1,0:T(8,128)(2,1)S(1)}, u32[]{:S(2)}, u32[]{:S(2)}) %collective-permute-start.19) | collective-permute-done | bytes 81952 | tf_op jit(solution)/shard_map/ppermute | solution.py:298
  38.9 0.2 collective-permute-start.2
  39.2 1.9 %collective-permute-done.9.refs_9_ = bf16[576,256]{1,0:T(8,128)(2,1)S(1)} collective-permute-done((bf16[576,256]{1,0:T(8,128)(2,1)S(1)}, bf16[576,256]{1,0:T(8,128)(2,1)S(1)}, u32[]{:S(2)}, u32[]{:S(2)}) %collective-permute-start.9) | collective-permute-done | bytes 294944 | tf_op jit(solution)/shard_map/ppermute | solution.py:298
  41.1 4.3 %collective-permute-done.7.refs_7_ = bf16[576,512]{1,0:T(8,128)(2,1)S(1)} collective-permute-done((bf16[576,512]{1,0:T(8,128)(2,1)S(1)}, bf16[576,512]{1,0:T(8,128)(2,1)S(1)}, u32[]{:S(2)}, u32[]{:S(2)}) %collective-permute-start.7) | collective-permute-done | bytes 589856 | tf_op jit(solution)/shard_map/ppermute | solution.py:298
  45.4 0.0 collective-permute-start.4
  45.4 0.0 collective-permute-done.10.refs_10_
  45.4 0.5 collective-permute-start.6
  45.9 1.4 %collective-permute-done.1.refs_0_ = bf16[4,592,128]{2,1,0:T(8,128)(2,1)S(1)} collective-permute-done((bf16[4,592,128]{2,1,0:T(8,128)(2,1)S(1)}, bf16[4,592,128]{2,1,0:T(8,128)(2,1)S(1)}, u32[]{:S(2)}, u32[]{:S(2)}) %collective-permute-start.1) | collective-permute-done | bytes 606240 | tf_op jit(solution)/shard_map/ppermute | solution.py:298
  47.3 0.5 collective-permute-start.11
  47.8 9.0 %collective-permute-done.14.refs_13_ = bf16[576,512]{1,0:T(8,128)(2,1)S(1)} collective-permute-done((bf16[576,512]{1,0:T(8,128)(2,1)S(1)}, bf16[576,512]{1,0:T(8,128)(2,1)S(1)}, u32[]{:S(2)}, u32[]{:S(2)}) %collective-permute-start.14) | collective-permute-done | bytes 589856 | tf_op jit(solution)/shard_map/ppermute | solution.py:298
  56.8 0.5 collective-permute-start.8
  57.4 0.1 collective-permute-start.13
  57.5 1.4 %collective-permute-start.20 = (bf16[8,80,128]{2,1,0:T(8,128)(2,1)S(1)}, bf16[8,80,128]{2,1,0:T(8,128)(2,1)S(1)}, u32[]{:S(2)}, u32[]{:S(2)}) collective-permute-start(bf16[8,80,128]{2,1,0:T(8,128)(2,1)S(1)} %pad_maximum_fusion.2), channel_id=1, source_target_pairs={{0,16},{4,20},{8,24},{12,28},{16,0},{20,4},{24,8},{28,12},{1,17},{... | collective-permute-start | bytes 491528 | tf_op jit(solution)/shard_map/ppermute | solution.py:298
  58.9 1.2 %collective-permute-done.13.refs_12_ = bf16[576,256]{1,0:T(8,128)(2,1)S(1)} collective-permute-done((bf16[576,256]{1,0:T(8,128)(2,1)S(1)}, bf16[576,256]{1,0:T(8,128)(2,1)S(1)}, u32[]{:S(2)}, u32[]{:S(2)}) %collective-permute-start.13) | collective-permute-done | bytes 294944 | tf_op jit(solution)/shard_map/ppermute | solution.py:298
  60.1 4.1 %attend.4 = (bf16[272,512]{1,0:T(8,128)(2,1)S(1)}, bf16[272,512]{1,0:T(8,128)(2,1)S(1)}) custom-call(bf16[4,592,128]{2,1,0:T(8,128)(2,1)S(1)} %collective-permute-done.1.refs_0_, bf16[576,1024]{1,0:T(8,128)(2,1)S(1)} %bitcast.7, bf16[576,1024]{1,0:T(8,128)(2,1)S(1)} %collective-permute-done.2.refs_2_, bf16[576,1024]{1,0:T(8,128)(2,1)S(1)} %collective-permute-done.3.refs_3_, ...), custom_call_target="tpu_custom_call" | custom-call | flops 1000 | bytes 1000 | tf_op jit(solution)/shard_map/attend/pallas_call | solution.py:163
  64.3 1.4 %collective-permute-start.18 = (bf16[272,512]{1,0:T(8,128)(2,1)S(1)}, bf16[272,512]{1,0:T(8,128)(2,1)S(1)}, u32[]{:S(2)}, u32[]{:S(2)}) collective-permute-start(bf16[272,512]{1,0:T(8,128)(2,1)S(1)} %get-tuple-element.22), channel_id=1, source_target_pairs={{0,16},{4,20},{8,24},{12,28},{16,0},{20,4},{24,8},{28,12},{1,17},{... | collective-permute-start | bytes 835592 | tf_op jit(solution)/shard_map/ppermute | solution.py:298
  65.7 1.2 %collective-permute-start.21 = (bf16[16,80,128]{2,1,0:T(8,128)(2,1)S(1)}, bf16[16,80,128]{2,1,0:T(8,128)(2,1)S(1)}, u32[]{:S(2)}, u32[]{:S(2)}) collective-permute-start(bf16[16,80,128]{2,1,0:T(8,128)(2,1)S(1)} %pad_maximum_fusion.1), channel_id=1, source_target_pairs={{0,8},{4,12},{8,0},{12,4},{16,24},{20,28},{24,16},{28,20},{1,9},{5... | collective-permute-start | bytes 983048 | tf_op jit(solution)/shard_map/ppermute | solution.py:298
  66.9 0.5 collective-permute-start.16
  67.4 4.1 %attend.5 = (bf16[272,512]{1,0:T(8,128)(2,1)S(1)}, bf16[272,512]{1,0:T(8,128)(2,1)S(1)}) custom-call(bf16[4,592,128]{2,1,0:T(8,128)(2,1)S(1)} %collective-permute-done.refs_0_, bf16[576,1024]{1,0:T(8,128)(2,1)S(1)} %bitcast.8, bf16[576,1024]{1,0:T(8,128)(2,1)S(1)} %collective-permute-done.2.refs_2_, bf16[576,1024]{1,0:T(8,128)(2,1)S(1)} %collective-permute-done.3.refs_3_, ...), custom_call_target="tpu_custom_call" | custom-call | flops 1000 | bytes 1000 | tf_op jit(solution)/shard_map/attend/pallas_call | solution.py:163
  71.6 2.3 %collective-permute-done.18.refs_0_ = bf16[272,512]{1,0:T(8,128)(2,1)S(1)} collective-permute-done((bf16[272,512]{1,0:T(8,128)(2,1)S(1)}, bf16[272,512]{1,0:T(8,128)(2,1)S(1)}, u32[]{:S(2)}, u32[]{:S(2)}) %collective-permute-start.18) | collective-permute-done | bytes 278560 | tf_op jit(solution)/shard_map/ppermute | solution.py:298
  73.8 0.3 combine.3
  74.1 2.5 %collective-permute-start.22 = (bf16[272,512]{1,0:T(8,128)(2,1)S(1)}, bf16[272,512]{1,0:T(8,128)(2,1)S(1)}, u32[]{:S(2)}, u32[]{:S(2)}) collective-permute-start(bf16[272,512]{1,0:T(8,128)(2,1)S(1)} %combine.3), channel_id=1, source_target_pairs={{0,2},{1,3},{2,0},{3,1},{4,6},{5,7},{6,4},{7,5},{8,10},{9,11},{10,... | collective-permute-start | bytes 835592 | tf_op jit(solution)/shard_map/ppermute | solution.py:298
  76.7 2.3 %collective-permute-done.16.refs_0_ = bf16[272,512]{1,0:T(8,128)(2,1)S(1)} collective-permute-done((bf16[272,512]{1,0:T(8,128)(2,1)S(1)}, bf16[272,512]{1,0:T(8,128)(2,1)S(1)}, u32[]{:S(2)}, u32[]{:S(2)}) %collective-permute-start.16) | collective-permute-done | bytes 278560 | tf_op jit(solution)/shard_map/ppermute | solution.py:298
  79.0 0.3 combine.2
  79.3 4.3 %attend.6 = bf16[528,512]{1,0:T(8,128)(2,1)S(1)} custom-call(bf16[4,592,128]{2,1,0:T(8,128)(2,1)S(1)} %collective-permute-done.12.refs_0_, bf16[576,1024]{1,0:T(8,128)(2,1)S(1)} %bitcast.9, bf16[576,1024]{1,0:T(8,128)(2,1)S(1)} %collective-permute-done.2.refs_2_, bf16[576,1024]{1,0:T(8,128)(2,1)S(1)} %collective-permute-done.3.refs_3_, ...), custom_call_target="tpu_custom_call" | custom-call | flops 1000 | bytes 1000 | tf_op jit(solution)/shard_map/attend/pallas_call | solution.py:163
  83.6 0.0 copy-start.1
  83.6 4.1 %attend.7.refs_2_ = bf16[528,512]{1,0:T(8,128)(2,1)S(1)} custom-call(bf16[4,592,128]{2,1,0:T(8,128)(2,1)S(1)} %table.1.refs_0_, bf16[576,1024]{1,0:T(8,128)(2,1)S(1)} %bitcast.10, bf16[576,1024]{1,0:T(8,128)(2,1)S(1)} %collective-permute-done.2.refs_2_, bf16[576,1024]{1,0:T(8,128)(2,1)S(1)} %collective-permute-done.3.refs_3_, ...), custom_call_target="tpu_custom_call" | custom-call | flops 1000 | bytes 1000 | tf_op jit(solution)/shard_map/attend/pallas_call | solution.py:163
  87.7 0.3 collective-permute-done.22.refs_0_
  88.1 1.4 %collective-permute-start.23 = (bf16[528,512]{1,0:T(8,128)(2,1)S(1)}, bf16[528,512]{1,0:T(8,128)(2,1)S(1)}, u32[]{:S(2)}, u32[]{:S(2)}) collective-permute-start(bf16[528,512]{1,0:T(8,128)(2,1)S(1)} %attend.6), channel_id=1, source_target_pairs={{0,16},{4,20},{8,24},{12,28},{16,0},{20,4},{24,8},{28,12},{1,17},{... | collective-permute-start | bytes 1622024 | tf_op jit(solution)/shard_map/ppermute | solution.py:298
  89.5 2.3 %collective-permute-start.17 = (bf16[272,512]{1,0:T(8,128)(2,1)S(1)}, bf16[272,512]{1,0:T(8,128)(2,1)S(1)}, u32[]{:S(2)}, u32[]{:S(2)}) collective-permute-start(bf16[272,512]{1,0:T(8,128)(2,1)S(1)} %combine.2), channel_id=1, source_target_pairs={{0,2},{1,3},{2,0},{3,1},{4,6},{5,7},{6,4},{7,5},{8,10},{9,11},{10,... | collective-permute-start | bytes 835592 | tf_op jit(solution)/shard_map/ppermute | solution.py:298
  91.8 6.8 %index.1 = f32[32,4096]{1,0:T(8,128)} custom-call(bf16[32,80,128]{2,1,0:T(8,128)(2,1)S(1)} %constant_dynamic-update-slice_fusion.meta_ref, bf16[4096,128]{1,0:T(8,128)(2,1)S(1)} %copy-done.1), custom_call_target="tpu_custom_call" | custom-call | flops 1000 | bytes 1000 | tf_op jit(solution)/shard_map/index/pallas_call | solution.py:273
  98.6 2.7 %collective-permute-done.23.refs_1_ = bf16[528,512]{1,0:T(8,128)(2,1)S(1)} collective-permute-done((bf16[528,512]{1,0:T(8,128)(2,1)S(1)}, bf16[528,512]{1,0:T(8,128)(2,1)S(1)}, u32[]{:S(2)}, u32[]{:S(2)}) %collective-permute-start.23) | collective-permute-done | bytes 540704 | tf_op jit(solution)/shard_map/ppermute | solution.py:298
  101.3 1.1 %finish.2.refs_3_ = bf16[4,128,512]{2,1,0:T(8,128)(2,1)} custom-call(bf16[272,512]{1,0:T(8,128)(2,1)S(1)} %collective-permute-done.22.refs_0_, bf16[528,512]{1,0:T(8,128)(2,1)S(1)} %collective-permute-done.23.refs_1_, bf16[528,512]{1,0:T(8,128)(2,1)S(1)} %attend.7.refs_2_), custom_call_target="tpu_custom_call" | custom-call | flops 1000 | bytes 60000000 | tf_op jit(solution)/shard_map/finish/pallas_call | solution.py:222
  102.4 1.2 %collective-permute-done.17.refs_0_ = bf16[272,512]{1,0:T(8,128)(2,1)S(1)} collective-permute-done((bf16[272,512]{1,0:T(8,128)(2,1)S(1)}, bf16[272,512]{1,0:T(8,128)(2,1)S(1)}, u32[]{:S(2)}, u32[]{:S(2)}) %collective-permute-start.17) | collective-permute-done | bytes 278560 | tf_op jit(solution)/shard_map/ppermute | solution.py:298
  103.6 1.1 %finish.3 = bf16[4,128,512]{2,1,0:T(8,128)(2,1)} custom-call(bf16[272,512]{1,0:T(8,128)(2,1)S(1)} %collective-permute-done.17.refs_0_, bf16[528,512]{1,0:T(8,128)(2,1)S(1)} %collective-permute-done.23.refs_1_, bf16[528,512]{1,0:T(8,128)(2,1)S(1)} %attend.7.refs_2_, bf16[4,128,512]{2,1,0:T(8,128)(2,1)} %finish.2.refs_3_), custom_call_target="tpu_custom_call", output_to_operand_aliasing={{}: (3, {})} | custom-call | flops 1000 | bytes 1000 | tf_op jit(solution)/shard_map/finish/pallas_call | solution.py:222
  (33 shorter events, 0.3 us)
Async XLA Ops:
  0.6 5.8 %copy-start.3 = (s32[4,2048]{1,0:T(4,128)S(1)}, s32[4,2048]{1,0:T(4,128)}, u32[]{:S(2)}) copy-start(s32[4,2048]{1,0:T(4,128)} %selected_ref.1) | copy-start | bytes 98308
  0.6 5.8 %copy-start.2 = (bf16[4,128,576]{1,2,0:T(8,128)(2,1)S(1)}, bf16[4,128,576]{1,2,0:T(8,128)(2,1)}, u32[]{:S(2)}) copy-start(bf16[4,128,576]{1,2,0:T(8,128)(2,1)} %param.8) | copy-start | bytes 1769476
  0.7 10.6 %copy-start.5 = (bf16[4,64]{1,0:T(4,128)(2,1)S(1)}, bf16[4,64]{1,0:T(4,128)(2,1)}, u32[]{:S(2)}) copy-start(bf16[4,64]{1,0:T(4,128)(2,1)} %param.10) | copy-start | bytes 1540
  0.7 31.4 %copy-start = (bf16[1024,576]{0,1:T(8,128)(2,1)S(1)}, bf16[1024,576]{0,1:T(8,128)(2,1)}, u32[]{:S(2)}) copy-start(bf16[1024,576]{0,1:T(8,128)(2,1)} %param.6) | copy-start | bytes 3538948
  0.7 30.8 %collective-permute-start.3 = (bf16[576,1024]{1,0:T(8,128)(2,1)}, bf16[576,1024]{1,0:T(8,128)(2,1)S(1)}, u32[]{:S(2)}, u32[]{:S(2)}) collective-permute-start(bf16[576,1024]{1,0:T(8,128)(2,1)} %bitcast.3), channel_id=1, source_target_pairs={{0,8},{4,12},{8,0},{12,4},{16,24},{20,28},{24,16},{28,20},{1,9},{5... | collective-permute-start | bytes 3538952 | tf_op jit(solution)/shard_map/ppermute | solution.py:298
  4.8 26.7 %collective-permute-start.5 = (bf16[576,512]{1,0:T(8,128)(2,1)S(1)}, bf16[576,512]{1,0:T(8,128)(2,1)S(1)}, u32[]{:S(2)}, u32[]{:S(2)}) collective-permute-start(bf16[576,512]{1,0:T(8,128)(2,1)S(1)} %slice.16), channel_id=1, source_target_pairs={{0,1},{1,0},{2,3},{3,2},{4,5},{5,4},{6,7},{7,6},{8,9},{9,8},{10,11... | collective-permute-start | bytes 1769480 | tf_op jit(solution)/shard_map/ppermute | solution.py:298
  6.5 31.1 %copy-start.4 = (bf16[4,64,128]{2,1,0:T(8,128)(2,1)S(1)}, bf16[4,64,128]{2,1,0:T(8,128)(2,1)}, u32[]{:S(2)}) copy-start(bf16[4,64,128]{2,1,0:T(8,128)(2,1)} %param.9) | copy-start | bytes 196612
  7.1 28.9 %collective-permute-start = (bf16[4,592,128]{2,1,0:T(8,128)(2,1)S(1)}, bf16[4,592,128]{2,1,0:T(8,128)(2,1)S(1)}, u32[]{:S(2)}, u32[]{:S(2)}) collective-permute-start(bf16[4,592,128]{2,1,0:T(8,128)(2,1)S(1)} %table.1.refs_0_), channel_id=1, source_target_pairs={{0,2},{1,3},{2,0},{3,1},{4,6},{5,7},{6,4},{7,5},{8,10},{9,11},{10,... | collective-permute-start | bytes 1818632 | tf_op jit(solution)/shard_map/ppermute | solution.py:298
  9.7 31.4 %collective-permute-start.12 = (bf16[4,592,128]{2,1,0:T(8,128)(2,1)S(1)}, bf16[4,592,128]{2,1,0:T(8,128)(2,1)S(1)}, u32[]{:S(2)}, u32[]{:S(2)}) collective-permute-start(bf16[4,592,128]{2,1,0:T(8,128)(2,1)S(1)} %table.1.refs_0_), channel_id=1, source_target_pairs={{0,16},{4,20},{8,24},{12,28},{16,0},{20,4},{24,8},{28,12},{1,17},{... | collective-permute-start | bytes 1818632 | tf_op jit(solution)/shard_map/ppermute | solution.py:298
  31.5 13.9 %collective-permute-start.7 = (bf16[576,512]{1,0:T(8,128)(2,1)S(1)}, bf16[576,512]{1,0:T(8,128)(2,1)S(1)}, u32[]{:S(2)}, u32[]{:S(2)}) collective-permute-start(bf16[576,512]{1,0:T(8,128)(2,1)S(1)} %collective-permute-done.5.refs_5_), channel_id=1, source_target_pairs={{0,8},{4,12},{8,0},{12,4},{16,24},{20,28},{24,16},{28,20},{1,9},{5... | collective-permute-start | bytes 1769480 | tf_op jit(solution)/shard_map/ppermute | solution.py:298
  32.1 9.0 %collective-permute-start.9 = (bf16[576,256]{1,0:T(8,128)(2,1)S(1)}, bf16[576,256]{1,0:T(8,128)(2,1)S(1)}, u32[]{:S(2)}, u32[]{:S(2)}) collective-permute-start(bf16[576,256]{1,0:T(8,128)(2,1)S(1)} %get-tuple-element.18), channel_id=1, source_target_pairs={{0,1},{1,0},{2,3},{3,2},{4,5},{5,4},{6,7},{7,6},{8,9},{9,8},{10,11... | collective-permute-start | bytes 884744 | tf_op jit(solution)/shard_map/ppermute | solution.py:298
  36.0 11.2 %collective-permute-start.1 = (bf16[4,592,128]{2,1,0:T(8,128)(2,1)S(1)}, bf16[4,592,128]{2,1,0:T(8,128)(2,1)S(1)}, u32[]{:S(2)}, u32[]{:S(2)}) collective-permute-start(bf16[4,592,128]{2,1,0:T(8,128)(2,1)S(1)} %collective-permute-done.refs_0_), channel_id=1, source_target_pairs={{0,16},{4,20},{8,24},{12,28},{16,0},{20,4},{24,8},{28,12},{1,17},{... | collective-permute-start | bytes 1818632 | tf_op jit(solution)/shard_map/ppermute | solution.py:298
  37.6 1.3 %collective-permute-start.19 = (bf16[4,80,128]{2,1,0:T(8,128)(2,1)S(1)}, bf16[4,80,128]{2,1,0:T(8,128)(2,1)S(1)}, u32[]{:S(2)}, u32[]{:S(2)}) collective-permute-start(bf16[4,80,128]{2,1,0:T(8,128)(2,1)S(1)} %pad_maximum_fusion.3), channel_id=1, source_target_pairs={{0,4},{4,0},{8,12},{12,8},{16,20},{20,16},{24,28},{28,24},{1,5},{5... | collective-permute-start | bytes 245768 | tf_op jit(solution)/shard_map/ppermute | solution.py:298
  38.9 18.5 %collective-permute-start.2 = (bf16[576,1024]{1,0:T(8,128)(2,1)S(1)}, bf16[576,1024]{1,0:T(8,128)(2,1)S(1)}, u32[]{:S(2)}, u32[]{:S(2)}) collective-permute-start(bf16[576,1024]{1,0:T(8,128)(2,1)S(1)} %bitcast.6), channel_id=1, source_target_pairs={{0,4},{4,0},{8,12},{12,8},{16,20},{20,16},{24,28},{28,24},{1,5},{5... | collective-permute-start | bytes 3538952 | tf_op jit(solution)/shard_map/ppermute | solution.py:298
  41.1 4.3 %collective-permute-start.10 = (bf16[576,256]{1,0:T(8,128)(2,1)S(1)}, bf16[576,256]{1,0:T(8,128)(2,1)S(1)}, u32[]{:S(2)}, u32[]{:S(2)}) collective-permute-start(bf16[576,256]{1,0:T(8,128)(2,1)S(1)} %collective-permute-done.9.refs_9_), channel_id=1, source_target_pairs={{0,4},{4,0},{8,12},{12,8},{16,20},{20,16},{24,28},{28,24},{1,5},{5... | collective-permute-start | bytes 884744 | tf_op jit(solution)/shard_map/ppermute | solution.py:298
  41.1 15.7 %collective-permute-start.14 = (bf16[576,512]{1,0:T(8,128)(2,1)S(1)}, bf16[576,512]{1,0:T(8,128)(2,1)S(1)}, u32[]{:S(2)}, u32[]{:S(2)}) collective-permute-start(bf16[576,512]{1,0:T(8,128)(2,1)S(1)} %pad_maximum_fusion), channel_id=1, source_target_pairs={{0,1},{1,0},{2,3},{3,2},{4,5},{5,4},{6,7},{7,6},{8,9},{9,8},{10,11... | collective-permute-start | bytes 1769480 | tf_op jit(solution)/shard_map/ppermute | solution.py:298
  45.4 14.7 %collective-permute-start.4 = (bf16[576,1024]{1,0:T(8,128)(2,1)S(1)}, bf16[576,1024]{1,0:T(8,128)(2,1)S(1)}, u32[]{:S(2)}, u32[]{:S(2)}) collective-permute-start(bf16[576,1024]{1,0:T(8,128)(2,1)S(1)} %collective-permute-done.3.refs_3_), channel_id=1, source_target_pairs={{0,4},{4,0},{8,12},{12,8},{16,20},{20,16},{24,28},{28,24},{1,5},{5... | collective-permute-start | bytes 3538952 | tf_op jit(solution)/shard_map/ppermute | solution.py:298
  45.4 12.0 %collective-permute-start.6 = (bf16[576,512]{1,0:T(8,128)(2,1)S(1)}, bf16[576,512]{1,0:T(8,128)(2,1)S(1)}, u32[]{:S(2)}, u32[]{:S(2)}) collective-permute-start(bf16[576,512]{1,0:T(8,128)(2,1)S(1)} %collective-permute-done.5.refs_5_), channel_id=1, source_target_pairs={{0,4},{4,0},{8,12},{12,8},{16,20},{20,16},{24,28},{28,24},{1,5},{5... | collective-permute-start | bytes 1769480 | tf_op jit(solution)/shard_map/ppermute | solution.py:298
  47.3 9.6 %collective-permute-start.11 = (bf16[576,256]{1,0:T(8,128)(2,1)S(1)}, bf16[576,256]{1,0:T(8,128)(2,1)S(1)}, u32[]{:S(2)}, u32[]{:S(2)}) collective-permute-start(bf16[576,256]{1,0:T(8,128)(2,1)S(1)} %collective-permute-done.9.refs_9_), channel_id=1, source_target_pairs={{0,8},{4,12},{8,0},{12,4},{16,24},{20,28},{24,16},{28,20},{1,9},{5... | collective-permute-start | bytes 884744 | tf_op jit(solution)/shard_map/ppermute | solution.py:298
  56.8 3.3 %collective-permute-start.15 = (bf16[576,512]{1,0:T(8,128)(2,1)S(1)}, bf16[576,512]{1,0:T(8,128)(2,1)S(1)}, u32[]{:S(2)}, u32[]{:S(2)}) collective-permute-start(bf16[576,512]{1,0:T(8,128)(2,1)S(1)} %collective-permute-done.14.refs_13_), channel_id=1, source_target_pairs={{0,4},{4,0},{8,12},{12,8},{16,20},{20,16},{24,28},{28,24},{1,5},{5... | collective-permute-start | bytes 1769480 | tf_op jit(solution)/shard_map/ppermute | solution.py:298
  56.8 3.3 %collective-permute-start.8 = (bf16[576,512]{1,0:T(8,128)(2,1)S(1)}, bf16[576,512]{1,0:T(8,128)(2,1)S(1)}, u32[]{:S(2)}, u32[]{:S(2)}) collective-permute-start(bf16[576,512]{1,0:T(8,128)(2,1)S(1)} %collective-permute-done.7.refs_7_), channel_id=1, source_target_pairs={{0,4},{4,0},{8,12},{12,8},{16,20},{20,16},{24,28},{28,24},{1,5},{5... | collective-permute-start | bytes 1769480 | tf_op jit(solution)/shard_map/ppermute | solution.py:298
  57.4 2.8 %collective-permute-start.13 = (bf16[576,256]{1,0:T(8,128)(2,1)S(1)}, bf16[576,256]{1,0:T(8,128)(2,1)S(1)}, u32[]{:S(2)}, u32[]{:S(2)}) collective-permute-start(bf16[576,256]{1,0:T(8,128)(2,1)S(1)} %collective-permute-done.11.refs_11_), channel_id=1, source_target_pairs={{0,4},{4,0},{8,12},{12,8},{16,20},{20,16},{24,28},{28,24},{1,5},{5... | collective-permute-start | bytes 884744 | tf_op jit(solution)/shard_map/ppermute | solution.py:298
  57.5 8.2 %collective-permute-start.20 = (bf16[8,80,128]{2,1,0:T(8,128)(2,1)S(1)}, bf16[8,80,128]{2,1,0:T(8,128)(2,1)S(1)}, u32[]{:S(2)}, u32[]{:S(2)}) collective-permute-start(bf16[8,80,128]{2,1,0:T(8,128)(2,1)S(1)} %pad_maximum_fusion.2), channel_id=1, source_target_pairs={{0,16},{4,20},{8,24},{12,28},{16,0},{20,4},{24,8},{28,12},{1,17},{... | collective-permute-start | bytes 491528 | tf_op jit(solution)/shard_map/ppermute | solution.py:298
  64.3 9.6 %collective-permute-start.18 = (bf16[272,512]{1,0:T(8,128)(2,1)S(1)}, bf16[272,512]{1,0:T(8,128)(2,1)S(1)}, u32[]{:S(2)}, u32[]{:S(2)}) collective-permute-start(bf16[272,512]{1,0:T(8,128)(2,1)S(1)} %get-tuple-element.22), channel_id=1, source_target_pairs={{0,16},{4,20},{8,24},{12,28},{16,0},{20,4},{24,8},{28,12},{1,17},{... | collective-permute-start | bytes 835592 | tf_op jit(solution)/shard_map/ppermute | solution.py:298
  65.7 10.9 %collective-permute-start.21 = (bf16[16,80,128]{2,1,0:T(8,128)(2,1)S(1)}, bf16[16,80,128]{2,1,0:T(8,128)(2,1)S(1)}, u32[]{:S(2)}, u32[]{:S(2)}) collective-permute-start(bf16[16,80,128]{2,1,0:T(8,128)(2,1)S(1)} %pad_maximum_fusion.1), channel_id=1, source_target_pairs={{0,8},{4,12},{8,0},{12,4},{16,24},{20,28},{24,16},{28,20},{1,9},{5... | collective-permute-start | bytes 983048 | tf_op jit(solution)/shard_map/ppermute | solution.py:298
  66.9 12.1 %collective-permute-start.16 = (bf16[272,512]{1,0:T(8,128)(2,1)S(1)}, bf16[272,512]{1,0:T(8,128)(2,1)S(1)}, u32[]{:S(2)}, u32[]{:S(2)}) collective-permute-start(bf16[272,512]{1,0:T(8,128)(2,1)S(1)} %get-tuple-element.21), channel_id=1, source_target_pairs={{0,16},{4,20},{8,24},{12,28},{16,0},{20,4},{24,8},{28,12},{1,17},{... | collective-permute-start | bytes 835592 | tf_op jit(solution)/shard_map/ppermute | solution.py:298
  74.1 14.0 %collective-permute-start.22 = (bf16[272,512]{1,0:T(8,128)(2,1)S(1)}, bf16[272,512]{1,0:T(8,128)(2,1)S(1)}, u32[]{:S(2)}, u32[]{:S(2)}) collective-permute-start(bf16[272,512]{1,0:T(8,128)(2,1)S(1)} %combine.3), channel_id=1, source_target_pairs={{0,2},{1,3},{2,0},{3,1},{4,6},{5,7},{6,4},{7,5},{8,10},{9,11},{10,... | collective-permute-start | bytes 835592 | tf_op jit(solution)/shard_map/ppermute | solution.py:298
  83.6 8.2 %copy-start.1 = (bf16[4096,128]{1,0:T(8,128)(2,1)S(1)}, bf16[4096,128]{1,0:T(8,128)(2,1)}, u32[]{:S(2)}) copy-start(bf16[4096,128]{1,0:T(8,128)(2,1)} %keys_ref.1) | copy-start | bytes 3145732
  88.1 13.2 %collective-permute-start.23 = (bf16[528,512]{1,0:T(8,128)(2,1)S(1)}, bf16[528,512]{1,0:T(8,128)(2,1)S(1)}, u32[]{:S(2)}, u32[]{:S(2)}) collective-permute-start(bf16[528,512]{1,0:T(8,128)(2,1)S(1)} %attend.6), channel_id=1, source_target_pairs={{0,16},{4,20},{8,24},{12,28},{16,0},{20,4},{24,8},{28,12},{1,17},{... | collective-permute-start | bytes 1622024 | tf_op jit(solution)/shard_map/ppermute | solution.py:298
  89.5 14.2 %collective-permute-start.17 = (bf16[272,512]{1,0:T(8,128)(2,1)S(1)}, bf16[272,512]{1,0:T(8,128)(2,1)S(1)}, u32[]{:S(2)}, u32[]{:S(2)}) collective-permute-start(bf16[272,512]{1,0:T(8,128)(2,1)S(1)} %combine.2), channel_id=1, source_target_pairs={{0,2},{1,3},{2,0},{3,1},{4,6},{5,7},{6,4},{7,5},{8,10},{9,11},{10,... | collective-permute-start | bytes 835592 | tf_op jit(solution)/shard_map/ppermute | solution.py:298
